TPU v7x, 32 devices: a whole 2x2x4 slice. The times are simulated.
32 devices in a mesh: row: 4 (over y, x), col: 8 (over z, core).
Axes of the slice: x: 2, y: 2, z: 4, core: 2. Of those that a mesh axis runs over, the one named last changes fastest.
Arguments:
- start_block: float32 [8192, 128], P(('row', 'col')), may hold values from -6 to 6
- vertex_scale: float32 [8192], P(('row', 'col')), may hold values from 0.022097087 to 0.088388346
- adj_tiles: bfloat16 [4, 8, 64, 128, 128], P('row', 'col'), may hold values from 0 to 1
- tile_row: int32 [4, 8, 64], P('row', 'col'), may hold values from 0 to 7
- tile_col: int32 [4, 8, 64], P('row', 'col'), may hold values from 0 to 15
- live_count: int32 [4, 8], P('row', 'col'), may hold values from 16 to 64, as said below
- rotation_first: float32 [256, 128], replicated, may hold values from -0.375 to 0.375
- rotation_second: float32 [384, 128], replicated, may hold values from -0.3125 to 0.3125
Outputs:
- final_block: float32 [8192, 128], P(('row', 'col'))
- final_image: float32 [8192, 128], P(('row', 'col'))
Inputs may be any that keep to these rules, and one draw needn't show every extreme that they name: Slots from live_count on are ignored; at least one device has all 64 slots live in every draw.
All inputs are finite; a program needn't handle non-finite values.
Results may differ from a plain program's by a relative error of at most 0.01.
Values may be sent and summed in bfloat16 or wider, within the bound.
No kernel may reach another device: no remote copies, remote signals or barrier semaphores. Data moves between devices by JAX's collectives and lax.ppermute only.
A program may use at most 64 MiB of HBM per device.

v0:
```python
import jax
import jax.numpy as jnp
from jax import lax
from jax.sharding import PartitionSpec as P

HIGH = lax.Precision.HIGHEST


def tile_products(tiles_here, cols_here, count_here, flat_panel, span_slots, tile_side, width_k):
    alive_mask = jnp.arange(span_slots, dtype=jnp.int32) < count_here
    pieces = jnp.take(flat_panel, cols_here, axis=0)
    pieces = jnp.where(alive_mask[:, None], pieces, jnp.zeros_like(pieces))
    pieces = pieces.reshape(span_slots, tile_side, width_k)
    tile_out = jnp.einsum("tab,tbk->tak", tiles_here, pieces, preferred_element_type=jnp.float32)
    return tile_out.reshape(span_slots, tile_side * width_k)


def place_rows(rows_slot, tile_out, row_tiles, tile_side, width_k):
    placed = jax.ops.segment_sum(tile_out, rows_slot, num_segments=row_tiles)
    return placed.reshape(row_tiles * tile_side, width_k)


def apply_operator(block, vertex_scale, tiles_here, rows_here, cols_here, count_here):
    tile_side = tiles_here.shape[-1]
    width_k = block.shape[1]
    slot_total = tiles_here.shape[0]
    scaled = (vertex_scale[:, None] * block).astype(jnp.bfloat16)
    gathered = lax.all_gather(scaled, "col", axis=0, tiled=True)
    flat_panel = gathered.reshape(gathered.shape[0] // tile_side, tile_side * width_k)
    row_tiles = lax.axis_size("row") * block.shape[0] // tile_side
    tile_out = tile_products(
        tiles_here, cols_here, count_here, flat_panel, slot_total, tile_side, width_k
    )
    partial_value = place_rows(rows_here, tile_out, row_tiles, tile_side, width_k)
    summed = lax.psum_scatter(
        partial_value.astype(jnp.bfloat16), "row", scatter_dimension=0, tiled=True
    ).astype(jnp.float32)
    return block - vertex_scale[:, None] * summed


def inner(left, right):
    return jnp.einsum("sk,sl->kl", left, right, precision=HIGH)


def residual_block(block, image, verts_all):
    gram = lax.psum(inner(block, image), ("row", "col")) / verts_all
    resid = image - jnp.dot(block, gram, precision=HIGH)
    colsq = lax.psum(jnp.sum(resid * resid, axis=0), ("row", "col"))
    return resid * lax.rsqrt(colsq / verts_all + 1e-06)


def local(
    start_block,
    vertex_scale,
    adj_tiles,
    tile_row,
    tile_col,
    live_count,
    rotation_first,
    rotation_second,
):
    width_k = start_block.shape[1]
    verts_all = start_block.shape[0] * lax.axis_size("row") * lax.axis_size("col")
    tiles_here = adj_tiles[0, 0]
    rows_here = tile_row[0, 0]
    cols_here = tile_col[0, 0]
    count_here = live_count[0, 0]

    def oper(block):
        return apply_operator(block, vertex_scale, tiles_here, rows_here, cols_here, count_here)

    image0 = oper(start_block)
    search0 = residual_block(start_block, image0, verts_all)
    simage0 = oper(search0)
    rot_x, rot_w = (rotation_first[:width_k], rotation_first[width_k:])
    block1 = jnp.dot(start_block, rot_x, precision=HIGH) + jnp.dot(search0, rot_w, precision=HIGH)
    image1 = jnp.dot(image0, rot_x, precision=HIGH) + jnp.dot(simage0, rot_w, precision=HIGH)
    prev1 = jnp.dot(search0, rot_w, precision=HIGH)
    pimage1 = jnp.dot(simage0, rot_w, precision=HIGH)
    search1 = residual_block(block1, image1, verts_all)
    simage1 = oper(search1)
    rot_qx = rotation_second[:width_k]
    rot_qw = rotation_second[width_k : 2 * width_k]
    rot_qp = rotation_second[2 * width_k :]
    final_block = (
        jnp.dot(block1, rot_qx, precision=HIGH)
        + jnp.dot(search1, rot_qw, precision=HIGH)
        + jnp.dot(prev1, rot_qp, precision=HIGH)
    )
    final_image = (
        jnp.dot(image1, rot_qx, precision=HIGH)
        + jnp.dot(simage1, rot_qw, precision=HIGH)
        + jnp.dot(pimage1, rot_qp, precision=HIGH)
    )
    return (final_block, final_image)


def solution(mesh):
    placed = (
        P(("row", "col"), None),
        P(("row", "col")),
        P("row", "col", None, None, None),
        P("row", "col", None),
        P("row", "col", None),
        P("row", "col"),
        P(),
        P(),
    )
    return jax.shard_map(
        local,
        mesh=mesh,
        in_specs=placed,
        out_specs=(P(("row", "col"), None), P(("row", "col"), None)),
        check_vma=False,
    )
```

profile of v0, /device:TPU:0, one launch (start us, length us, event | category | flops | bytes accessed | tf_op | source)
XLA Modules:
  0.0 549.7 jit_solution(9371434053643963289)
XLA Ops:
  9.1 16.6 %all_gather.9 = bf16[2048,128]{0,1:T(8,128)(2,1)S(1)} all-gather(bf16[256,128]{0,1:T(8,128)(2,1)S(1)} %multiply_convert_fusion.2), channel_id=1, replica_groups=mesh['row'=4,'col'=8] {'col'}, dimensions={0}, use_global_device_ids=true | all-gather | bytes 589824 | tf_op jit(solution)/shard_map/all_gather | solution.py:28
  26.9 3.2 gather_fusion
  30.1 1.9 fusion.14
  32.6 3.5 convolution_bitcast_fusion.2
  36.1 5.6 %copy.21 = f32[64,128,128]{2,1,0:T(8,128)} copy(f32[64,128,128]{1,2,0:T(8,128)} %convolution_bitcast_fusion.2) | data formatting | bytes 8388608 | tf_op jit(solution)/shard_map/tab,tbk->tak/dot_general | solution.py:14
  41.7 9.6 %scatter_custom_fusion = f32[8,16384]{1,0:T(8,128)S(1)} fusion(s32[64]{0:T(128)} %bitcast.66, f32[8,8,128,128]{3,2,1,0:T(8,128)} %bitcast.61, f32[]{:T(128)} %constant.4.clone.1), kind=kCustom, calls=%fused_computation.12 | custom fusion | flops 1048576 | bytes 4719104 | tf_op jit(solution)/shard_map/scatter-add | solution.py:19
  52.4 25.2 %reduce-scatter.4.cloned.1.call-done = bf16[256,128]{0,1:T(8,128)(2,1)} async-done(((bf16[1024,128]{0,1:T(8,128)(2,1)}), bf16[256,128]{0,1:T(8,128)(2,1)}) %reduce-scatter.4.cloned.1.call-update) | async-done | bytes 65552 | tf_op jit(solution)/shard_map/reduce_scatter | solution.py:35
  77.7 1.7 convolution_bitcast_fusion.4
  79.5 122.8 %all-reduce.3.cloned.1.call-done = f32[128,128]{0,1:T(8,128)} async-done(((f32[128,128]{0,1:T(8,128)}), f32[128,128]{0,1:T(8,128)}) %all-reduce.3.cloned.1.call-update) | async-done | bytes 65552 | tf_op jit(solution)/shard_map/psum | solution.py:46
  202.3 1.2 multiply_reduce_fusion.1
  203.6 40.9 %psum.29 = f32[128]{0:T(128)S(1)} all-reduce(f32[128]{0:T(128)S(1)} %get-tuple-element.3), channel_id=1, replica_groups=mesh['row'=4,'col'=8] {'row','col'}, use_global_device_ids=true, to_apply=%region_4.6 | all-reduce | flops 128 | bytes 1024 | tf_op jit(solution)/shard_map/psum | solution.py:48
  245.0 14.8 %all_gather.10 = bf16[2048,128]{0,1:T(8,128)(2,1)S(1)} all-gather(bf16[256,128]{0,1:T(8,128)(2,1)S(1)} %multiply_convert_fusion.1), channel_id=1, replica_groups=mesh['row'=4,'col'=8] {'col'}, dimensions={0}, use_global_device_ids=true | all-gather | bytes 589824 | tf_op jit(solution)/shard_map/all_gather | solution.py:28
  260.3 3.2 gather_fusion.1
  263.5 1.9 fusion.13
  266.0 3.5 convolution_bitcast_fusion.1
  269.5 5.6 %copy.26 = f32[64,128,128]{2,1,0:T(8,128)} copy(f32[64,128,128]{1,2,0:T(8,128)} %convolution_bitcast_fusion.1) | data formatting | bytes 8388608 | tf_op jit(solution)/shard_map/tab,tbk->tak/dot_general | solution.py:14
  275.1 9.3 %scatter_custom_fusion.1 = f32[8,16384]{1,0:T(8,128)S(1)} fusion(s32[64]{0:T(128)} %bitcast.67, f32[8,8,128,128]{3,2,1,0:T(8,128)} %bitcast.62, f32[]{:T(128)} %constant.4.clone.1), kind=kCustom, calls=%fused_computation.9 | custom fusion | flops 1048576 | bytes 4719104 | tf_op jit(solution)/shard_map/scatter-add | solution.py:19
  285.6 11.4 %all-reduce.5.cloned.1.call-start = ((), (), s32[]{:S(2)}) async-start(), calls=%async_computation.6 | async-start | bytes 131072 | tf_op jit(solution)/shard_map/psum | solution.py:46
  298.3 11.4 %reduce-scatter.6.cloned.1.call-done = bf16[256,128]{0,1:T(8,128)(2,1)} async-done(((bf16[1024,128]{0,1:T(8,128)(2,1)}), bf16[256,128]{0,1:T(8,128)(2,1)}) %reduce-scatter.6.cloned.1.call-update) | async-done | bytes 65552 | tf_op jit(solution)/shard_map/reduce_scatter | solution.py:35
  309.8 1.3 fusion.22
  312.5 1.8 fusion.45
  314.2 119.1 %all-reduce.5.cloned.1.call-done = f32[128,128]{0,1:T(8,128)} async-done(((f32[128,128]{0,1:T(8,128)}), f32[128,128]{0,1:T(8,128)}) %all-reduce.5.cloned.1.call-update) | async-done | bytes 65552 | tf_op jit(solution)/shard_map/psum | solution.py:46
  434.5 40.9 %psum.31 = f32[128]{0:T(128)S(1)} all-reduce(f32[128]{0:T(128)S(1)} %get-tuple-element.5), channel_id=1, replica_groups=mesh['row'=4,'col'=8] {'row','col'}, use_global_device_ids=true, to_apply=%region_9.11 | all-reduce | flops 128 | bytes 1024 | tf_op jit(solution)/shard_map/psum | solution.py:48
  475.9 14.8 %all_gather.11 = bf16[2048,128]{0,1:T(8,128)(2,1)S(1)} all-gather(bf16[256,128]{0,1:T(8,128)(2,1)S(1)} %multiply_convert_fusion), channel_id=1, replica_groups=mesh['row'=4,'col'=8] {'col'}, dimensions={0}, use_global_device_ids=true | all-gather | bytes 589824 | tf_op jit(solution)/shard_map/all_gather | solution.py:28
  491.3 3.2 gather_fusion.2
  494.5 1.9 fusion.12
  497.0 3.5 convolution_bitcast_fusion
  500.5 5.6 %copy.33 = f32[64,128,128]{2,1,0:T(8,128)} copy(f32[64,128,128]{1,2,0:T(8,128)} %convolution_bitcast_fusion) | data formatting | bytes 8388608 | tf_op jit(solution)/shard_map/tab,tbk->tak/dot_general | solution.py:14
  506.1 9.3 %scatter_custom_fusion.2 = f32[8,16384]{1,0:T(8,128)S(1)} fusion(s32[64]{0:T(128)} %bitcast.68, f32[8,8,128,128]{3,2,1,0:T(8,128)} %bitcast.60, f32[]{:T(128)} %constant.4.clone.1), kind=kCustom, calls=%fused_computation.6 | custom fusion | flops 1048576 | bytes 4719104 | tf_op jit(solution)/shard_map/scatter-add | solution.py:19
  517.8 1.3 convolution_add_fusion.3
  520.0 20.7 %reduce-scatter.8.cloned.1.call-done = bf16[256,128]{0,1:T(8,128)(2,1)} async-done(((bf16[1024,128]{0,1:T(8,128)(2,1)}), bf16[256,128]{0,1:T(8,128)(2,1)}) %reduce-scatter.8.cloned.1.call-update) | async-done | bytes 65552 | tf_op jit(solution)/shard_map/reduce_scatter | solution.py:35
  540.7 1.3 convolution_add_fusion.1
  (75 shorter events, 16.3 us)
Async XLA Ops:
  7.2 25.4 %copy-start = (bf16[1,1,64,128,128]{4,3,2,1,0:T(8,128)(2,1)S(1)}, bf16[1,1,64,128,128]{4,3,2,1,0:T(8,128)(2,1)}, u32[]{:S(2)}) copy-start(bf16[1,1,64,128,128]{4,3,2,1,0:T(8,128)(2,1)} %param.12) | copy-start | bytes 6291460
  7.2 19.0 %copy-start.14 = (s32[1,1,64]{2,1,0:T(1,128)S(1)}, s32[1,1,64]{2,1,0:T(1,128)}, u32[]{:S(2)}) copy-start(s32[1,1,64]{2,1,0:T(1,128)} %param.14) | copy-start | bytes 772
  7.2 70.5 %reduce-scatter.4.cloned.1.call-start = ((), (), s32[]{:S(2)}) async-start(), calls=%async_computation.3 | async-start | bytes 327680 | tf_op jit(solution)/shard_map/reduce_scatter | solution.py:35
  51.3 26.3 %copy-start.1 = (f32[256,128]{1,0:T(8,128)S(1)}, f32[256,128]{1,0:T(8,128)}, u32[]{:S(2)}) copy-start(f32[256,128]{1,0:T(8,128)} %param.10) | copy-start | bytes 393220
  51.3 26.3 %copy-start.9 = (f32[256]{0:T(256)S(1)}, f32[256]{0:T(256)}, u32[]{:S(2)}) copy-start(f32[256]{0:T(256)} %param.11) | copy-start | bytes 3076
  52.4 149.9 %all-reduce.3.cloned.1.call-start = ((), (), s32[]{:S(2)}) async-start(), calls=%async_computation.4 | async-start | bytes 131072 | tf_op jit(solution)/shard_map/psum | solution.py:46
  79.4 230.3 %reduce-scatter.6.cloned.1.call-start = ((), (), s32[]{:S(2)}) async-start(), calls=%async_computation.5 | async-start | bytes 327680 | tf_op jit(solution)/shard_map/reduce_scatter | solution.py:35
  244.4 0.5 copy-start.10
  284.5 12.4 %copy-start.6 = (f32[256,128]{1,0:T(8,128)S(1)}, f32[256,128]{1,0:T(8,128)}, u32[]{:S(2)}) copy-start(f32[256,128]{1,0:T(8,128)} %param.16) | copy-start | bytes 393220
  284.5 25.2 %copy-start.11 = (f32[128]{0:T(128)S(1)}, f32[128]{0:T(128)}, u32[]{:S(2)}) copy-start(f32[128]{0:T(128)} %copy-done.10) | copy-start | bytes 1540
  284.5 26.6 %copy-start.5 = (bf16[256,128]{0,1:T(8,128)(2,1)S(1)}, bf16[256,128]{0,1:T(8,128)(2,1)}, u32[]{:S(2)}) copy-start(bf16[256,128]{0,1:T(8,128)(2,1)} %reduce-scatter.4.cloned.1.call-done) | copy-start | bytes 196612
  284.6 26.6 %copy-start.7 = (f32[256,128]{1,0:T(8,128)S(1)}, f32[256,128]{1,0:T(8,128)}, u32[]{:S(2)}) copy-start(f32[256,128]{1,0:T(8,128)} %param.16) | copy-start | bytes 393220
  285.6 147.8 %all-reduce.5.cloned.1.call-start = ((), (), s32[]{:S(2)}) async-start(), calls=%async_computation.6 | async-start | bytes 131072 | tf_op jit(solution)/shard_map/psum | solution.py:46
  311.1 164.5 %copy-start.2 = (f32[256,128]{1,0:T(8,128)}, f32[256,128]{1,0:T(8,128)S(1)}, u32[]{:S(2)}) copy-start(f32[256,128]{1,0:T(8,128)S(1)} %fusion.22) | copy-start | bytes 393220
  312.4 228.3 %reduce-scatter.8.cloned.1.call-start = ((), (), s32[]{:S(2)}) async-start(), calls=%async_computation.7 | async-start | bytes 327680 | tf_op jit(solution)/shard_map/reduce_scatter | solution.py:35
  475.4 0.5 copy-start.12
  515.5 2.3 copy-start.8
  515.5 2.3 copy-start.13
  515.5 26.6 %copy-start.3 = (f32[256,128]{1,0:T(8,128)S(1)}, f32[256,128]{1,0:T(8,128)}, u32[]{:S(2)}) copy-start(f32[256,128]{1,0:T(8,128)} %copy-done.2) | copy-start | bytes 393220
  515.5 3.6 copy-start.4
Sparse Core Ops, SparseCore 0:
  52.5 25.1 reduce-scatter.3
  84.7 117.5 all-reduce.2
  285.7 24.0 reduce-scatter.5
  315.8 117.5 all-reduce.4
  516.7 24.0 reduce-scatter.7
where the time goes:
time: 559 us; the launch traced here: 550 us
  waiting for transfers between devices  299 us (53%)
  blocking collectives  128 us (23%)
  other arithmetic  34.9 us (6%)
  local copies, waits for them, and re-layouts  34.7 us (6%)
  matrix products  26.1 us (5%)
  between operations  15.1 us (3%)
  starting transfers between devices  11.5 us (2%)
    psum x2, waiting for transfers between devices, residual_block(): gram = lax.psum(inner(block, image), ('row', 'col')) / verts_all  242 us
    psum x2, blocking collectives, residual_block(): colsq = lax.psum(jnp.sum(resid * resid, axis=0), ('row', 'col'))  81.7 us
    reduce_scatter x3, waiting for transfers between devices, apply_operator(): lax.psum_scatter(partial_value.astype(jnp.bfloat16), 'row', scatter_dimen...  57.4 us
    all_gather x3, blocking collectives, apply_operator(): gathered = lax.all_gather(scaled, 'col', axis=0, tiled=True)  46.2 us
    scatter-add x3, other arithmetic, place_rows(): placed = jax.ops.segment_sum(tile_out, rows_slot, num_segments=row_tiles)  28.3 us
    dot_general x3, local copies, waits for them, and re-layouts, tile_products(): jnp.einsum('tab,tbk->tak', tiles_here, pieces, preferred_element_type=jnp...  16.8 us
    psum x2, starting transfers between devices, residual_block(): gram = lax.psum(inner(block, image), ('row', 'col')) / verts_all  11.4 us
  transfers between devices with their start and end apart: 5, of which 5 were waited for; matrix products, arithmetic and copies ran while one was open for 1% of the time, Pallas kernels for 0%

commit v1 on v0

v1 whole, which is shorter than its diff:
```python
import functools

import jax
import jax.numpy as jnp
from jax import lax
from jax.experimental import pallas as pl
from jax.experimental.pallas import tpu as pltpu
from jax.sharding import PartitionSpec as P

HIGH = lax.Precision.HIGHEST
VMEM_BYTES = 40 * 1024 * 1024


def swap(array, axis, mask):
    size = lax.axis_size(axis)
    return lax.ppermute(array, axis, [(k, k ^ mask) for k in range(size)])


def vmem(count):
    return [pl.BlockSpec(memory_space=pltpu.VMEM)] * count


def smem(count):
    return [pl.BlockSpec(memory_space=pltpu.SMEM)] * count


def dot(left, right, contract=((1,), (0,))):
    return lax.dot_general(
        left, right, (contract, ((), ())), precision=HIGH, preferred_element_type=jnp.float32
    )


def tiles_kernel(n_col, n_row, unroll, cols_ref, rows_ref, tiles_ref, *refs):
    pieces, outs = refs[:n_col], refs[n_col : n_col + n_row]
    panel, total = refs[n_col + n_row :]
    sub = pieces[0].shape[0]
    slots, side = tiles_ref.shape[0], tiles_ref.shape[1]
    for m, piece in enumerate(pieces):
        panel[m * sub : (m + 1) * sub] = piece[...]
    total[...] = jnp.zeros_like(total)

    def step(group, carry):
        products = []
        for u in range(unroll):
            slot = group * unroll + u
            column = pl.multiple_of(cols_ref[slot] * side, side)
            products.append(
                jnp.dot(
                    tiles_ref[slot],
                    panel[pl.ds(column, side), :],
                    preferred_element_type=jnp.float32,
                )
            )
        for u in range(unroll):
            row = pl.multiple_of(rows_ref[group * unroll + u] * side, side)
            total[pl.ds(row, side), :] += products[u]
        return carry

    lax.fori_loop(0, slots // unroll, step, 0)
    outs[0][...] = total[:sub]
    for k in range(1, n_row):
        outs[k][...] = total[k * sub : (k + 1) * sub].astype(outs[k].dtype)


def tile_products(cols, rows, tiles, pieces, n_row):
    n_col = len(pieces)
    sub, width = pieces[0].shape
    slots, side = tiles.shape[0], tiles.shape[1]
    unroll = 4 if slots % 4 == 0 else 1
    return pl.pallas_call(
        functools.partial(tiles_kernel, n_col, n_row, unroll),
        out_shape=[
            jax.ShapeDtypeStruct((sub, width), jnp.float32 if k == 0 else jnp.bfloat16)
            for k in range(n_row)
        ],
        in_specs=smem(2) + vmem(1 + n_col),
        out_specs=vmem(n_row),
        scratch_shapes=[
            pltpu.VMEM((n_col * sub, width), jnp.bfloat16),
            pltpu.VMEM((n_row * sub + side, width), jnp.float32),
        ],
        compiler_params=pltpu.CompilerParams(vmem_limit_bytes=VMEM_BYTES),
        cost_estimate=pl.CostEstimate(
            flops=2 * slots * side * side * width,
            bytes_accessed=2 * slots * side * side,
            transcendentals=0,
        ),
        name="tile_products",
    )(cols, rows, tiles, *pieces)


def gram_kernel(n_col, index_ref, x_ref, z1_ref, z2_ref, near_ref, far_ref, whole):
    x, z1, z2 = x_ref[...], z1_ref[...], z2_ref[...]
    contract = ((0,), (0,))
    for at, (left, right) in enumerate(
        ((x, x), (x, z1), (z1, z1), (x, z2), (z1, z2), (z2, z2))
    ):
        whole[at] = dot(left, right, contract)
    rows = whole.shape[1] // n_col
    for m in range(n_col):
        out = far_ref if m % 2 else near_ref
        start = pl.multiple_of((index_ref[0] ^ m) * rows, rows)
        for at in range(whole.shape[0]):
            out[m // 2, at * rows : (at + 1) * rows] = whole[at, pl.ds(start, rows), :]


def grams(index, x, z1, z2, n_col):
    width = x.shape[1]
    cut = jax.ShapeDtypeStruct((n_col // 2, 6 * (width // n_col), width), jnp.float32)
    return pl.pallas_call(
        functools.partial(gram_kernel, n_col),
        out_shape=[cut, cut],
        in_specs=smem(1) + vmem(3),
        out_specs=vmem(2),
        scratch_shapes=[pltpu.VMEM((6, width, width), jnp.float32)],
        compiler_params=pltpu.CompilerParams(vmem_limit_bytes=VMEM_BYTES),
        name="grams",
    )(index, x, z1, z2)


def finish_kernel(
    n_col,
    verts_all,
    index_ref,
    x_ref,
    z1_ref,
    z2_ref,
    z3_ref,
    first_ref,
    second_ref,
    near_ref,
    far_ref,
    block_ref,
    image_ref,
    whole,
):
    width = x_ref.shape[1]
    rows = width // n_col
    for m in range(n_col):
        piece = far_ref if m % 2 else near_ref
        start = pl.multiple_of((index_ref[0] ^ m) * rows, rows)
        for at in range(whole.shape[0]):
            whole[at, pl.ds(start, rows), :] = piece[m // 2, at * rows : (at + 1) * rows]
    n00, n01, n11, n02, n12, n22 = (whole[at] for at in range(6))
    n10, n21 = n01.T, n12.T
    eye = (
        lax.broadcasted_iota(jnp.int32, (width, width), 0)
        == lax.broadcasted_iota(jnp.int32, (width, width), 1)
    ).astype(jnp.float32)
    scale = 1.0 / verts_all

    def inverse_norm(colsq):
        row = lax.rsqrt(jnp.maximum(colsq, 0.0) * scale + 1e-06)
        return jnp.sum(eye * row, axis=1, keepdims=True)

    def column_sum(array):
        return jnp.sum(array, axis=0, keepdims=True)

    keep0 = eye - (n00 - n01) * scale
    colsq0 = column_sum(keep0 * (dot(n00, keep0) - 2.0 * n01) + eye * n11)
    q = inverse_norm(colsq0) * first_ref[width:]
    p = first_ref[:width] + dot(keep0, q)
    coeff = jnp.concatenate([p, -q], axis=0)
    blocks = jnp.concatenate(
        [
            jnp.concatenate([n00, n01], axis=1),
            jnp.concatenate([n10, n11], axis=1),
            jnp.concatenate([n01, n02], axis=1),
            jnp.concatenate([n11, n12], axis=1),
            jnp.concatenate([n11, n12], axis=1),
            jnp.concatenate([n21, n22], axis=1),
        ],
        axis=0,
    )
    applied = dot(blocks, coeff)
    pair = jnp.concatenate(
        [applied[: 2 * width], applied[2 * width : 4 * width]], axis=1
    )
    both = dot(coeff, pair, ((0,), (0,)))
    s, t = both[:, :width], both[:, width:]
    u = column_sum(coeff * applied[4 * width :])
    keep1 = eye - (s - t) * scale
    colsq1 = column_sum(keep1 * (dot(s, keep1) - 2.0 * t)) + u
    v = inverse_norm(colsq1) * second_ref[width : 2 * width]
    e = second_ref[:width] + dot(keep1, v)
    f = dot(q, second_ref[2 * width :])
    mixed = dot(jnp.concatenate([p, q], axis=0), jnp.concatenate([e, v], axis=1))
    a0 = mixed[:width, :width] + dot(keep0, f)
    a1 = -(mixed[width:, :width] + mixed[:width, width:] + f)
    a2 = mixed[width:, width:]
    stacked = jnp.concatenate([a0, a1, a2], axis=0)
    z1, z2 = z1_ref[...], z2_ref[...]
    block = dot(jnp.concatenate([x_ref[...], z1, z2], axis=1), stacked)
    block_ref[...] = block
    image_ref[...] = block - dot(jnp.concatenate([z1, z2, z3_ref[...]], axis=1), stacked)


def finish(index, x, z1, z2, z3, first, second, near, far, n_col, verts_all):
    out = jax.ShapeDtypeStruct(x.shape, jnp.float32)
    width = x.shape[1]
    return pl.pallas_call(
        functools.partial(finish_kernel, n_col, verts_all),
        out_shape=[out, out],
        in_specs=smem(1) + vmem(8),
        out_specs=vmem(2),
        scratch_shapes=[pltpu.VMEM((6, width, width), jnp.float32)],
        compiler_params=pltpu.CompilerParams(vmem_limit_bytes=VMEM_BYTES),
        name="finish",
    )(index, x, z1, z2, z3, first, second, near, far)


def local(
    start_block,
    vertex_scale,
    adj_tiles,
    tile_row,
    tile_col,
    live_count,
    rotation_first,
    rotation_second,
):
    n_row, n_col = lax.axis_size("row"), lax.axis_size("col")
    row_at, col_at = lax.axis_index("row"), lax.axis_index("col")
    sub = start_block.shape[0]
    verts_all = sub * n_row * n_col
    tiles = adj_tiles[0, 0]
    halves = sub // tiles.shape[1]
    slots = jnp.arange(tiles.shape[0], dtype=jnp.int32)
    cols = ((tile_col[0, 0] // halves) ^ col_at) * halves + tile_col[0, 0] % halves
    rows = ((tile_row[0, 0] // halves) ^ row_at) * halves + tile_row[0, 0] % halves
    rows = jnp.where(slots < live_count[0, 0], rows, n_row * halves)
    index = col_at.reshape(1)
    scale = vertex_scale[:, None]

    def adjacency(block):
        own = (scale * block).astype(jnp.bfloat16)
        near = [own] + [swap(own, "col", m) for m in range(2, n_col, 2)]
        far = [swap(piece, "col", 1) for piece in near]
        pieces = [piece for pair in zip(near, far) for piece in pair]
        parts = tile_products(cols, rows, tiles, pieces, n_row)
        summed = parts[0]
        for k in range(1, n_row):
            summed = summed + swap(parts[k], "row", k).astype(jnp.float32)
        return scale * summed

    z1 = adjacency(start_block)
    z2 = adjacency(z1)
    near, far = grams(index, start_block, z1, z2, n_col)
    near = near + swap(far, "col", 1)
    mine = near[0]
    for q in range(1, n_col // 2):
        mine = mine + swap(near[q], "col", 2 * q)
    whole = mine
    for k in range(1, n_row):
        whole = whole + swap(mine, "row", k)
    near = jnp.stack([whole] + [swap(whole, "col", m) for m in range(2, n_col, 2)])
    far = swap(near, "col", 1)
    z3 = adjacency(z2)
    return tuple(
        finish(
            index,
            start_block,
            z1,
            z2,
            z3,
            rotation_first,
            rotation_second,
            near,
            far,
            n_col,
            verts_all,
        )
    )


def solution(mesh):
    placed = (
        P(("row", "col"), None),
        P(("row", "col")),
        P("row", "col", None, None, None),
        P("row", "col", None),
        P("row", "col", None),
        P("row", "col"),
        P(),
        P(),
    )
    return jax.shard_map(
        local,
        mesh=mesh,
        in_specs=placed,
        out_specs=(P(("row", "col"), None), P(("row", "col"), None)),
        check_vma=False,
    )
```

time: 559 us -> 88.9 us (0.16); the launches traced: 550 us -> 88.7 us
  waiting for transfers between devices: 299 us -> 28.4 us
  blocking collectives: 128 us -> 0 us
  local copies, waits for them, and re-layouts: 34.7 us -> 1.63 us
  other arithmetic: 34.9 us -> 2.08 us
  starting transfers between devices: 11.5 us -> 38.5 us
  matrix products: 26.1 us -> 0 us
  Pallas kernels: 0 us -> 16.5 us
  between operations: 15.1 us -> 1.51 us
    psum x2 -> x0, waiting for transfers between devices: 242 us -> none  [residual_block(): gram = lax.psum(inner(block, image), ('row', 'col')) / verts_all]
    psum x2 -> x0, blocking collectives: 81.7 us -> none  [residual_block(): colsq = lax.psum(jnp.sum(resid * resid, axis=0), ('row', 'col'))]
    reduce_scatter x3 -> x0, waiting for transfers between devices: 57.4 us -> none  [apply_operator(): lax.psum_scatter(partial_value.astype(jnp.bfloat16), 'row', scatter_dimen...]
    all_gather x3 -> x0, blocking collectives: 46.2 us -> none  [apply_operator(): gathered = lax.all_gather(scaled, 'col', axis=0, tiled=True)]
    ppermute x0 -> x41, starting transfers between devices: none -> 38.5 us  [swap(): return lax.ppermute(array, axis, [(k, k ^ mask) for k in range(size)])]
    ppermute x0 -> x41, waiting for transfers between devices: none -> 28.4 us  [swap(): return lax.ppermute(array, axis, [(k, k ^ mask) for k in range(size)])]
    scatter-add x3 -> x0, other arithmetic: 28.3 us -> none  [place_rows(): placed = jax.ops.segment_sum(tile_out, rows_slot, num_segments=row_tiles)]
    dot_general x17 -> x0, matrix products: 26.1 us -> none  [the longest x3 10.6 us: tile_products(): jnp.einsum('tab,tbk->tak', tiles_here, pieces, preferred_element_type=jnp...]
  transfers between devices with their start and end apart: 5 -> 41, of which waited for: 5 -> 21; matrix products, arithmetic and copies ran while one was open for 1% -> 1% of each run, Pallas kernels for 0% -> 4%
where the time goes in v1:
time: 88.9 us; the launch traced here: 88.7 us
  starting transfers between devices  38.5 us (43%)
  waiting for transfers between devices  28.4 us (32%)
  Pallas kernels  16.5 us (19%)
  other arithmetic  2.08 us (2%)
  local copies, waits for them, and re-layouts  1.63 us (2%)
  between operations  1.51 us (2%)
    ppermute x41, starting transfers between devices, swap(): return lax.ppermute(array, axis, [(k, k ^ mask) for k in range(size)])  38.5 us
    ppermute x41, waiting for transfers between devices, swap(): return lax.ppermute(array, axis, [(k, k ^ mask) for k in range(size)])  28.4 us
    pallas_call x3, Pallas kernels, tile_products(): pl.pallas_call(functools.partial(tiles_kernel, n_col, n_row, unroll), out...  11 us
    pallas_call x1, Pallas kernels, finish(): pl.pallas_call(functools.partial(finish_kernel, n_col, verts_all), out_sh...  4.69 us
  transfers between devices with their start and end apart: 41, of which 21 were waited for; matrix products, arithmetic and copies ran while one was open for 1% of the time, Pallas kernels for 4%

profile of v1, /device:TPU:0, one launch (start us, length us, event | category | flops | bytes accessed | tf_op | source)
XLA Modules:
  0.0 88.7 jit_solution(3164645412123830176)
XLA Ops:
  0.6 1.0 %multiply_convert_fusion.2.refs_0_ = bf16[256,128]{1,0:T(8,128)(2,1)S(1)} fusion(f32[256,128]{1,0:T(8,128)} %x_ref.3, f32[256]{0:T(256)} %param.9), kind=kLoop, calls=%fused_computation.6 | loop fusion | flops 65536 | bytes 197632 | tf_op jit(solution)/shard_map/convert_element_type | solution.py:236
  1.7 5.1 %collective-permute-start.5 = (bf16[256,128]{1,0:T(8,128)(2,1)S(1)}, bf16[256,128]{1,0:T(8,128)(2,1)S(1)}, u32[]{:S(2)}, u32[]{:S(2)}) collective-permute-start(bf16[256,128]{1,0:T(8,128)(2,1)S(1)} %multiply_convert_fusion.2.refs_0_), channel_id=1, source_target_pairs={{0,6},{1,7},{2,4},{3,5},{4,2},{5,3},{6,0},{7,1},{8,14},{9,15},{10,... | collective-permute-start | bytes 196616 | tf_op jit(solution)/shard_map/ppermute | solution.py:16
  8.1 1.3 %collective-permute-done.5.refs_6_ = bf16[256,128]{1,0:T(8,128)(2,1)S(1)} collective-permute-done((bf16[256,128]{1,0:T(8,128)(2,1)S(1)}, bf16[256,128]{1,0:T(8,128)(2,1)S(1)}, u32[]{:S(2)}, u32[]{:S(2)}) %collective-permute-start.5) | collective-permute-done | bytes 65568 | tf_op jit(solution)/shard_map/ppermute | solution.py:16
  9.4 3.0 %collective-permute-done.3.refs_4_ = bf16[256,128]{1,0:T(8,128)(2,1)S(1)} collective-permute-done((bf16[256,128]{1,0:T(8,128)(2,1)S(1)}, bf16[256,128]{1,0:T(8,128)(2,1)S(1)}, u32[]{:S(2)}, u32[]{:S(2)}) %collective-permute-start.3) | collective-permute-done | bytes 65568 | tf_op jit(solution)/shard_map/ppermute | solution.py:16
  13.8 1.6 %copy-done = bf16[1,1,64,128,128]{4,3,2,1,0:T(8,128)(2,1)S(1)} copy-done((bf16[1,1,64,128,128]{4,3,2,1,0:T(8,128)(2,1)S(1)}, bf16[1,1,64,128,128]{4,3,2,1,0:T(8,128)(2,1)}, u32[]{:S(2)}) %copy-start) | copy-done | bytes 2097176
  15.4 3.7 %tile_products.3 = (f32[256,128]{1,0:T(8,128)S(1)}, bf16[256,128]{1,0:T(8,128)(2,1)S(1)}, bf16[256,128]{1,0:T(8,128)(2,1)S(1)}, bf16[256,128]{1,0:T(8,128)(2,1)S(1)}) custom-call(s32[64]{0:T(128)S(1)} %get-tuple-element.38.cols_ref, s32[64]{0:T(128)S(1)} %get-tuple-element.37.rows_ref, bf16[64,128,128]{2,1,0:T(8,128)(2,1)S(1)} %bitcast.48, ...), custom_call_target="tpu_custom_call" | custom-call | flops 268435456 | bytes 2097152 | tf_op jit(solution)/shard_map/tile_products/pallas_call | solution.py:70
  19.1 1.6 %collective-permute-start.7 = (bf16[256,128]{1,0:T(8,128)(2,1)S(1)}, bf16[256,128]{1,0:T(8,128)(2,1)S(1)}, u32[]{:S(2)}, u32[]{:S(2)}) collective-permute-start(bf16[256,128]{1,0:T(8,128)(2,1)S(1)} %get-tuple-element.17), channel_id=1, source_target_pairs={{0,8},{8,0},{16,24},{24,16},{1,9},{9,1},{17,25},{25,17},{2,10},{10... | collective-permute-start | bytes 196616 | tf_op jit(solution)/shard_map/ppermute | solution.py:16
  20.6 1.5 %collective-permute-start.8 = (bf16[256,128]{1,0:T(8,128)(2,1)S(1)}, bf16[256,128]{1,0:T(8,128)(2,1)S(1)}, u32[]{:S(2)}, u32[]{:S(2)}) collective-permute-start(bf16[256,128]{1,0:T(8,128)(2,1)S(1)} %get-tuple-element.18), channel_id=1, source_target_pairs={{0,16},{8,24},{16,0},{24,8},{1,17},{9,25},{17,1},{25,9},{2,18},{10... | collective-permute-start | bytes 196616 | tf_op jit(solution)/shard_map/ppermute | solution.py:16
  23.5 1.4 %collective-permute-done.8 = bf16[256,128]{1,0:T(8,128)(2,1)S(1)} collective-permute-done((bf16[256,128]{1,0:T(8,128)(2,1)S(1)}, bf16[256,128]{1,0:T(8,128)(2,1)S(1)}, u32[]{:S(2)}, u32[]{:S(2)}) %collective-permute-start.8) | collective-permute-done | bytes 65568 | tf_op jit(solution)/shard_map/ppermute | solution.py:16
  24.9 2.4 %collective-permute-done.9 = bf16[256,128]{1,0:T(8,128)(2,1)S(1)} collective-permute-done((bf16[256,128]{1,0:T(8,128)(2,1)S(1)}, bf16[256,128]{1,0:T(8,128)(2,1)S(1)}, u32[]{:S(2)}, u32[]{:S(2)}) %collective-permute-start.9) | collective-permute-done | bytes 65568 | tf_op jit(solution)/shard_map/ppermute | solution.py:16
  27.5 2.8 %collective-permute-start.15 = (bf16[256,128]{1,0:T(8,128)(2,1)S(1)}, bf16[256,128]{1,0:T(8,128)(2,1)S(1)}, u32[]{:S(2)}, u32[]{:S(2)}) collective-permute-start(bf16[256,128]{1,0:T(8,128)(2,1)S(1)} %get-tuple-element.32.refs_0_), channel_id=1, source_target_pairs={{0,6},{1,7},{2,4},{3,5},{4,2},{5,3},{6,0},{7,1},{8,14},{9,15},{10,... | collective-permute-start | bytes 196616 | tf_op jit(solution)/shard_map/ppermute | solution.py:16
  30.2 1.7 %collective-permute-start.11 = (bf16[256,128]{1,0:T(8,128)(2,1)S(1)}, bf16[256,128]{1,0:T(8,128)(2,1)S(1)}, u32[]{:S(2)}, u32[]{:S(2)}) collective-permute-start(bf16[256,128]{1,0:T(8,128)(2,1)S(1)} %get-tuple-element.32.refs_0_), channel_id=1, source_target_pairs={{0,2},{1,3},{2,0},{3,1},{4,6},{5,7},{6,4},{7,5},{8,10},{9,11},{10,... | collective-permute-start | bytes 196616 | tf_op jit(solution)/shard_map/ppermute | solution.py:16
  31.9 2.2 %collective-permute-done.15.refs_6_ = bf16[256,128]{1,0:T(8,128)(2,1)S(1)} collective-permute-done((bf16[256,128]{1,0:T(8,128)(2,1)S(1)}, bf16[256,128]{1,0:T(8,128)(2,1)S(1)}, u32[]{:S(2)}, u32[]{:S(2)}) %collective-permute-start.15) | collective-permute-done | bytes 65568 | tf_op jit(solution)/shard_map/ppermute | solution.py:16
  34.1 1.6 %collective-permute-done.13.refs_4_ = bf16[256,128]{1,0:T(8,128)(2,1)S(1)} collective-permute-done((bf16[256,128]{1,0:T(8,128)(2,1)S(1)}, bf16[256,128]{1,0:T(8,128)(2,1)S(1)}, u32[]{:S(2)}, u32[]{:S(2)}) %collective-permute-start.13) | collective-permute-done | bytes 65568 | tf_op jit(solution)/shard_map/ppermute | solution.py:16
  37.1 3.7 %tile_products.4 = (f32[256,128]{1,0:T(8,128)S(1)}, bf16[256,128]{1,0:T(8,128)(2,1)S(1)}, bf16[256,128]{1,0:T(8,128)(2,1)S(1)}, bf16[256,128]{1,0:T(8,128)(2,1)S(1)}) custom-call(s32[64]{0:T(128)S(1)} %get-tuple-element.38.cols_ref, s32[64]{0:T(128)S(1)} %get-tuple-element.37.rows_ref, bf16[64,128,128]{2,1,0:T(8,128)(2,1)S(1)} %bitcast.49, ...), custom_call_target="tpu_custom_call" | custom-call | flops 268435456 | bytes 2097152 | tf_op jit(solution)/shard_map/tile_products/pallas_call | solution.py:70
  41.9 2.4 %collective-permute-start.19 = (bf16[256,128]{1,0:T(8,128)(2,1)S(1)}, bf16[256,128]{1,0:T(8,128)(2,1)S(1)}, u32[]{:S(2)}, u32[]{:S(2)}) collective-permute-start(bf16[256,128]{1,0:T(8,128)(2,1)S(1)} %get-tuple-element.23), channel_id=1, source_target_pairs={{0,24},{8,16},{16,8},{24,0},{1,25},{9,17},{17,9},{25,1},{2,26},{10... | collective-permute-start | bytes 196616 | tf_op jit(solution)/shard_map/ppermute | solution.py:16
  45.2 1.1 %collective-permute-done.18 = bf16[256,128]{1,0:T(8,128)(2,1)S(1)} collective-permute-done((bf16[256,128]{1,0:T(8,128)(2,1)S(1)}, bf16[256,128]{1,0:T(8,128)(2,1)S(1)}, u32[]{:S(2)}, u32[]{:S(2)}) %collective-permute-start.18) | collective-permute-done | bytes 65568 | tf_op jit(solution)/shard_map/ppermute | solution.py:16
  48.1 1.4 %collective-permute-done.30 = f32[4,96,128]{2,1,0:T(8,128)S(1)} collective-permute-done((f32[4,96,128]{2,1,0:T(8,128)S(1)}, f32[4,96,128]{2,1,0:T(8,128)S(1)}, u32[]{:S(2)}, u32[]{:S(2)}) %collective-permute-start.30) | collective-permute-done | bytes 196640 | tf_op jit(solution)/shard_map/ppermute | solution.py:16
  50.0 2.7 %collective-permute-start.33 = (f32[96,128]{1,0:T(8,128)S(1)}, f32[96,128]{1,0:T(8,128)S(1)}, u32[]{:S(2)}, u32[]{:S(2)}) collective-permute-start(f32[96,128]{1,0:T(8,128)S(1)} %get-tuple-element.35), channel_id=1, source_target_pairs={{0,6},{1,7},{2,4},{3,5},{4,2},{5,3},{6,0},{7,1},{8,14},{9,15},{10,... | collective-permute-start | bytes 147464 | tf_op jit(solution)/shard_map/ppermute | solution.py:16
  53.2 2.5 %collective-permute-start.25 = (bf16[256,128]{1,0:T(8,128)(2,1)S(1)}, bf16[256,128]{1,0:T(8,128)(2,1)S(1)}, u32[]{:S(2)}, u32[]{:S(2)}) collective-permute-start(bf16[256,128]{1,0:T(8,128)(2,1)S(1)} %get-tuple-element.30.refs_0_), channel_id=1, source_target_pairs={{0,6},{1,7},{2,4},{3,5},{4,2},{5,3},{6,0},{7,1},{8,14},{9,15},{10,... | collective-permute-start | bytes 196616 | tf_op jit(solution)/shard_map/ppermute | solution.py:16
  55.9 1.7 %collective-permute-start.21 = (bf16[256,128]{1,0:T(8,128)(2,1)S(1)}, bf16[256,128]{1,0:T(8,128)(2,1)S(1)}, u32[]{:S(2)}, u32[]{:S(2)}) collective-permute-start(bf16[256,128]{1,0:T(8,128)(2,1)S(1)} %get-tuple-element.30.refs_0_), channel_id=1, source_target_pairs={{0,2},{1,3},{2,0},{3,1},{4,6},{5,7},{6,4},{7,5},{8,10},{9,11},{10,... | collective-permute-start | bytes 196616 | tf_op jit(solution)/shard_map/ppermute | solution.py:16
  57.6 3.7 %collective-permute-done.32 = f32[96,128]{1,0:T(8,128)S(1)} collective-permute-done((f32[96,128]{1,0:T(8,128)S(1)}, f32[96,128]{1,0:T(8,128)S(1)}, u32[]{:S(2)}, u32[]{:S(2)}) %collective-permute-start.32) | collective-permute-done | bytes 49184 | tf_op jit(solution)/shard_map/ppermute | solution.py:16
  61.3 2.5 %collective-permute-start.36 = (f32[96,128]{1,0:T(8,128)S(1)}, f32[96,128]{1,0:T(8,128)S(1)}, u32[]{:S(2)}, u32[]{:S(2)}) collective-permute-start(f32[96,128]{1,0:T(8,128)S(1)} %fusion.2), channel_id=1, source_target_pairs={{0,24},{8,16},{16,8},{24,0},{1,25},{9,17},{17,9},{25,1},{2,26},{10... | collective-permute-start | bytes 147464 | tf_op jit(solution)/shard_map/ppermute | solution.py:16
  65.4 1.2 %collective-permute-done.36 = f32[96,128]{1,0:T(8,128)S(1)} collective-permute-done((f32[96,128]{1,0:T(8,128)S(1)}, f32[96,128]{1,0:T(8,128)S(1)}, u32[]{:S(2)}, u32[]{:S(2)}) %collective-permute-start.36) | collective-permute-done | bytes 49184 | tf_op jit(solution)/shard_map/ppermute | solution.py:16
  66.6 1.3 %collective-permute-done.35 = f32[96,128]{1,0:T(8,128)S(1)} collective-permute-done((f32[96,128]{1,0:T(8,128)S(1)}, f32[96,128]{1,0:T(8,128)S(1)}, u32[]{:S(2)}, u32[]{:S(2)}) %collective-permute-start.35) | collective-permute-done | bytes 49184 | tf_op jit(solution)/shard_map/ppermute | solution.py:16
  68.4 2.9 %collective-permute-start.39 = (f32[96,128]{1,0:T(8,128)S(1)}, f32[96,128]{1,0:T(8,128)S(1)}, u32[]{:S(2)}, u32[]{:S(2)}) collective-permute-start(f32[96,128]{1,0:T(8,128)S(1)} %add_add_fusion), channel_id=1, source_target_pairs={{0,6},{1,7},{2,4},{3,5},{4,2},{5,3},{6,0},{7,1},{8,14},{9,15},{10,... | collective-permute-start | bytes 147464 | tf_op jit(solution)/shard_map/ppermute | solution.py:16
  71.3 1.5 %collective-permute-start.37 = (f32[96,128]{1,0:T(8,128)S(1)}, f32[96,128]{1,0:T(8,128)S(1)}, u32[]{:S(2)}, u32[]{:S(2)}) collective-permute-start(f32[96,128]{1,0:T(8,128)S(1)} %add_add_fusion), channel_id=1, source_target_pairs={{0,2},{1,3},{2,0},{3,1},{4,6},{5,7},{6,4},{7,5},{8,10},{9,11},{10,... | collective-permute-start | bytes 147464 | tf_op jit(solution)/shard_map/ppermute | solution.py:16
  72.9 3.7 %tile_products.5 = (f32[256,128]{1,0:T(8,128)S(1)}, bf16[256,128]{1,0:T(8,128)(2,1)S(1)}, bf16[256,128]{1,0:T(8,128)(2,1)S(1)}, bf16[256,128]{1,0:T(8,128)(2,1)S(1)}) custom-call(s32[64]{0:T(128)S(1)} %get-tuple-element.38.cols_ref, s32[64]{0:T(128)S(1)} %get-tuple-element.37.rows_ref, bf16[64,128,128]{2,1,0:T(8,128)(2,1)S(1)} %bitcast.50, ...), custom_call_target="tpu_custom_call" | custom-call | flops 268435456 | bytes 2097152 | tf_op jit(solution)/shard_map/tile_products/pallas_call | solution.py:70
  77.2 1.5 %collective-permute-start.28 = (bf16[256,128]{1,0:T(8,128)(2,1)S(1)}, bf16[256,128]{1,0:T(8,128)(2,1)S(1)}, u32[]{:S(2)}, u32[]{:S(2)}) collective-permute-start(bf16[256,128]{1,0:T(8,128)(2,1)S(1)} %get-tuple-element.26), channel_id=1, source_target_pairs={{0,16},{8,24},{16,0},{24,8},{1,17},{9,25},{17,1},{25,9},{2,18},{10... | collective-permute-start | bytes 196616 | tf_op jit(solution)/shard_map/ppermute | solution.py:16
  78.7 1.4 %collective-permute-start.29 = (bf16[256,128]{1,0:T(8,128)(2,1)S(1)}, bf16[256,128]{1,0:T(8,128)(2,1)S(1)}, u32[]{:S(2)}, u32[]{:S(2)}) collective-permute-start(bf16[256,128]{1,0:T(8,128)(2,1)S(1)} %get-tuple-element.27), channel_id=1, source_target_pairs={{0,24},{8,16},{16,8},{24,0},{1,25},{9,17},{17,9},{25,1},{2,26},{10... | collective-permute-start | bytes 196616 | tf_op jit(solution)/shard_map/ppermute | solution.py:16
  81.7 2.1 %collective-permute-done.29 = bf16[256,128]{1,0:T(8,128)(2,1)S(1)} collective-permute-done((bf16[256,128]{1,0:T(8,128)(2,1)S(1)}, bf16[256,128]{1,0:T(8,128)(2,1)S(1)}, u32[]{:S(2)}, u32[]{:S(2)}) %collective-permute-start.29) | collective-permute-done | bytes 65568 | tf_op jit(solution)/shard_map/ppermute | solution.py:16
  84.0 4.7 %finish.1 = (f32[256,128]{1,0:T(8,128)}, f32[256,128]{1,0:T(8,128)}) custom-call(s32[1]{0:T(128)} %bitcast.index_ref, f32[256,128]{1,0:T(8,128)S(1)} %copy-done.2, f32[256,128]{1,0:T(8,128)S(1)} %get-tuple-element.33.z1_ref, f32[256,128]{1,0:T(8,128)S(1)} %get-tuple-element.31.z2_ref, f32[256,128]{1,0:T(8,128)S(1)} %add_multiply_fusion.z3_ref, ...), custom_call_target="tpu_custom_call" | custom-call | tf_op jit(solution)/shard_map/finish/pallas_call | solution.py:201
  (77 shorter events, 14.2 us)
Async XLA Ops:
  1.7 7.7 %collective-permute-start.5 = (bf16[256,128]{1,0:T(8,128)(2,1)S(1)}, bf16[256,128]{1,0:T(8,128)(2,1)S(1)}, u32[]{:S(2)}, u32[]{:S(2)}) collective-permute-start(bf16[256,128]{1,0:T(8,128)(2,1)S(1)} %multiply_convert_fusion.2.refs_0_), channel_id=1, source_target_pairs={{0,6},{1,7},{2,4},{3,5},{4,2},{5,3},{6,0},{7,1},{8,14},{9,15},{10,... | collective-permute-start | bytes 196616 | tf_op jit(solution)/shard_map/ppermute | solution.py:16
  6.8 5.6 %collective-permute-start.3 = (bf16[256,128]{1,0:T(8,128)(2,1)S(1)}, bf16[256,128]{1,0:T(8,128)(2,1)S(1)}, u32[]{:S(2)}, u32[]{:S(2)}) collective-permute-start(bf16[256,128]{1,0:T(8,128)(2,1)S(1)} %multiply_convert_fusion.2.refs_0_), channel_id=1, source_target_pairs={{0,4},{1,5},{2,6},{3,7},{4,0},{5,1},{6,2},{7,3},{8,12},{9,13},{10,... | collective-permute-start | bytes 196616 | tf_op jit(solution)/shard_map/ppermute | solution.py:16
  6.8 5.6 %collective-permute-start.1 = (bf16[256,128]{1,0:T(8,128)(2,1)S(1)}, bf16[256,128]{1,0:T(8,128)(2,1)S(1)}, u32[]{:S(2)}, u32[]{:S(2)}) collective-permute-start(bf16[256,128]{1,0:T(8,128)(2,1)S(1)} %multiply_convert_fusion.2.refs_0_), channel_id=1, source_target_pairs={{0,2},{1,3},{2,0},{3,1},{4,6},{5,7},{6,4},{7,5},{8,10},{9,11},{10,... | collective-permute-start | bytes 196616 | tf_op jit(solution)/shard_map/ppermute | solution.py:16
  7.4 6.2 %collective-permute-start = (bf16[256,128]{1,0:T(8,128)(2,1)S(1)}, bf16[256,128]{1,0:T(8,128)(2,1)S(1)}, u32[]{:S(2)}, u32[]{:S(2)}) collective-permute-start(bf16[256,128]{1,0:T(8,128)(2,1)S(1)} %multiply_convert_fusion.2.refs_0_), channel_id=1, source_target_pairs={{0,1},{1,0},{2,3},{3,2},{4,5},{5,4},{6,7},{7,6},{8,9},{9,8},{10,11... | collective-permute-start | bytes 196616 | tf_op jit(solution)/shard_map/ppermute | solution.py:16
  9.3 4.2 %collective-permute-start.6 = (bf16[256,128]{1,0:T(8,128)(2,1)S(1)}, bf16[256,128]{1,0:T(8,128)(2,1)S(1)}, u32[]{:S(2)}, u32[]{:S(2)}) collective-permute-start(bf16[256,128]{1,0:T(8,128)(2,1)S(1)} %collective-permute-done.5.refs_6_), channel_id=1, source_target_pairs={{0,1},{1,0},{2,3},{3,2},{4,5},{5,4},{6,7},{7,6},{8,9},{9,8},{10,11... | collective-permute-start | bytes 196616 | tf_op jit(solution)/shard_map/ppermute | solution.py:16
  19.1 4.4 %collective-permute-start.7 = (bf16[256,128]{1,0:T(8,128)(2,1)S(1)}, bf16[256,128]{1,0:T(8,128)(2,1)S(1)}, u32[]{:S(2)}, u32[]{:S(2)}) collective-permute-start(bf16[256,128]{1,0:T(8,128)(2,1)S(1)} %get-tuple-element.17), channel_id=1, source_target_pairs={{0,8},{8,0},{16,24},{24,16},{1,9},{9,1},{17,25},{25,17},{2,10},{10... | collective-permute-start | bytes 196616 | tf_op jit(solution)/shard_map/ppermute | solution.py:16
  20.6 4.3 %collective-permute-start.8 = (bf16[256,128]{1,0:T(8,128)(2,1)S(1)}, bf16[256,128]{1,0:T(8,128)(2,1)S(1)}, u32[]{:S(2)}, u32[]{:S(2)}) collective-permute-start(bf16[256,128]{1,0:T(8,128)(2,1)S(1)} %get-tuple-element.18), channel_id=1, source_target_pairs={{0,16},{8,24},{16,0},{24,8},{1,17},{9,25},{17,1},{25,9},{2,18},{10... | collective-permute-start | bytes 196616 | tf_op jit(solution)/shard_map/ppermute | solution.py:16
  22.2 5.2 %collective-permute-start.9 = (bf16[256,128]{1,0:T(8,128)(2,1)S(1)}, bf16[256,128]{1,0:T(8,128)(2,1)S(1)}, u32[]{:S(2)}, u32[]{:S(2)}) collective-permute-start(bf16[256,128]{1,0:T(8,128)(2,1)S(1)} %get-tuple-element.19), channel_id=1, source_target_pairs={{0,24},{8,16},{16,8},{24,0},{1,25},{9,17},{17,9},{25,1},{2,26},{10... | collective-permute-start | bytes 196616 | tf_op jit(solution)/shard_map/ppermute | solution.py:16
  27.5 6.6 %collective-permute-start.15 = (bf16[256,128]{1,0:T(8,128)(2,1)S(1)}, bf16[256,128]{1,0:T(8,128)(2,1)S(1)}, u32[]{:S(2)}, u32[]{:S(2)}) collective-permute-start(bf16[256,128]{1,0:T(8,128)(2,1)S(1)} %get-tuple-element.32.refs_0_), channel_id=1, source_target_pairs={{0,6},{1,7},{2,4},{3,5},{4,2},{5,3},{6,0},{7,1},{8,14},{9,15},{10,... | collective-permute-start | bytes 196616 | tf_op jit(solution)/shard_map/ppermute | solution.py:16
  30.2 5.5 %collective-permute-start.13 = (bf16[256,128]{1,0:T(8,128)(2,1)S(1)}, bf16[256,128]{1,0:T(8,128)(2,1)S(1)}, u32[]{:S(2)}, u32[]{:S(2)}) collective-permute-start(bf16[256,128]{1,0:T(8,128)(2,1)S(1)} %get-tuple-element.32.refs_0_), channel_id=1, source_target_pairs={{0,4},{1,5},{2,6},{3,7},{4,0},{5,1},{6,2},{7,3},{8,12},{9,13},{10,... | collective-permute-start | bytes 196616 | tf_op jit(solution)/shard_map/ppermute | solution.py:16
  30.2 5.5 %collective-permute-start.11 = (bf16[256,128]{1,0:T(8,128)(2,1)S(1)}, bf16[256,128]{1,0:T(8,128)(2,1)S(1)}, u32[]{:S(2)}, u32[]{:S(2)}) collective-permute-start(bf16[256,128]{1,0:T(8,128)(2,1)S(1)} %get-tuple-element.32.refs_0_), channel_id=1, source_target_pairs={{0,2},{1,3},{2,0},{3,1},{4,6},{5,7},{6,4},{7,5},{8,10},{9,11},{10,... | collective-permute-start | bytes 196616 | tf_op jit(solution)/shard_map/ppermute | solution.py:16
  31.9 4.3 %collective-permute-start.10 = (bf16[256,128]{1,0:T(8,128)(2,1)S(1)}, bf16[256,128]{1,0:T(8,128)(2,1)S(1)}, u32[]{:S(2)}, u32[]{:S(2)}) collective-permute-start(bf16[256,128]{1,0:T(8,128)(2,1)S(1)} %get-tuple-element.32.refs_0_), channel_id=1, source_target_pairs={{0,1},{1,0},{2,3},{3,2},{4,5},{5,4},{6,7},{7,6},{8,9},{9,8},{10,11... | collective-permute-start | bytes 196616 | tf_op jit(solution)/shard_map/ppermute | solution.py:16
  40.8 4.4 %collective-permute-start.17 = (bf16[256,128]{1,0:T(8,128)(2,1)S(1)}, bf16[256,128]{1,0:T(8,128)(2,1)S(1)}, u32[]{:S(2)}, u32[]{:S(2)}) collective-permute-start(bf16[256,128]{1,0:T(8,128)(2,1)S(1)} %get-tuple-element.21), channel_id=1, source_target_pairs={{0,8},{8,0},{16,24},{24,16},{1,9},{9,1},{17,25},{25,17},{2,10},{10... | collective-permute-start | bytes 196616 | tf_op jit(solution)/shard_map/ppermute | solution.py:16
  41.4 5.0 %collective-permute-start.18 = (bf16[256,128]{1,0:T(8,128)(2,1)S(1)}, bf16[256,128]{1,0:T(8,128)(2,1)S(1)}, u32[]{:S(2)}, u32[]{:S(2)}) collective-permute-start(bf16[256,128]{1,0:T(8,128)(2,1)S(1)} %get-tuple-element.22), channel_id=1, source_target_pairs={{0,16},{8,24},{16,0},{24,8},{1,17},{9,25},{17,1},{25,9},{2,18},{10... | collective-permute-start | bytes 196616 | tf_op jit(solution)/shard_map/ppermute | solution.py:16
  41.9 5.2 %collective-permute-start.19 = (bf16[256,128]{1,0:T(8,128)(2,1)S(1)}, bf16[256,128]{1,0:T(8,128)(2,1)S(1)}, u32[]{:S(2)}, u32[]{:S(2)}) collective-permute-start(bf16[256,128]{1,0:T(8,128)(2,1)S(1)} %get-tuple-element.23), channel_id=1, source_target_pairs={{0,24},{8,16},{16,8},{24,0},{1,25},{9,17},{17,9},{25,1},{2,26},{10... | collective-permute-start | bytes 196616 | tf_op jit(solution)/shard_map/ppermute | solution.py:16
  49.6 6.2 %collective-permute-start.31 = (f32[96,128]{1,0:T(8,128)S(1)}, f32[96,128]{1,0:T(8,128)S(1)}, u32[]{:S(2)}, u32[]{:S(2)}) collective-permute-start(f32[96,128]{1,0:T(8,128)S(1)} %get-tuple-element.34), channel_id=1, source_target_pairs={{0,2},{1,3},{2,0},{3,1},{4,6},{5,7},{6,4},{7,5},{8,10},{9,11},{10,... | collective-permute-start | bytes 147464 | tf_op jit(solution)/shard_map/ppermute | solution.py:16
  50.0 7.6 %collective-permute-start.33 = (f32[96,128]{1,0:T(8,128)S(1)}, f32[96,128]{1,0:T(8,128)S(1)}, u32[]{:S(2)}, u32[]{:S(2)}) collective-permute-start(f32[96,128]{1,0:T(8,128)S(1)} %get-tuple-element.35), channel_id=1, source_target_pairs={{0,6},{1,7},{2,4},{3,5},{4,2},{5,3},{6,0},{7,1},{8,14},{9,15},{10,... | collective-permute-start | bytes 147464 | tf_op jit(solution)/shard_map/ppermute | solution.py:16
  52.7 8.5 %collective-permute-start.32 = (f32[96,128]{1,0:T(8,128)S(1)}, f32[96,128]{1,0:T(8,128)S(1)}, u32[]{:S(2)}, u32[]{:S(2)}) collective-permute-start(f32[96,128]{1,0:T(8,128)S(1)} %get-tuple-element.36), channel_id=1, source_target_pairs={{0,4},{1,5},{2,6},{3,7},{4,0},{5,1},{6,2},{7,3},{8,12},{9,13},{10,... | collective-permute-start | bytes 147464 | tf_op jit(solution)/shard_map/ppermute | solution.py:16
  53.2 11.1 %collective-permute-start.25 = (bf16[256,128]{1,0:T(8,128)(2,1)S(1)}, bf16[256,128]{1,0:T(8,128)(2,1)S(1)}, u32[]{:S(2)}, u32[]{:S(2)}) collective-permute-start(bf16[256,128]{1,0:T(8,128)(2,1)S(1)} %get-tuple-element.30.refs_0_), channel_id=1, source_target_pairs={{0,6},{1,7},{2,4},{3,5},{4,2},{5,3},{6,0},{7,1},{8,14},{9,15},{10,... | collective-permute-start | bytes 196616 | tf_op jit(solution)/shard_map/ppermute | solution.py:16
  55.7 9.1 %collective-permute-start.23 = (bf16[256,128]{1,0:T(8,128)(2,1)S(1)}, bf16[256,128]{1,0:T(8,128)(2,1)S(1)}, u32[]{:S(2)}, u32[]{:S(2)}) collective-permute-start(bf16[256,128]{1,0:T(8,128)(2,1)S(1)} %get-tuple-element.30.refs_0_), channel_id=1, source_target_pairs={{0,4},{1,5},{2,6},{3,7},{4,0},{5,1},{6,2},{7,3},{8,12},{9,13},{10,... | collective-permute-start | bytes 196616 | tf_op jit(solution)/shard_map/ppermute | solution.py:16
  55.9 9.0 %collective-permute-start.21 = (bf16[256,128]{1,0:T(8,128)(2,1)S(1)}, bf16[256,128]{1,0:T(8,128)(2,1)S(1)}, u32[]{:S(2)}, u32[]{:S(2)}) collective-permute-start(bf16[256,128]{1,0:T(8,128)(2,1)S(1)} %get-tuple-element.30.refs_0_), channel_id=1, source_target_pairs={{0,2},{1,3},{2,0},{3,1},{4,6},{5,7},{6,4},{7,5},{8,10},{9,11},{10,... | collective-permute-start | bytes 196616 | tf_op jit(solution)/shard_map/ppermute | solution.py:16
  61.3 5.3 %collective-permute-start.36 = (f32[96,128]{1,0:T(8,128)S(1)}, f32[96,128]{1,0:T(8,128)S(1)}, u32[]{:S(2)}, u32[]{:S(2)}) collective-permute-start(f32[96,128]{1,0:T(8,128)S(1)} %fusion.2), channel_id=1, source_target_pairs={{0,24},{8,16},{16,8},{24,0},{1,25},{9,17},{17,9},{25,1},{2,26},{10... | collective-permute-start | bytes 147464 | tf_op jit(solution)/shard_map/ppermute | solution.py:16
  64.8 6.5 %collective-permute-start.20 = (bf16[256,128]{1,0:T(8,128)(2,1)S(1)}, bf16[256,128]{1,0:T(8,128)(2,1)S(1)}, u32[]{:S(2)}, u32[]{:S(2)}) collective-permute-start(bf16[256,128]{1,0:T(8,128)(2,1)S(1)} %get-tuple-element.30.refs_0_), channel_id=1, source_target_pairs={{0,1},{1,0},{2,3},{3,2},{4,5},{5,4},{6,7},{7,6},{8,9},{9,8},{10,11... | collective-permute-start | bytes 196616 | tf_op jit(solution)/shard_map/ppermute | solution.py:16
  64.8 6.5 %collective-permute-start.26 = (bf16[256,128]{1,0:T(8,128)(2,1)S(1)}, bf16[256,128]{1,0:T(8,128)(2,1)S(1)}, u32[]{:S(2)}, u32[]{:S(2)}) collective-permute-start(bf16[256,128]{1,0:T(8,128)(2,1)S(1)} %collective-permute-done.25.refs_6_), channel_id=1, source_target_pairs={{0,1},{1,0},{2,3},{3,2},{4,5},{5,4},{6,7},{7,6},{8,9},{9,8},{10,11... | collective-permute-start | bytes 196616 | tf_op jit(solution)/shard_map/ppermute | solution.py:16
  66.6 6.3 %collective-permute-start.24 = (bf16[256,128]{1,0:T(8,128)(2,1)S(1)}, bf16[256,128]{1,0:T(8,128)(2,1)S(1)}, u32[]{:S(2)}, u32[]{:S(2)}) collective-permute-start(bf16[256,128]{1,0:T(8,128)(2,1)S(1)} %collective-permute-done.23.refs_4_), channel_id=1, source_target_pairs={{0,1},{1,0},{2,3},{3,2},{4,5},{5,4},{6,7},{7,6},{8,9},{9,8},{10,11... | collective-permute-start | bytes 196616 | tf_op jit(solution)/shard_map/ppermute | solution.py:16
  67.9 5.0 %collective-permute-start.22 = (bf16[256,128]{1,0:T(8,128)(2,1)S(1)}, bf16[256,128]{1,0:T(8,128)(2,1)S(1)}, u32[]{:S(2)}, u32[]{:S(2)}) collective-permute-start(bf16[256,128]{1,0:T(8,128)(2,1)S(1)} %collective-permute-done.21.refs_2_), channel_id=1, source_target_pairs={{0,1},{1,0},{2,3},{3,2},{4,5},{5,4},{6,7},{7,6},{8,9},{9,8},{10,11... | collective-permute-start | bytes 196616 | tf_op jit(solution)/shard_map/ppermute | solution.py:16
  68.4 10.3 %collective-permute-start.39 = (f32[96,128]{1,0:T(8,128)S(1)}, f32[96,128]{1,0:T(8,128)S(1)}, u32[]{:S(2)}, u32[]{:S(2)}) collective-permute-start(f32[96,128]{1,0:T(8,128)S(1)} %add_add_fusion), channel_id=1, source_target_pairs={{0,6},{1,7},{2,4},{3,5},{4,2},{5,3},{6,0},{7,1},{8,14},{9,15},{10,... | collective-permute-start | bytes 147464 | tf_op jit(solution)/shard_map/ppermute | solution.py:16
  71.3 8.8 %collective-permute-start.38 = (f32[96,128]{1,0:T(8,128)S(1)}, f32[96,128]{1,0:T(8,128)S(1)}, u32[]{:S(2)}, u32[]{:S(2)}) collective-permute-start(f32[96,128]{1,0:T(8,128)S(1)} %add_add_fusion), channel_id=1, source_target_pairs={{0,4},{1,5},{2,6},{3,7},{4,0},{5,1},{6,2},{7,3},{8,12},{9,13},{10,... | collective-permute-start | bytes 147464 | tf_op jit(solution)/shard_map/ppermute | solution.py:16
  71.3 8.8 %collective-permute-start.37 = (f32[96,128]{1,0:T(8,128)S(1)}, f32[96,128]{1,0:T(8,128)S(1)}, u32[]{:S(2)}, u32[]{:S(2)}) collective-permute-start(f32[96,128]{1,0:T(8,128)S(1)} %add_add_fusion), channel_id=1, source_target_pairs={{0,2},{1,3},{2,0},{3,1},{4,6},{5,7},{6,4},{7,5},{8,10},{9,11},{10,... | collective-permute-start | bytes 147464 | tf_op jit(solution)/shard_map/ppermute | solution.py:16
  76.5 4.7 %collective-permute-start.27 = (bf16[256,128]{1,0:T(8,128)(2,1)S(1)}, bf16[256,128]{1,0:T(8,128)(2,1)S(1)}, u32[]{:S(2)}, u32[]{:S(2)}) collective-permute-start(bf16[256,128]{1,0:T(8,128)(2,1)S(1)} %get-tuple-element.25), channel_id=1, source_target_pairs={{0,8},{8,0},{16,24},{24,16},{1,9},{9,1},{17,25},{25,17},{2,10},{10... | collective-permute-start | bytes 196616 | tf_op jit(solution)/shard_map/ppermute | solution.py:16
  77.2 4.6 %collective-permute-start.28 = (bf16[256,128]{1,0:T(8,128)(2,1)S(1)}, bf16[256,128]{1,0:T(8,128)(2,1)S(1)}, u32[]{:S(2)}, u32[]{:S(2)}) collective-permute-start(bf16[256,128]{1,0:T(8,128)(2,1)S(1)} %get-tuple-element.26), channel_id=1, source_target_pairs={{0,16},{8,24},{16,0},{24,8},{1,17},{9,25},{17,1},{25,9},{2,18},{10... | collective-permute-start | bytes 196616 | tf_op jit(solution)/shard_map/ppermute | solution.py:16
  78.7 5.2 %collective-permute-start.29 = (bf16[256,128]{1,0:T(8,128)(2,1)S(1)}, bf16[256,128]{1,0:T(8,128)(2,1)S(1)}, u32[]{:S(2)}, u32[]{:S(2)}) collective-permute-start(bf16[256,128]{1,0:T(8,128)(2,1)S(1)} %get-tuple-element.27), channel_id=1, source_target_pairs={{0,24},{8,16},{16,8},{24,0},{1,25},{9,17},{17,9},{25,1},{2,26},{10... | collective-permute-start | bytes 196616 | tf_op jit(solution)/shard_map/ppermute | solution.py:16
  (15 other events, 191.6 us)

commit v2 on v1

--- a/solution.py
+++ b/solution.py
@@ -8,7 +8,8 @@
 from jax.sharding import PartitionSpec as P
 
 HIGH = lax.Precision.HIGHEST
-VMEM_BYTES = 40 * 1024 * 1024
+VMEM_BYTES = 2 * 1024 * 1024
+DENSE_BYTES = 8 * 1024 * 1024
 
 
 def swap(array, axis, mask):
@@ -79,7 +80,7 @@
             pltpu.VMEM((n_col * sub, width), jnp.bfloat16),
             pltpu.VMEM((n_row * sub + side, width), jnp.float32),
         ],
-        compiler_params=pltpu.CompilerParams(vmem_limit_bytes=VMEM_BYTES),
+        compiler_params=pltpu.CompilerParams(vmem_limit_bytes=8 * VMEM_BYTES),
         cost_estimate=pl.CostEstimate(
             flops=2 * slots * side * side * width,
             bytes_accessed=2 * slots * side * side,
@@ -89,26 +90,87 @@
     )(cols, rows, tiles, *pieces)
 
 
-def gram_kernel(n_col, index_ref, x_ref, z1_ref, z2_ref, near_ref, far_ref, whole):
+def place_kernel(count_ref, cols_ref, rows_ref, tiles_ref, dense_ref):
+    side = tiles_ref.shape[1]
+    dense_ref[...] = jnp.zeros_like(dense_ref)
+
+    def step(slot, carry):
+        row = pl.multiple_of(rows_ref[slot] * side, side)
+        column = pl.multiple_of(cols_ref[slot] * side, side)
+        at = (pl.ds(row, side), pl.ds(column, side))
+        total = dense_ref[at].astype(jnp.float32) + tiles_ref[slot].astype(jnp.float32)
+        dense_ref[at] = total.astype(dense_ref.dtype)
+        return carry
+
+    lax.fori_loop(0, jnp.minimum(count_ref[0], tiles_ref.shape[0]), step, 0)
+
+
+def place_tiles(count, cols, rows, tiles, height, width):
+    return pl.pallas_call(
+        place_kernel,
+        out_shape=jax.ShapeDtypeStruct((height, width), jnp.bfloat16),
+        in_specs=smem(3) + vmem(1),
+        out_specs=vmem(1)[0],
+        compiler_params=pltpu.CompilerParams(vmem_limit_bytes=VMEM_BYTES),
+        cost_estimate=pl.CostEstimate(
+            flops=0, bytes_accessed=4 * height * width, transcendentals=0
+        ),
+        name="place_tiles",
+    )(count, cols, rows, tiles)
+
+
+def dense_kernel(n_col, n_row, dense_ref, *refs):
+    pieces, outs, panel = refs[:n_col], refs[n_col : n_col + n_row], refs[-1]
+    sub = pieces[0].shape[0]
+    for m, piece in enumerate(pieces):
+        panel[m * sub : (m + 1) * sub] = piece[...]
+    for k in range(n_row):
+        part = jnp.dot(
+            dense_ref[k * sub : (k + 1) * sub], panel[...], preferred_element_type=jnp.float32
+        )
+        outs[k][...] = part.astype(outs[k].dtype)
+
+
+def dense_products(dense, pieces, n_row):
+    n_col = len(pieces)
+    sub, width = pieces[0].shape
+    return pl.pallas_call(
+        functools.partial(dense_kernel, n_col, n_row),
+        out_shape=[
+            jax.ShapeDtypeStruct((sub, width), jnp.float32 if k == 0 else jnp.bfloat16)
+            for k in range(n_row)
+        ],
+        in_specs=vmem(1 + n_col),
+        out_specs=vmem(n_row),
+        scratch_shapes=[pltpu.VMEM((n_col * sub, width), jnp.bfloat16)],
+        compiler_params=pltpu.CompilerParams(vmem_limit_bytes=VMEM_BYTES),
+        cost_estimate=pl.CostEstimate(
+            flops=2 * dense.size * width, bytes_accessed=2 * dense.size, transcendentals=0
+        ),
+        name="dense_products",
+    )(dense, *pieces)
+
+
+def gram_kernel(pieces, index_ref, x_ref, z1_ref, z2_ref, near_ref, far_ref, whole):
     x, z1, z2 = x_ref[...], z1_ref[...], z2_ref[...]
     contract = ((0,), (0,))
     for at, (left, right) in enumerate(
         ((x, x), (x, z1), (z1, z1), (x, z2), (z1, z2), (z2, z2))
     ):
         whole[at] = dot(left, right, contract)
-    rows = whole.shape[1] // n_col
-    for m in range(n_col):
+    rows = whole.shape[1] // pieces
+    for m in range(pieces):
         out = far_ref if m % 2 else near_ref
         start = pl.multiple_of((index_ref[0] ^ m) * rows, rows)
         for at in range(whole.shape[0]):
             out[m // 2, at * rows : (at + 1) * rows] = whole[at, pl.ds(start, rows), :]
 
 
-def grams(index, x, z1, z2, n_col):
+def grams(index, x, z1, z2, pieces):
     width = x.shape[1]
-    cut = jax.ShapeDtypeStruct((n_col // 2, 6 * (width // n_col), width), jnp.float32)
-    return pl.pallas_call(
-        functools.partial(gram_kernel, n_col),
+    cut = jax.ShapeDtypeStruct((pieces // 2, 6 * (width // pieces), width), jnp.float32)
+    return pl.pallas_call(
+        functools.partial(gram_kernel, pieces),
         out_shape=[cut, cut],
         in_specs=smem(1) + vmem(3),
         out_specs=vmem(2),
@@ -119,7 +181,7 @@
 
 
 def finish_kernel(
-    n_col,
+    pieces,
     verts_all,
     index_ref,
     x_ref,
@@ -135,8 +197,8 @@
     whole,
 ):
     width = x_ref.shape[1]
-    rows = width // n_col
-    for m in range(n_col):
+    rows = width // pieces
+    for m in range(pieces):
         piece = far_ref if m % 2 else near_ref
         start = pl.multiple_of((index_ref[0] ^ m) * rows, rows)
         for at in range(whole.shape[0]):
@@ -188,23 +250,32 @@
     a0 = mixed[:width, :width] + dot(keep0, f)
     a1 = -(mixed[width:, :width] + mixed[:width, width:] + f)
     a2 = mixed[width:, width:]
-    stacked = jnp.concatenate([a0, a1, a2], axis=0)
-    z1, z2 = z1_ref[...], z2_ref[...]
-    block = dot(jnp.concatenate([x_ref[...], z1, z2], axis=1), stacked)
-    block_ref[...] = block
-    image_ref[...] = block - dot(jnp.concatenate([z1, z2, z3_ref[...]], axis=1), stacked)
-
-
-def finish(index, x, z1, z2, z3, first, second, near, far, n_col, verts_all):
+    none = jnp.zeros_like(a0)
+    spread = jnp.concatenate(
+        [
+            jnp.concatenate([a0, none], axis=1),
+            jnp.concatenate([a1, a0], axis=1),
+            jnp.concatenate([a2, a1], axis=1),
+            jnp.concatenate([none, a2], axis=1),
+        ],
+        axis=0,
+    )
+    basis = jnp.concatenate([x_ref[...], z1_ref[...], z2_ref[...], z3_ref[...]], axis=1)
+    result = dot(basis, spread)
+    block_ref[...] = result[:, :width]
+    image_ref[...] = result[:, :width] - result[:, width:]
+
+
+def finish(index, x, z1, z2, z3, first, second, near, far, pieces, verts_all):
     out = jax.ShapeDtypeStruct(x.shape, jnp.float32)
     width = x.shape[1]
     return pl.pallas_call(
-        functools.partial(finish_kernel, n_col, verts_all),
+        functools.partial(finish_kernel, pieces, verts_all),
         out_shape=[out, out],
         in_specs=smem(1) + vmem(8),
         out_specs=vmem(2),
         scratch_shapes=[pltpu.VMEM((6, width, width), jnp.float32)],
-        compiler_params=pltpu.CompilerParams(vmem_limit_bytes=VMEM_BYTES),
+        compiler_params=pltpu.CompilerParams(vmem_limit_bytes=4 * VMEM_BYTES),
         name="finish",
     )(index, x, z1, z2, z3, first, second, near, far)
 
@@ -228,34 +299,64 @@
     slots = jnp.arange(tiles.shape[0], dtype=jnp.int32)
     cols = ((tile_col[0, 0] // halves) ^ col_at) * halves + tile_col[0, 0] % halves
     rows = ((tile_row[0, 0] // halves) ^ row_at) * halves + tile_row[0, 0] % halves
-    rows = jnp.where(slots < live_count[0, 0], rows, n_row * halves)
-    index = col_at.reshape(1)
+    dense = None
+    if 2 * n_row * n_col * sub * sub <= DENSE_BYTES:
+        dense = place_tiles(live_count[0], cols, rows, tiles, n_row * sub, n_col * sub)
+    else:
+        rows = jnp.where(slots < live_count[0, 0], rows, n_row * halves)
+    width = start_block.shape[1]
     scale = vertex_scale[:, None]
 
-    def adjacency(block):
+    def gather(block, dense=None):
         own = (scale * block).astype(jnp.bfloat16)
         near = [own] + [swap(own, "col", m) for m in range(2, n_col, 2)]
-        far = [swap(piece, "col", 1) for piece in near]
+        if dense is not None:
+            own, dense = lax.optimization_barrier((own, dense))
+        return near, [swap(piece, "col", 1) for piece in [own] + near[1:]]
+
+    def multiply(near, far):
         pieces = [piece for pair in zip(near, far) for piece in pair]
-        parts = tile_products(cols, rows, tiles, pieces, n_row)
+        if dense is None:
+            return tile_products(cols, rows, tiles, pieces, n_row)
+        return dense_products(dense, pieces, n_row)
+
+    def send(parts):
+        return [parts[0]] + [swap(parts[k], "row", k) for k in range(1, n_row)]
+
+    def collect(parts):
         summed = parts[0]
-        for k in range(1, n_row):
-            summed = summed + swap(parts[k], "row", k).astype(jnp.float32)
+        for part in parts[1:]:
+            summed = summed + part.astype(jnp.float32)
         return scale * summed
 
-    z1 = adjacency(start_block)
-    z2 = adjacency(z1)
-    near, far = grams(index, start_block, z1, z2, n_col)
-    near = near + swap(far, "col", 1)
-    mine = near[0]
-    for q in range(1, n_col // 2):
-        mine = mine + swap(near[q], "col", 2 * q)
-    whole = mine
-    for k in range(1, n_row):
-        whole = whole + swap(mine, "row", k)
-    near = jnp.stack([whole] + [swap(whole, "col", m) for m in range(2, n_col, 2)])
-    far = swap(near, "col", 1)
-    z3 = adjacency(z2)
+    inner = [("col", m) for m in range(2, n_col, 2)]
+    outer = [("row", k) for k in range(1, n_row)]
+    place = 2 * row_at + col_at % 2
+    if (width // (2 * n_row)) % 8 != 0:
+        inner, outer, place = outer, inner, col_at
+    index = place.reshape(1)
+
+    def cut_grams(x, z1, z2):
+        near, far = grams(index, x, z1, z2, 2 * (len(outer) + 1))
+        near = near + swap(far, "col", 1)
+        return near[0], [swap(near[q + 1], *hop) for q, hop in enumerate(outer)]
+
+    def add(mine, arrived):
+        for piece in arrived:
+            mine = mine + piece
+        return mine
+
+    z1 = collect(send(multiply(*gather(start_block, dense))))
+    z2 = collect(send(multiply(*gather(z1))))
+    near, far = gather(z2)
+    mine, arrived = cut_grams(start_block, z1, z2)
+    mine = add(mine, arrived)
+    arrived = [swap(mine, *hop) for hop in inner]
+    parts, arrived = lax.optimization_barrier((multiply(near, far), arrived))
+    whole = add(mine, arrived)
+    gram_near = jnp.stack([whole] + [swap(whole, *hop) for hop in outer])
+    gram_far = swap(gram_near, "col", 1)
+    z3 = collect(send(parts))
     return tuple(
         finish(
             index,
@@ -265,9 +366,9 @@
             z3,
             rotation_first,
             rotation_second,
-            near,
-            far,
-            n_col,
+            gram_near,
+            gram_far,
+            2 * gram_near.shape[0],
             verts_all,
         )
     )

time: 88.9 us -> 78.6 us (0.88)
  waiting for transfers between devices: 28.4 us -> 20.8 us
  Pallas kernels: 16.5 us -> 10.7 us
  local copies, waits for them, and re-layouts: 1.63 us -> 3.81 us
  starting transfers between devices: 38.5 us -> 39.5 us
    ppermute x41, waiting for transfers between devices: 28.4 us -> 20.8 us  [swap(): return lax.ppermute(array, axis, [(k, k ^ mask) for k in range(size)])]
    pallas_call x5 -> x6, Pallas kernels: 16.5 us -> 10.7 us  [the longest x1 4.85 us: finish(): pl.pallas_call(functools.partial(finish_kernel, pieces, verts_all), out_s...]
    unnamed x12 -> x14, local copies, waits for them, and re-layouts: 1.62 us -> 3.8 us
    ppermute x41, starting transfers between devices: 38.5 us -> 39.5 us  [swap(): return lax.ppermute(array, axis, [(k, k ^ mask) for k in range(size)])]
  transfers between devices with their start and end apart: 41 -> 41, of which waited for: 21 -> 20; matrix products, arithmetic and copies ran while one was open for 1% -> 1% of each run, Pallas kernels for 4% -> 3%
where the time goes in v2:
time: 78.6 us; the launch traced here: 78.4 us
  starting transfers between devices  39.5 us (50%)
  waiting for transfers between devices  20.8 us (26%)
  Pallas kernels  10.7 us (14%)
  local copies, waits for them, and re-layouts  3.81 us (5%)
  other arithmetic  2.05 us (3%)
  between operations  1.53 us (2%)
    ppermute x41, starting transfers between devices, swap(): return lax.ppermute(array, axis, [(k, k ^ mask) for k in range(size)])  39.5 us
    ppermute x41, waiting for transfers between devices, swap(): return lax.ppermute(array, axis, [(k, k ^ mask) for k in range(size)])  20.8 us
    pallas_call x1, Pallas kernels, finish(): pl.pallas_call(functools.partial(finish_kernel, pieces, verts_all), out_s...  4.85 us
    pallas_call x3, Pallas kernels, dense_products(): pl.pallas_call(functools.partial(dense_kernel, n_col, n_row), out_shape=[...  3.83 us
    unnamed x14, local copies, waits for them, and re-layouts  3.8 us
  transfers between devices with their start and end apart: 41, of which 20 were waited for; matrix products, arithmetic and copies ran while one was open for 1% of the time, Pallas kernels for 3%

profile of v2, /device:TPU:0, one launch (start us, length us, event | category | flops | bytes accessed | tf_op | source)
XLA Modules:
  0.0 78.4 jit_solution(8504018487047902484)
XLA Ops:
  0.6 1.0 %multiply_convert_fusion.2.refs_0_ = bf16[256,128]{1,0:T(8,128)(2,1)S(1)} fusion(f32[256,128]{1,0:T(8,128)} %x_ref.3, f32[256]{0:T(256)} %param.9), kind=kLoop, calls=%fused_computation.6 | loop fusion | flops 65536 | bytes 197632 | tf_op jit(solution)/shard_map/convert_element_type | solution.py:311
  1.6 5.1 %collective-permute-start.5 = (bf16[256,128]{1,0:T(8,128)(2,1)S(1)}, bf16[256,128]{1,0:T(8,128)(2,1)S(1)}, u32[]{:S(2)}, u32[]{:S(2)}) collective-permute-start(bf16[256,128]{1,0:T(8,128)(2,1)S(1)} %multiply_convert_fusion.2.refs_0_), channel_id=1, source_target_pairs={{0,6},{1,7},{2,4},{3,5},{4,2},{5,3},{6,0},{7,1},{8,14},{9,15},{10,... | collective-permute-start | bytes 196616 | tf_op jit(solution)/shard_map/ppermute | solution.py:17
  8.7 1.6 %copy-done.2 = bf16[1,1,64,128,128]{4,3,2,1,0:T(8,128)(2,1)S(1)} copy-done((bf16[1,1,64,128,128]{4,3,2,1,0:T(8,128)(2,1)S(1)}, bf16[1,1,64,128,128]{4,3,2,1,0:T(8,128)(2,1)}, u32[]{:S(2)}) %copy-start.2) | copy-done | bytes 2097176
  10.3 1.1 %place_tiles.1.dense_ref = bf16[1024,2048]{1,0:T(8,128)(2,1)S(1)} custom-call(s32[1]{0:T(128)} %bitcast.47.count_ref, s32[64]{0:T(128)S(1)} %get-tuple-element.53.cols_ref, s32[64]{0:T(128)S(1)} %get-tuple-element.54.rows_ref, bf16[64,128,128]{2,1,0:T(8,128)(2,1)S(1)} %bitcast.48), custom_call_target="tpu_custom_call" | custom-call | bytes 8388608 | tf_op jit(solution)/shard_map/place_tiles/pallas_call | solution.py:109
  13.8 1.3 %dense_products.3 = (f32[256,128]{1,0:T(8,128)S(1)}, bf16[256,128]{1,0:T(8,128)(2,1)S(1)}, bf16[256,128]{1,0:T(8,128)(2,1)S(1)}, bf16[256,128]{1,0:T(8,128)(2,1)S(1)}) custom-call(bf16[1024,2048]{1,0:T(8,128)(2,1)S(1)} %place_tiles.1.dense_ref, bf16[256,128]{1,0:T(8,128)(2,1)S(1)} %multiply_convert_fusion.2.refs_0_, ...), custom_call_target="tpu_custom_call" | custom-call | flops 536870912 | bytes 4194304 | tf_op jit(solution)/shard_map/dense_products/pallas_call | solution.py:137
  15.1 1.9 %collective-permute-start.7 = (bf16[256,128]{1,0:T(8,128)(2,1)S(1)}, bf16[256,128]{1,0:T(8,128)(2,1)S(1)}, u32[]{:S(2)}, u32[]{:S(2)}) collective-permute-start(bf16[256,128]{1,0:T(8,128)(2,1)S(1)} %get-tuple-element.26), channel_id=1, source_target_pairs={{0,8},{8,0},{16,24},{24,16},{1,9},{9,1},{17,25},{25,17},{2,10},{10... | collective-permute-start | bytes 196616 | tf_op jit(solution)/shard_map/ppermute | solution.py:17
  17.0 1.3 %collective-permute-start.8 = (bf16[256,128]{1,0:T(8,128)(2,1)S(1)}, bf16[256,128]{1,0:T(8,128)(2,1)S(1)}, u32[]{:S(2)}, u32[]{:S(2)}) collective-permute-start(bf16[256,128]{1,0:T(8,128)(2,1)S(1)} %get-tuple-element.27), channel_id=1, source_target_pairs={{0,16},{8,24},{16,0},{24,8},{1,17},{9,25},{17,1},{25,9},{2,18},{10... | collective-permute-start | bytes 196616 | tf_op jit(solution)/shard_map/ppermute | solution.py:17
  19.6 1.7 %collective-permute-done.8 = bf16[256,128]{1,0:T(8,128)(2,1)S(1)} collective-permute-done((bf16[256,128]{1,0:T(8,128)(2,1)S(1)}, bf16[256,128]{1,0:T(8,128)(2,1)S(1)}, u32[]{:S(2)}, u32[]{:S(2)}) %collective-permute-start.8) | collective-permute-done | bytes 65568 | tf_op jit(solution)/shard_map/ppermute | solution.py:17
  21.3 2.2 %collective-permute-done.9 = bf16[256,128]{1,0:T(8,128)(2,1)S(1)} collective-permute-done((bf16[256,128]{1,0:T(8,128)(2,1)S(1)}, bf16[256,128]{1,0:T(8,128)(2,1)S(1)}, u32[]{:S(2)}, u32[]{:S(2)}) %collective-permute-start.9) | collective-permute-done | bytes 65568 | tf_op jit(solution)/shard_map/ppermute | solution.py:17
  23.6 3.8 %collective-permute-start.15 = (bf16[256,128]{1,0:T(8,128)(2,1)S(1)}, bf16[256,128]{1,0:T(8,128)(2,1)S(1)}, u32[]{:S(2)}, u32[]{:S(2)}) collective-permute-start(bf16[256,128]{1,0:T(8,128)(2,1)S(1)} %get-tuple-element.48.refs_0_), channel_id=1, source_target_pairs={{0,6},{1,7},{2,4},{3,5},{4,2},{5,3},{6,0},{7,1},{8,14},{9,15},{10,... | collective-permute-start | bytes 196616 | tf_op jit(solution)/shard_map/ppermute | solution.py:17
  28.0 1.7 %collective-permute-done.15.refs_6_ = bf16[256,128]{1,0:T(8,128)(2,1)S(1)} collective-permute-done((bf16[256,128]{1,0:T(8,128)(2,1)S(1)}, bf16[256,128]{1,0:T(8,128)(2,1)S(1)}, u32[]{:S(2)}, u32[]{:S(2)}) %collective-permute-start.15) | collective-permute-done | bytes 65568 | tf_op jit(solution)/shard_map/ppermute | solution.py:17
  29.7 2.8 %collective-permute-done.13.refs_4_ = bf16[256,128]{1,0:T(8,128)(2,1)S(1)} collective-permute-done((bf16[256,128]{1,0:T(8,128)(2,1)S(1)}, bf16[256,128]{1,0:T(8,128)(2,1)S(1)}, u32[]{:S(2)}, u32[]{:S(2)}) %collective-permute-start.13) | collective-permute-done | bytes 65568 | tf_op jit(solution)/shard_map/ppermute | solution.py:17
  33.9 1.3 %dense_products.4 = (f32[256,128]{1,0:T(8,128)S(1)}, bf16[256,128]{1,0:T(8,128)(2,1)S(1)}, bf16[256,128]{1,0:T(8,128)(2,1)S(1)}, bf16[256,128]{1,0:T(8,128)(2,1)S(1)}) custom-call(bf16[1024,2048]{1,0:T(8,128)(2,1)S(1)} %place_tiles.1.dense_ref, bf16[256,128]{1,0:T(8,128)(2,1)S(1)} %get-tuple-element.48.refs_0_, ...), custom_call_target="tpu_custom_call" | custom-call | flops 536870912 | bytes 4194304 | tf_op jit(solution)/shard_map/dense_products/pallas_call | solution.py:137
  36.4 2.4 %collective-permute-start.19 = (bf16[256,128]{1,0:T(8,128)(2,1)S(1)}, bf16[256,128]{1,0:T(8,128)(2,1)S(1)}, u32[]{:S(2)}, u32[]{:S(2)}) collective-permute-start(bf16[256,128]{1,0:T(8,128)(2,1)S(1)} %get-tuple-element.32), channel_id=1, source_target_pairs={{0,24},{8,16},{16,8},{24,0},{1,25},{9,17},{17,9},{25,1},{2,26},{10... | collective-permute-start | bytes 196616 | tf_op jit(solution)/shard_map/ppermute | solution.py:17
  40.4 1.2 %collective-permute-done.19 = bf16[256,128]{1,0:T(8,128)(2,1)S(1)} collective-permute-done((bf16[256,128]{1,0:T(8,128)(2,1)S(1)}, bf16[256,128]{1,0:T(8,128)(2,1)S(1)}, u32[]{:S(2)}, u32[]{:S(2)}) %collective-permute-start.19) | collective-permute-done | bytes 65568 | tf_op jit(solution)/shard_map/ppermute | solution.py:17
  42.6 2.4 %collective-permute-start.25 = (bf16[256,128]{1,0:T(8,128)(2,1)S(1)}, bf16[256,128]{1,0:T(8,128)(2,1)S(1)}, u32[]{:S(2)}, u32[]{:S(2)}) collective-permute-start(bf16[256,128]{1,0:T(8,128)(2,1)S(1)} %get-tuple-element.46.refs_0_), channel_id=1, source_target_pairs={{0,6},{1,7},{2,4},{3,5},{4,2},{5,3},{6,0},{7,1},{8,14},{9,15},{10,... | collective-permute-start | bytes 196616 | tf_op jit(solution)/shard_map/ppermute | solution.py:17
  45.0 2.0 %collective-permute-start.21 = (bf16[256,128]{1,0:T(8,128)(2,1)S(1)}, bf16[256,128]{1,0:T(8,128)(2,1)S(1)}, u32[]{:S(2)}, u32[]{:S(2)}) collective-permute-start(bf16[256,128]{1,0:T(8,128)(2,1)S(1)} %get-tuple-element.46.refs_0_), channel_id=1, source_target_pairs={{0,2},{1,3},{2,0},{3,1},{4,6},{5,7},{6,4},{7,5},{8,10},{9,11},{10,... | collective-permute-start | bytes 196616 | tf_op jit(solution)/shard_map/ppermute | solution.py:17
  47.1 2.0 %collective-permute-start.28 = (f32[96,128]{1,0:T(8,128)S(1)}, f32[96,128]{1,0:T(8,128)S(1)}, u32[]{:S(2)}, u32[]{:S(2)}) collective-permute-start(f32[96,128]{1,0:T(8,128)S(1)} %get-tuple-element.50), channel_id=1, source_target_pairs={{0,8},{8,0},{16,24},{24,16},{1,9},{9,1},{17,25},{25,17},{2,10},{10... | collective-permute-start | bytes 147464 | tf_op jit(solution)/shard_map/ppermute | solution.py:17
  49.1 1.0 %collective-permute-start.30 = (f32[96,128]{1,0:T(8,128)S(1)}, f32[96,128]{1,0:T(8,128)S(1)}, u32[]{:S(2)}, u32[]{:S(2)}) collective-permute-start(f32[96,128]{1,0:T(8,128)S(1)} %get-tuple-element.51), channel_id=1, source_target_pairs={{0,24},{8,16},{16,8},{24,0},{1,25},{9,17},{17,9},{25,1},{2,26},{10... | collective-permute-start | bytes 147464 | tf_op jit(solution)/shard_map/ppermute | solution.py:17
  52.3 1.8 %collective-permute-done.30 = f32[96,128]{1,0:T(8,128)S(1)} collective-permute-done((f32[96,128]{1,0:T(8,128)S(1)}, f32[96,128]{1,0:T(8,128)S(1)}, u32[]{:S(2)}, u32[]{:S(2)}) %collective-permute-start.30) | collective-permute-done | bytes 49184 | tf_op jit(solution)/shard_map/ppermute | solution.py:17
  54.6 2.1 %collective-permute-start.33 = (f32[96,128]{1,0:T(8,128)S(1)}, f32[96,128]{1,0:T(8,128)S(1)}, u32[]{:S(2)}, u32[]{:S(2)}) collective-permute-start(f32[96,128]{1,0:T(8,128)S(1)} %fusion.2), channel_id=1, source_target_pairs={{0,6},{1,7},{2,4},{3,5},{4,2},{5,3},{6,0},{7,1},{8,14},{9,15},{10,... | collective-permute-start | bytes 147464 | tf_op jit(solution)/shard_map/ppermute | solution.py:17
  56.8 2.3 %collective-permute-start.31 = (f32[96,128]{1,0:T(8,128)S(1)}, f32[96,128]{1,0:T(8,128)S(1)}, u32[]{:S(2)}, u32[]{:S(2)}) collective-permute-start(f32[96,128]{1,0:T(8,128)S(1)} %fusion.2), channel_id=1, source_target_pairs={{0,2},{1,3},{2,0},{3,1},{4,6},{5,7},{6,4},{7,5},{8,10},{9,11},{10,... | collective-permute-start | bytes 147464 | tf_op jit(solution)/shard_map/ppermute | solution.py:17
  59.1 2.2 %copy-done.1 = bf16[1024,2048]{1,0:T(8,128)(2,1)S(1)} copy-done((bf16[1024,2048]{1,0:T(8,128)(2,1)S(1)}, bf16[1024,2048]{1,0:T(8,128)(2,1)}, u32[]{:S(2)}) %copy-start.1) | copy-done | bytes 4194328
  61.3 1.3 %dense_products.5 = (f32[256,128]{1,0:T(8,128)S(1)}, bf16[256,128]{1,0:T(8,128)(2,1)S(1)}, bf16[256,128]{1,0:T(8,128)(2,1)S(1)}, bf16[256,128]{1,0:T(8,128)(2,1)S(1)}) custom-call(bf16[1024,2048]{1,0:T(8,128)(2,1)S(1)} %copy-done.1, bf16[256,128]{1,0:T(8,128)(2,1)S(1)} %get-tuple-element.46.refs_0_, bf16[256,128]{1,0:T(8,128)(2,1)S(1)} %collective-permute-done.20.refs_1_, ...), custom_call_target="tpu_custom_call" | custom-call | flops 536870912 | bytes 4194304 | tf_op jit(solution)/shard_map/dense_products/pallas_call | solution.py:137
  62.6 1.6 %collective-permute-start.39 = (f32[96,128]{1,0:T(8,128)S(1)}, f32[96,128]{1,0:T(8,128)S(1)}, u32[]{:S(2)}, u32[]{:S(2)}) collective-permute-start(f32[96,128]{1,0:T(8,128)S(1)} %add_add_fusion), channel_id=1, source_target_pairs={{0,24},{8,16},{16,8},{24,0},{1,25},{9,17},{17,9},{25,1},{2,26},{10... | collective-permute-start | bytes 147464 | tf_op jit(solution)/shard_map/ppermute | solution.py:17
  64.2 1.0 %collective-permute-start.38 = (f32[96,128]{1,0:T(8,128)S(1)}, f32[96,128]{1,0:T(8,128)S(1)}, u32[]{:S(2)}, u32[]{:S(2)}) collective-permute-start(f32[96,128]{1,0:T(8,128)S(1)} %add_add_fusion), channel_id=1, source_target_pairs={{0,16},{8,24},{16,0},{24,8},{1,17},{9,25},{17,1},{25,9},{2,18},{10... | collective-permute-start | bytes 147464 | tf_op jit(solution)/shard_map/ppermute | solution.py:17
  66.2 1.1 %collective-permute-start.34 = (bf16[256,128]{1,0:T(8,128)(2,1)S(1)}, bf16[256,128]{1,0:T(8,128)(2,1)S(1)}, u32[]{:S(2)}, u32[]{:S(2)}) collective-permute-start(bf16[256,128]{1,0:T(8,128)(2,1)S(1)} %get-tuple-element.40), channel_id=1, source_target_pairs={{0,8},{8,0},{16,24},{24,16},{1,9},{9,1},{17,25},{25,17},{2,10},{10... | collective-permute-start | bytes 196616 | tf_op jit(solution)/shard_map/ppermute | solution.py:17
  67.2 1.0 %collective-permute-start.35 = (bf16[256,128]{1,0:T(8,128)(2,1)S(1)}, bf16[256,128]{1,0:T(8,128)(2,1)S(1)}, u32[]{:S(2)}, u32[]{:S(2)}) collective-permute-start(bf16[256,128]{1,0:T(8,128)(2,1)S(1)} %get-tuple-element.41), channel_id=1, source_target_pairs={{0,16},{8,24},{16,0},{24,8},{1,17},{9,25},{17,1},{25,9},{2,18},{10... | collective-permute-start | bytes 196616 | tf_op jit(solution)/shard_map/ppermute | solution.py:17
  68.2 1.4 %collective-permute-start.36 = (bf16[256,128]{1,0:T(8,128)(2,1)S(1)}, bf16[256,128]{1,0:T(8,128)(2,1)S(1)}, u32[]{:S(2)}, u32[]{:S(2)}) collective-permute-start(bf16[256,128]{1,0:T(8,128)(2,1)S(1)} %get-tuple-element.42), channel_id=1, source_target_pairs={{0,24},{8,16},{16,8},{24,0},{1,25},{9,17},{17,9},{25,1},{2,26},{10... | collective-permute-start | bytes 196616 | tf_op jit(solution)/shard_map/ppermute | solution.py:17
  69.8 1.0 %collective-permute-done.34 = bf16[256,128]{1,0:T(8,128)(2,1)S(1)} collective-permute-done((bf16[256,128]{1,0:T(8,128)(2,1)S(1)}, bf16[256,128]{1,0:T(8,128)(2,1)S(1)}, u32[]{:S(2)}, u32[]{:S(2)}) %collective-permute-start.34) | collective-permute-done | bytes 65568 | tf_op jit(solution)/shard_map/ppermute | solution.py:17
  71.5 1.9 %collective-permute-done.36 = bf16[256,128]{1,0:T(8,128)(2,1)S(1)} collective-permute-done((bf16[256,128]{1,0:T(8,128)(2,1)S(1)}, bf16[256,128]{1,0:T(8,128)(2,1)S(1)}, u32[]{:S(2)}, u32[]{:S(2)}) %collective-permute-start.36) | collective-permute-done | bytes 65568 | tf_op jit(solution)/shard_map/ppermute | solution.py:17
  73.5 4.8 %finish.1 = (f32[256,128]{1,0:T(8,128)}, f32[256,128]{1,0:T(8,128)}) custom-call(s32[1]{0:T(128)} %bitcast.index_ref, f32[256,128]{1,0:T(8,128)S(1)} %copy-done.3, f32[256,128]{1,0:T(8,128)S(1)} %get-tuple-element.49.z1_ref, f32[256,128]{1,0:T(8,128)S(1)} %get-tuple-element.47.z2_ref, f32[256,128]{1,0:T(8,128)S(1)} %add_multiply_fusion.z3_ref, ...), custom_call_target="tpu_custom_call" | custom-call | tf_op jit(solution)/shard_map/finish/pallas_call | solution.py:272
  (80 shorter events, 15.6 us)
Async XLA Ops:
  1.6 10.0 %collective-permute-start.5 = (bf16[256,128]{1,0:T(8,128)(2,1)S(1)}, bf16[256,128]{1,0:T(8,128)(2,1)S(1)}, u32[]{:S(2)}, u32[]{:S(2)}) collective-permute-start(bf16[256,128]{1,0:T(8,128)(2,1)S(1)} %multiply_convert_fusion.2.refs_0_), channel_id=1, source_target_pairs={{0,6},{1,7},{2,4},{3,5},{4,2},{5,3},{6,0},{7,1},{8,14},{9,15},{10,... | collective-permute-start | bytes 196616 | tf_op jit(solution)/shard_map/ppermute | solution.py:17
  6.8 5.6 %collective-permute-start.3 = (bf16[256,128]{1,0:T(8,128)(2,1)S(1)}, bf16[256,128]{1,0:T(8,128)(2,1)S(1)}, u32[]{:S(2)}, u32[]{:S(2)}) collective-permute-start(bf16[256,128]{1,0:T(8,128)(2,1)S(1)} %multiply_convert_fusion.2.refs_0_), channel_id=1, source_target_pairs={{0,4},{1,5},{2,6},{3,7},{4,0},{5,1},{6,2},{7,3},{8,12},{9,13},{10,... | collective-permute-start | bytes 196616 | tf_op jit(solution)/shard_map/ppermute | solution.py:17
  6.8 5.6 %collective-permute-start.1 = (bf16[256,128]{1,0:T(8,128)(2,1)S(1)}, bf16[256,128]{1,0:T(8,128)(2,1)S(1)}, u32[]{:S(2)}, u32[]{:S(2)}) collective-permute-start(bf16[256,128]{1,0:T(8,128)(2,1)S(1)} %multiply_convert_fusion.2.refs_0_), channel_id=1, source_target_pairs={{0,2},{1,3},{2,0},{3,1},{4,6},{5,7},{6,4},{7,5},{8,10},{9,11},{10,... | collective-permute-start | bytes 196616 | tf_op jit(solution)/shard_map/ppermute | solution.py:17
  15.1 4.6 %collective-permute-start.7 = (bf16[256,128]{1,0:T(8,128)(2,1)S(1)}, bf16[256,128]{1,0:T(8,128)(2,1)S(1)}, u32[]{:S(2)}, u32[]{:S(2)}) collective-permute-start(bf16[256,128]{1,0:T(8,128)(2,1)S(1)} %get-tuple-element.26), channel_id=1, source_target_pairs={{0,8},{8,0},{16,24},{24,16},{1,9},{9,1},{17,25},{25,17},{2,10},{10... | collective-permute-start | bytes 196616 | tf_op jit(solution)/shard_map/ppermute | solution.py:17
  18.3 5.2 %collective-permute-start.9 = (bf16[256,128]{1,0:T(8,128)(2,1)S(1)}, bf16[256,128]{1,0:T(8,128)(2,1)S(1)}, u32[]{:S(2)}, u32[]{:S(2)}) collective-permute-start(bf16[256,128]{1,0:T(8,128)(2,1)S(1)} %get-tuple-element.28), channel_id=1, source_target_pairs={{0,24},{8,16},{16,8},{24,0},{1,25},{9,17},{17,9},{25,1},{2,26},{10... | collective-permute-start | bytes 196616 | tf_op jit(solution)/shard_map/ppermute | solution.py:17
  23.6 6.1 %collective-permute-start.15 = (bf16[256,128]{1,0:T(8,128)(2,1)S(1)}, bf16[256,128]{1,0:T(8,128)(2,1)S(1)}, u32[]{:S(2)}, u32[]{:S(2)}) collective-permute-start(bf16[256,128]{1,0:T(8,128)(2,1)S(1)} %get-tuple-element.48.refs_0_), channel_id=1, source_target_pairs={{0,6},{1,7},{2,4},{3,5},{4,2},{5,3},{6,0},{7,1},{8,14},{9,15},{10,... | collective-permute-start | bytes 196616 | tf_op jit(solution)/shard_map/ppermute | solution.py:17
  27.3 5.2 %collective-permute-start.13 = (bf16[256,128]{1,0:T(8,128)(2,1)S(1)}, bf16[256,128]{1,0:T(8,128)(2,1)S(1)}, u32[]{:S(2)}, u32[]{:S(2)}) collective-permute-start(bf16[256,128]{1,0:T(8,128)(2,1)S(1)} %get-tuple-element.48.refs_0_), channel_id=1, source_target_pairs={{0,4},{1,5},{2,6},{3,7},{4,0},{5,1},{6,2},{7,3},{8,12},{9,13},{10,... | collective-permute-start | bytes 196616 | tf_op jit(solution)/shard_map/ppermute | solution.py:17
  27.3 5.2 %collective-permute-start.11 = (bf16[256,128]{1,0:T(8,128)(2,1)S(1)}, bf16[256,128]{1,0:T(8,128)(2,1)S(1)}, u32[]{:S(2)}, u32[]{:S(2)}) collective-permute-start(bf16[256,128]{1,0:T(8,128)(2,1)S(1)} %get-tuple-element.48.refs_0_), channel_id=1, source_target_pairs={{0,2},{1,3},{2,0},{3,1},{4,6},{5,7},{6,4},{7,5},{8,10},{9,11},{10,... | collective-permute-start | bytes 196616 | tf_op jit(solution)/shard_map/ppermute | solution.py:17
  28.0 5.0 %collective-permute-start.10 = (bf16[256,128]{1,0:T(8,128)(2,1)S(1)}, bf16[256,128]{1,0:T(8,128)(2,1)S(1)}, u32[]{:S(2)}, u32[]{:S(2)}) collective-permute-start(bf16[256,128]{1,0:T(8,128)(2,1)S(1)} %get-tuple-element.48.refs_0_), channel_id=1, source_target_pairs={{0,1},{1,0},{2,3},{3,2},{4,5},{5,4},{6,7},{7,6},{8,9},{9,8},{10,11... | collective-permute-start | bytes 196616 | tf_op jit(solution)/shard_map/ppermute | solution.py:17
  35.2 4.4 %collective-permute-start.17 = (bf16[256,128]{1,0:T(8,128)(2,1)S(1)}, bf16[256,128]{1,0:T(8,128)(2,1)S(1)}, u32[]{:S(2)}, u32[]{:S(2)}) collective-permute-start(bf16[256,128]{1,0:T(8,128)(2,1)S(1)} %get-tuple-element.30), channel_id=1, source_target_pairs={{0,8},{8,0},{16,24},{24,16},{1,9},{9,1},{17,25},{25,17},{2,10},{10... | collective-permute-start | bytes 196616 | tf_op jit(solution)/shard_map/ppermute | solution.py:17
  35.8 4.6 %collective-permute-start.18 = (bf16[256,128]{1,0:T(8,128)(2,1)S(1)}, bf16[256,128]{1,0:T(8,128)(2,1)S(1)}, u32[]{:S(2)}, u32[]{:S(2)}) collective-permute-start(bf16[256,128]{1,0:T(8,128)(2,1)S(1)} %get-tuple-element.31), channel_id=1, source_target_pairs={{0,16},{8,24},{16,0},{24,8},{1,17},{9,25},{17,1},{25,9},{2,18},{10... | collective-permute-start | bytes 196616 | tf_op jit(solution)/shard_map/ppermute | solution.py:17
  36.4 5.2 %collective-permute-start.19 = (bf16[256,128]{1,0:T(8,128)(2,1)S(1)}, bf16[256,128]{1,0:T(8,128)(2,1)S(1)}, u32[]{:S(2)}, u32[]{:S(2)}) collective-permute-start(bf16[256,128]{1,0:T(8,128)(2,1)S(1)} %get-tuple-element.32), channel_id=1, source_target_pairs={{0,24},{8,16},{16,8},{24,0},{1,25},{9,17},{17,9},{25,1},{2,26},{10... | collective-permute-start | bytes 196616 | tf_op jit(solution)/shard_map/ppermute | solution.py:17
  42.5 4.5 %collective-permute-start.27 = (f32[4,96,128]{2,1,0:T(8,128)S(1)}, f32[4,96,128]{2,1,0:T(8,128)S(1)}, u32[]{:S(2)}, u32[]{:S(2)}) collective-permute-start(f32[4,96,128]{2,1,0:T(8,128)S(1)} %get-tuple-element.38), channel_id=1, source_target_pairs={{0,1},{1,0},{2,3},{3,2},{4,5},{5,4},{6,7},{7,6},{8,9},{9,8},{10,11... | collective-permute-start | bytes 589832 | tf_op jit(solution)/shard_map/ppermute | solution.py:17
  42.6 7.5 %collective-permute-start.25 = (bf16[256,128]{1,0:T(8,128)(2,1)S(1)}, bf16[256,128]{1,0:T(8,128)(2,1)S(1)}, u32[]{:S(2)}, u32[]{:S(2)}) collective-permute-start(bf16[256,128]{1,0:T(8,128)(2,1)S(1)} %get-tuple-element.46.refs_0_), channel_id=1, source_target_pairs={{0,6},{1,7},{2,4},{3,5},{4,2},{5,3},{6,0},{7,1},{8,14},{9,15},{10,... | collective-permute-start | bytes 196616 | tf_op jit(solution)/shard_map/ppermute | solution.py:17
  45.0 6.7 %collective-permute-start.23 = (bf16[256,128]{1,0:T(8,128)(2,1)S(1)}, bf16[256,128]{1,0:T(8,128)(2,1)S(1)}, u32[]{:S(2)}, u32[]{:S(2)}) collective-permute-start(bf16[256,128]{1,0:T(8,128)(2,1)S(1)} %get-tuple-element.46.refs_0_), channel_id=1, source_target_pairs={{0,4},{1,5},{2,6},{3,7},{4,0},{5,1},{6,2},{7,3},{8,12},{9,13},{10,... | collective-permute-start | bytes 196616 | tf_op jit(solution)/shard_map/ppermute | solution.py:17
  45.0 6.7 %collective-permute-start.21 = (bf16[256,128]{1,0:T(8,128)(2,1)S(1)}, bf16[256,128]{1,0:T(8,128)(2,1)S(1)}, u32[]{:S(2)}, u32[]{:S(2)}) collective-permute-start(bf16[256,128]{1,0:T(8,128)(2,1)S(1)} %get-tuple-element.46.refs_0_), channel_id=1, source_target_pairs={{0,2},{1,3},{2,0},{3,1},{4,6},{5,7},{6,4},{7,5},{8,10},{9,11},{10,... | collective-permute-start | bytes 196616 | tf_op jit(solution)/shard_map/ppermute | solution.py:17
  47.1 5.1 %collective-permute-start.28 = (f32[96,128]{1,0:T(8,128)S(1)}, f32[96,128]{1,0:T(8,128)S(1)}, u32[]{:S(2)}, u32[]{:S(2)}) collective-permute-start(f32[96,128]{1,0:T(8,128)S(1)} %get-tuple-element.50), channel_id=1, source_target_pairs={{0,8},{8,0},{16,24},{24,16},{1,9},{9,1},{17,25},{25,17},{2,10},{10... | collective-permute-start | bytes 147464 | tf_op jit(solution)/shard_map/ppermute | solution.py:17
  49.1 5.0 %collective-permute-start.30 = (f32[96,128]{1,0:T(8,128)S(1)}, f32[96,128]{1,0:T(8,128)S(1)}, u32[]{:S(2)}, u32[]{:S(2)}) collective-permute-start(f32[96,128]{1,0:T(8,128)S(1)} %get-tuple-element.51), channel_id=1, source_target_pairs={{0,24},{8,16},{16,8},{24,0},{1,25},{9,17},{17,9},{25,1},{2,26},{10... | collective-permute-start | bytes 147464 | tf_op jit(solution)/shard_map/ppermute | solution.py:17
  50.1 4.5 %collective-permute-start.29 = (f32[96,128]{1,0:T(8,128)S(1)}, f32[96,128]{1,0:T(8,128)S(1)}, u32[]{:S(2)}, u32[]{:S(2)}) collective-permute-start(f32[96,128]{1,0:T(8,128)S(1)} %get-tuple-element.52), channel_id=1, source_target_pairs={{0,16},{8,24},{16,0},{24,8},{1,17},{9,25},{17,1},{25,9},{2,18},{10... | collective-permute-start | bytes 147464 | tf_op jit(solution)/shard_map/ppermute | solution.py:17
  51.7 5.0 %collective-permute-start.20 = (bf16[256,128]{1,0:T(8,128)(2,1)S(1)}, bf16[256,128]{1,0:T(8,128)(2,1)S(1)}, u32[]{:S(2)}, u32[]{:S(2)}) collective-permute-start(bf16[256,128]{1,0:T(8,128)(2,1)S(1)} %get-tuple-element.46.refs_0_), channel_id=1, source_target_pairs={{0,1},{1,0},{2,3},{3,2},{4,5},{5,4},{6,7},{7,6},{8,9},{9,8},{10,11... | collective-permute-start | bytes 196616 | tf_op jit(solution)/shard_map/ppermute | solution.py:17
  51.8 5.0 %collective-permute-start.26 = (bf16[256,128]{1,0:T(8,128)(2,1)S(1)}, bf16[256,128]{1,0:T(8,128)(2,1)S(1)}, u32[]{:S(2)}, u32[]{:S(2)}) collective-permute-start(bf16[256,128]{1,0:T(8,128)(2,1)S(1)} %collective-permute-done.25.refs_6_), channel_id=1, source_target_pairs={{0,1},{1,0},{2,3},{3,2},{4,5},{5,4},{6,7},{7,6},{8,9},{9,8},{10,11... | collective-permute-start | bytes 196616 | tf_op jit(solution)/shard_map/ppermute | solution.py:17
  52.2 6.9 %collective-permute-start.24 = (bf16[256,128]{1,0:T(8,128)(2,1)S(1)}, bf16[256,128]{1,0:T(8,128)(2,1)S(1)}, u32[]{:S(2)}, u32[]{:S(2)}) collective-permute-start(bf16[256,128]{1,0:T(8,128)(2,1)S(1)} %collective-permute-done.23.refs_4_), channel_id=1, source_target_pairs={{0,1},{1,0},{2,3},{3,2},{4,5},{5,4},{6,7},{7,6},{8,9},{9,8},{10,11... | collective-permute-start | bytes 196616 | tf_op jit(solution)/shard_map/ppermute | solution.py:17
  54.1 5.0 %collective-permute-start.22 = (bf16[256,128]{1,0:T(8,128)(2,1)S(1)}, bf16[256,128]{1,0:T(8,128)(2,1)S(1)}, u32[]{:S(2)}, u32[]{:S(2)}) collective-permute-start(bf16[256,128]{1,0:T(8,128)(2,1)S(1)} %collective-permute-done.21.refs_2_), channel_id=1, source_target_pairs={{0,1},{1,0},{2,3},{3,2},{4,5},{5,4},{6,7},{7,6},{8,9},{9,8},{10,11... | collective-permute-start | bytes 196616 | tf_op jit(solution)/shard_map/ppermute | solution.py:17
  54.6 7.9 %collective-permute-start.33 = (f32[96,128]{1,0:T(8,128)S(1)}, f32[96,128]{1,0:T(8,128)S(1)}, u32[]{:S(2)}, u32[]{:S(2)}) collective-permute-start(f32[96,128]{1,0:T(8,128)S(1)} %fusion.2), channel_id=1, source_target_pairs={{0,6},{1,7},{2,4},{3,5},{4,2},{5,3},{6,0},{7,1},{8,14},{9,15},{10,... | collective-permute-start | bytes 147464 | tf_op jit(solution)/shard_map/ppermute | solution.py:17
  56.7 5.8 %collective-permute-start.32 = (f32[96,128]{1,0:T(8,128)S(1)}, f32[96,128]{1,0:T(8,128)S(1)}, u32[]{:S(2)}, u32[]{:S(2)}) collective-permute-start(f32[96,128]{1,0:T(8,128)S(1)} %fusion.2), channel_id=1, source_target_pairs={{0,4},{1,5},{2,6},{3,7},{4,0},{5,1},{6,2},{7,3},{8,12},{9,13},{10,... | collective-permute-start | bytes 147464 | tf_op jit(solution)/shard_map/ppermute | solution.py:17
  56.8 5.8 %collective-permute-start.31 = (f32[96,128]{1,0:T(8,128)S(1)}, f32[96,128]{1,0:T(8,128)S(1)}, u32[]{:S(2)}, u32[]{:S(2)}) collective-permute-start(f32[96,128]{1,0:T(8,128)S(1)} %fusion.2), channel_id=1, source_target_pairs={{0,2},{1,3},{2,0},{3,1},{4,6},{5,7},{6,4},{7,5},{8,10},{9,11},{10,... | collective-permute-start | bytes 147464 | tf_op jit(solution)/shard_map/ppermute | solution.py:17
  62.6 5.6 %collective-permute-start.39 = (f32[96,128]{1,0:T(8,128)S(1)}, f32[96,128]{1,0:T(8,128)S(1)}, u32[]{:S(2)}, u32[]{:S(2)}) collective-permute-start(f32[96,128]{1,0:T(8,128)S(1)} %add_add_fusion), channel_id=1, source_target_pairs={{0,24},{8,16},{16,8},{24,0},{1,25},{9,17},{17,9},{25,1},{2,26},{10... | collective-permute-start | bytes 147464 | tf_op jit(solution)/shard_map/ppermute | solution.py:17
  64.2 5.5 %collective-permute-start.38 = (f32[96,128]{1,0:T(8,128)S(1)}, f32[96,128]{1,0:T(8,128)S(1)}, u32[]{:S(2)}, u32[]{:S(2)}) collective-permute-start(f32[96,128]{1,0:T(8,128)S(1)} %add_add_fusion), channel_id=1, source_target_pairs={{0,16},{8,24},{16,0},{24,8},{1,17},{9,25},{17,1},{25,9},{2,18},{10... | collective-permute-start | bytes 147464 | tf_op jit(solution)/shard_map/ppermute | solution.py:17
  65.2 4.4 %collective-permute-start.37 = (f32[96,128]{1,0:T(8,128)S(1)}, f32[96,128]{1,0:T(8,128)S(1)}, u32[]{:S(2)}, u32[]{:S(2)}) collective-permute-start(f32[96,128]{1,0:T(8,128)S(1)} %add_add_fusion), channel_id=1, source_target_pairs={{0,8},{8,0},{16,24},{24,16},{1,9},{9,1},{17,25},{25,17},{2,10},{10... | collective-permute-start | bytes 147464 | tf_op jit(solution)/shard_map/ppermute | solution.py:17
  66.2 4.6 %collective-permute-start.34 = (bf16[256,128]{1,0:T(8,128)(2,1)S(1)}, bf16[256,128]{1,0:T(8,128)(2,1)S(1)}, u32[]{:S(2)}, u32[]{:S(2)}) collective-permute-start(bf16[256,128]{1,0:T(8,128)(2,1)S(1)} %get-tuple-element.40), channel_id=1, source_target_pairs={{0,8},{8,0},{16,24},{24,16},{1,9},{9,1},{17,25},{25,17},{2,10},{10... | collective-permute-start | bytes 196616 | tf_op jit(solution)/shard_map/ppermute | solution.py:17
  67.2 4.3 %collective-permute-start.35 = (bf16[256,128]{1,0:T(8,128)(2,1)S(1)}, bf16[256,128]{1,0:T(8,128)(2,1)S(1)}, u32[]{:S(2)}, u32[]{:S(2)}) collective-permute-start(bf16[256,128]{1,0:T(8,128)(2,1)S(1)} %get-tuple-element.41), channel_id=1, source_target_pairs={{0,16},{8,24},{16,0},{24,8},{1,17},{9,25},{17,1},{25,9},{2,18},{10... | collective-permute-start | bytes 196616 | tf_op jit(solution)/shard_map/ppermute | solution.py:17
  68.2 5.2 %collective-permute-start.36 = (bf16[256,128]{1,0:T(8,128)(2,1)S(1)}, bf16[256,128]{1,0:T(8,128)(2,1)S(1)}, u32[]{:S(2)}, u32[]{:S(2)}) collective-permute-start(bf16[256,128]{1,0:T(8,128)(2,1)S(1)} %get-tuple-element.42), channel_id=1, source_target_pairs={{0,24},{8,16},{16,8},{24,0},{1,25},{9,17},{17,9},{25,1},{2,26},{10... | collective-permute-start | bytes 196616 | tf_op jit(solution)/shard_map/ppermute | solution.py:17
  (16 other events, 166.8 us)

commit v3 on v2

--- a/solution.py
+++ b/solution.py
@@ -28,6 +28,17 @@
 def dot(left, right, contract=((1,), (0,))):
     return lax.dot_general(
         left, right, (contract, ((), ())), precision=HIGH, preferred_element_type=jnp.float32
+    )
+
+
+def dot_short(left, right):
+    left_high, right_high = left.astype(jnp.bfloat16), right.astype(jnp.bfloat16)
+    left_low = (left - left_high.astype(jnp.float32)).astype(jnp.bfloat16)
+    right_low = (right - right_high.astype(jnp.float32)).astype(jnp.bfloat16)
+    return jnp.dot(
+        jnp.concatenate([left_low, left_high, left_high], axis=1),
+        jnp.concatenate([right_high, right_low, right_high], axis=0),
+        preferred_element_type=jnp.float32,
     )
 
 
@@ -151,14 +162,34 @@
     )(dense, *pieces)
 
 
+def indices(width):
+    return (
+        lax.broadcasted_iota(jnp.int32, (width, width), 0),
+        lax.broadcasted_iota(jnp.int32, (width, width), 1),
+    )
+
+
+def column_sum(array):
+    return jnp.sum(array, axis=0, keepdims=True)
+
+
 def gram_kernel(pieces, index_ref, x_ref, z1_ref, z2_ref, near_ref, far_ref, whole):
     x, z1, z2 = x_ref[...], z1_ref[...], z2_ref[...]
+    width = x.shape[1]
+    row, col = indices(width)
+    eye = (row == col).astype(jnp.float32)
     contract = ((0,), (0,))
-    for at, (left, right) in enumerate(
-        ((x, x), (x, z1), (z1, z1), (x, z2), (z1, z2), (z2, z2))
-    ):
-        whole[at] = dot(left, right, contract)
-    rows = whole.shape[1] // pieces
+    n00 = dot(x, x, contract) - x.shape[0] * eye
+    n11 = dot(z1, z1, contract)
+    n22 = dot(z2, z2, contract)
+    diagonal = column_sum(eye * n11)
+    last = jnp.where((row == width - 2) & (col == 0), n11[width - 1 :, width - 1 :], 0.0)
+    whole[0] = jnp.where(row <= col, n00, n11)
+    whole[1] = jnp.where(row <= col, n22, jnp.where(row == width - 1, diagonal, last))
+    whole[2] = dot(x, z1, contract)
+    whole[3] = dot(x, z2, contract)
+    whole[4] = dot(z1, z2, contract)
+    rows = width // pieces
     for m in range(pieces):
         out = far_ref if m % 2 else near_ref
         start = pl.multiple_of((index_ref[0] ^ m) * rows, rows)
@@ -168,14 +199,14 @@
 
 def grams(index, x, z1, z2, pieces):
     width = x.shape[1]
-    cut = jax.ShapeDtypeStruct((pieces // 2, 6 * (width // pieces), width), jnp.float32)
+    cut = jax.ShapeDtypeStruct((pieces // 2, 5 * (width // pieces), width), jnp.float32)
     return pl.pallas_call(
         functools.partial(gram_kernel, pieces),
         out_shape=[cut, cut],
         in_specs=smem(1) + vmem(3),
         out_specs=vmem(2),
-        scratch_shapes=[pltpu.VMEM((6, width, width), jnp.float32)],
-        compiler_params=pltpu.CompilerParams(vmem_limit_bytes=VMEM_BYTES),
+        scratch_shapes=[pltpu.VMEM((5, width, width), jnp.float32)],
+        compiler_params=pltpu.CompilerParams(vmem_limit_bytes=4 * VMEM_BYTES),
         name="grams",
     )(index, x, z1, z2)
 
@@ -203,22 +234,25 @@
         start = pl.multiple_of((index_ref[0] ^ m) * rows, rows)
         for at in range(whole.shape[0]):
             whole[at, pl.ds(start, rows), :] = piece[m // 2, at * rows : (at + 1) * rows]
-    n00, n01, n11, n02, n12, n22 = (whole[at] for at in range(6))
+    row, col = indices(width)
+    eye = (row == col).astype(jnp.float32)
+    first, third, n01, n02, n12 = (whole[at] for at in range(5))
+    first_t = first.T
+    diagonal = jnp.where(
+        col[:1] == width - 1, third[width - 2 : width - 1, :1], third[width - 1 :, :]
+    )
+    excess = jnp.where(row <= col, first, first_t)
+    n00 = excess + verts_all * eye
+    n11 = jnp.where(row > col, first, jnp.where(row < col, first_t, diagonal))
+    n22 = jnp.where(row <= col, third, third.T)
     n10, n21 = n01.T, n12.T
-    eye = (
-        lax.broadcasted_iota(jnp.int32, (width, width), 0)
-        == lax.broadcasted_iota(jnp.int32, (width, width), 1)
-    ).astype(jnp.float32)
     scale = 1.0 / verts_all
 
     def inverse_norm(colsq):
-        row = lax.rsqrt(jnp.maximum(colsq, 0.0) * scale + 1e-06)
-        return jnp.sum(eye * row, axis=1, keepdims=True)
-
-    def column_sum(array):
-        return jnp.sum(array, axis=0, keepdims=True)
-
-    keep0 = eye - (n00 - n01) * scale
+        norm = lax.rsqrt(jnp.maximum(colsq, 0.0) * scale + 1e-06)
+        return jnp.sum(eye * norm, axis=1, keepdims=True)
+
+    keep0 = (n01 - excess) * scale
     colsq0 = column_sum(keep0 * (dot(n00, keep0) - 2.0 * n01) + eye * n11)
     q = inverse_norm(colsq0) * first_ref[width:]
     p = first_ref[:width] + dot(keep0, q)
@@ -229,7 +263,6 @@
             jnp.concatenate([n10, n11], axis=1),
             jnp.concatenate([n01, n02], axis=1),
             jnp.concatenate([n11, n12], axis=1),
-            jnp.concatenate([n11, n12], axis=1),
             jnp.concatenate([n21, n22], axis=1),
         ],
         axis=0,
@@ -240,14 +273,14 @@
     )
     both = dot(coeff, pair, ((0,), (0,)))
     s, t = both[:, :width], both[:, width:]
-    u = column_sum(coeff * applied[4 * width :])
+    u = column_sum(coeff * applied[3 * width :])
     keep1 = eye - (s - t) * scale
     colsq1 = column_sum(keep1 * (dot(s, keep1) - 2.0 * t)) + u
     v = inverse_norm(colsq1) * second_ref[width : 2 * width]
     e = second_ref[:width] + dot(keep1, v)
-    f = dot(q, second_ref[2 * width :])
-    mixed = dot(jnp.concatenate([p, q], axis=0), jnp.concatenate([e, v], axis=1))
-    a0 = mixed[:width, :width] + dot(keep0, f)
+    f = dot_short(q, second_ref[2 * width :])
+    mixed = dot_short(jnp.concatenate([p, q], axis=0), jnp.concatenate([e, v], axis=1))
+    a0 = mixed[:width, :width] + dot_short(keep0, f)
     a1 = -(mixed[width:, :width] + mixed[:width, width:] + f)
     a2 = mixed[width:, width:]
     none = jnp.zeros_like(a0)
@@ -261,7 +294,7 @@
         axis=0,
     )
     basis = jnp.concatenate([x_ref[...], z1_ref[...], z2_ref[...], z3_ref[...]], axis=1)
-    result = dot(basis, spread)
+    result = dot_short(basis, spread)
     block_ref[...] = result[:, :width]
     image_ref[...] = result[:, :width] - result[:, width:]
 
@@ -274,10 +307,20 @@
         out_shape=[out, out],
         in_specs=smem(1) + vmem(8),
         out_specs=vmem(2),
-        scratch_shapes=[pltpu.VMEM((6, width, width), jnp.float32)],
+        scratch_shapes=[pltpu.VMEM((5, width, width), jnp.float32)],
         compiler_params=pltpu.CompilerParams(vmem_limit_bytes=4 * VMEM_BYTES),
         name="finish",
     )(index, x, z1, z2, z3, first, second, near, far)
+
+
+def split(array):
+    high = lax.reduce_precision(array, 8, 7)
+    return jnp.concatenate([high, array - high]).astype(jnp.bfloat16)
+
+
+def join(coded):
+    high, low = jnp.split(coded.astype(jnp.float32), 2)
+    return high + low
 
 
 def local(
@@ -299,20 +342,27 @@
     slots = jnp.arange(tiles.shape[0], dtype=jnp.int32)
     cols = ((tile_col[0, 0] // halves) ^ col_at) * halves + tile_col[0, 0] % halves
     rows = ((tile_row[0, 0] // halves) ^ row_at) * halves + tile_row[0, 0] % halves
+    width = start_block.shape[1]
+    inner = [("col", m) for m in range(2, n_col, 2)]
+    outer = [("row", k) for k in range(1, n_row)]
+    place = 2 * row_at + col_at % 2
+    packed = (width // (2 * n_row)) % 8 == 0
+    if not packed:
+        inner, outer, place = outer, inner, col_at
+    cols, rows, index = lax.optimization_barrier((cols, rows, place.reshape(1)))
     dense = None
     if 2 * n_row * n_col * sub * sub <= DENSE_BYTES:
         dense = place_tiles(live_count[0], cols, rows, tiles, n_row * sub, n_col * sub)
     else:
         rows = jnp.where(slots < live_count[0, 0], rows, n_row * halves)
-    width = start_block.shape[1]
     scale = vertex_scale[:, None]
 
-    def gather(block, dense=None):
+    def spread(block):
         own = (scale * block).astype(jnp.bfloat16)
-        near = [own] + [swap(own, "col", m) for m in range(2, n_col, 2)]
-        if dense is not None:
-            own, dense = lax.optimization_barrier((own, dense))
-        return near, [swap(piece, "col", 1) for piece in [own] + near[1:]]
+        return [own] + [swap(own, "col", m) for m in range(2, n_col, 2)]
+
+    def twin(near):
+        return [swap(piece, "col", 1) for piece in near]
 
     def multiply(near, far):
         pieces = [piece for pair in zip(near, far) for piece in pair]
@@ -320,8 +370,13 @@
             return tile_products(cols, rows, tiles, pieces, n_row)
         return dense_products(dense, pieces, n_row)
 
-    def send(parts):
-        return [parts[0]] + [swap(parts[k], "row", k) for k in range(1, n_row)]
+    def send(parts, extra=None):
+        if extra is None:
+            return [parts[0]] + [swap(parts[k], "row", k) for k in range(1, n_row)], []
+        arrived = [
+            swap(jnp.concatenate([parts[k], extra[k]]), "row", k) for k in range(1, n_row)
+        ]
+        return [parts[0]] + [part[:sub] for part in arrived], [part[sub:] for part in arrived]
 
     def collect(parts):
         summed = parts[0]
@@ -329,34 +384,36 @@
             summed = summed + part.astype(jnp.float32)
         return scale * summed
 
-    inner = [("col", m) for m in range(2, n_col, 2)]
-    outer = [("row", k) for k in range(1, n_row)]
-    place = 2 * row_at + col_at % 2
-    if (width // (2 * n_row)) % 8 != 0:
-        inner, outer, place = outer, inner, col_at
-    index = place.reshape(1)
-
     def cut_grams(x, z1, z2):
         near, far = grams(index, x, z1, z2, 2 * (len(outer) + 1))
         near = near + swap(far, "col", 1)
-        return near[0], [swap(near[q + 1], *hop) for q, hop in enumerate(outer)]
+        return [near[q] for q in range(len(outer) + 1)]
 
     def add(mine, arrived):
         for piece in arrived:
             mine = mine + piece
         return mine
 
-    z1 = collect(send(multiply(*gather(start_block, dense))))
-    z2 = collect(send(multiply(*gather(z1))))
-    near, far = gather(z2)
-    mine, arrived = cut_grams(start_block, z1, z2)
-    mine = add(mine, arrived)
-    arrived = [swap(mine, *hop) for hop in inner]
-    parts, arrived = lax.optimization_barrier((multiply(near, far), arrived))
-    whole = add(mine, arrived)
-    gram_near = jnp.stack([whole] + [swap(whole, *hop) for hop in outer])
+    near = spread(start_block)
+    if dense is not None:
+        near[0], dense = lax.optimization_barrier((near[0], dense))
+    z1 = collect(send(multiply(near, twin(near)))[0])
+    near = spread(z1)
+    z2 = collect(send(multiply(near, twin(near)))[0])
+    gram = cut_grams(start_block, z1, z2)
+    near = spread(z2)
+    gram = add(gram[0], [swap(gram[q + 1], *hop) for q, hop in enumerate(outer)])
+    gram = add(gram, [swap(gram, *hop) for hop in inner])
+    parts = multiply(near, twin(near))
+    if packed:
+        parts, arrived = send(parts, [split(gram)] * n_row)
+        arrived = [join(piece) for piece in arrived]
+    else:
+        parts, _ = send(parts)
+        arrived = [swap(gram, *hop) for hop in outer]
+    z3 = collect(parts)
+    gram_near = jnp.stack([gram] + arrived)
     gram_far = swap(gram_near, "col", 1)
-    z3 = collect(send(parts))
     return tuple(
         finish(
             index,

time: 78.6 us -> 75.4 us (0.959)
  starting transfers between devices: 39.5 us -> 35.6 us
  waiting for transfers between devices: 20.8 us -> 23.9 us
  local copies, waits for them, and re-layouts: 3.81 us -> 1.62 us
    ppermute x41 -> x38, starting transfers between devices: 39.5 us -> 35.6 us  [swap(): return lax.ppermute(array, axis, [(k, k ^ mask) for k in range(size)])]
    ppermute x41 -> x38, waiting for transfers between devices: 20.8 us -> 23.9 us  [swap(): return lax.ppermute(array, axis, [(k, k ^ mask) for k in range(size)])]
    unnamed x14 -> x10, local copies, waits for them, and re-layouts: 3.8 us -> 1.61 us
  transfers between devices with their start and end apart: 41 -> 38, of which waited for: 20 -> 23; matrix products, arithmetic and copies ran while one was open for 1% -> 1% of each run, Pallas kernels for 3% -> 4%
where the time goes in v3:
time: 75.4 us; the launch traced here: 75.3 us
  starting transfers between devices  35.6 us (47%)
  waiting for transfers between devices  23.9 us (32%)
  Pallas kernels  10.6 us (14%)
  other arithmetic  2.13 us (3%)
  local copies, waits for them, and re-layouts  1.62 us (2%)
  between operations  1.53 us (2%)
    ppermute x38, starting transfers between devices, swap(): return lax.ppermute(array, axis, [(k, k ^ mask) for k in range(size)])  35.6 us
    ppermute x38, waiting for transfers between devices, swap(): return lax.ppermute(array, axis, [(k, k ^ mask) for k in range(size)])  23.9 us
    pallas_call x1, Pallas kernels, finish(): pl.pallas_call(functools.partial(finish_kernel, pieces, verts_all), out_s...  4.25 us
    pallas_call x3, Pallas kernels, dense_products(): pl.pallas_call(functools.partial(dense_kernel, n_col, n_row), out_shape=[...  3.84 us
    unnamed x10, local copies, waits for them, and re-layouts  1.61 us
    pallas_call x1, Pallas kernels, place_tiles(): pl.pallas_call(place_kernel, out_shape=jax.ShapeDtypeStruct((height, widt...  1.59 us
  transfers between devices with their start and end apart: 38, of which 23 were waited for; matrix products, arithmetic and copies ran while one was open for 1% of the time, Pallas kernels for 4%

profile of v3, /device:TPU:0, one launch (start us, length us, event | category | flops | bytes accessed | tf_op | source)
XLA Modules:
  0.0 75.3 jit_solution(8883980924709818205)
XLA Ops:
  1.6 5.1 %collective-permute-start.5 = (bf16[256,128]{1,0:T(8,128)(2,1)S(1)}, bf16[256,128]{1,0:T(8,128)(2,1)S(1)}, u32[]{:S(2)}, u32[]{:S(2)}) collective-permute-start(bf16[256,128]{1,0:T(8,128)(2,1)S(1)} %multiply_convert_fusion.2.refs_0_), channel_id=1, source_target_pairs={{0,6},{1,7},{2,4},{3,5},{4,2},{5,3},{6,0},{7,1},{8,14},{9,15},{10,... | collective-permute-start | bytes 196616 | tf_op jit(solution)/shard_map/ppermute | solution.py:17
  8.8 1.6 %copy-done = bf16[1,1,64,128,128]{4,3,2,1,0:T(8,128)(2,1)S(1)} copy-done((bf16[1,1,64,128,128]{4,3,2,1,0:T(8,128)(2,1)S(1)}, bf16[1,1,64,128,128]{4,3,2,1,0:T(8,128)(2,1)}, u32[]{:S(2)}) %copy-start) | copy-done | bytes 2097176
  10.3 1.6 %place_tiles.1.dense_ref = bf16[1024,2048]{1,0:T(8,128)(2,1)S(1)} custom-call(s32[1]{0:T(128)} %bitcast.50.count_ref, s32[64]{0:T(128)S(1)} %get-tuple-element.22.cols_ref, s32[64]{0:T(128)S(1)} %get-tuple-element.23.rows_ref, bf16[64,128,128]{2,1,0:T(8,128)(2,1)S(1)} %bitcast.51), custom_call_target="tpu_custom_call" | custom-call | bytes 8388608 | tf_op jit(solution)/shard_map/place_tiles/pallas_call | solution.py:120
  14.0 1.3 %dense_products.3 = (f32[256,128]{1,0:T(8,128)S(1)}, bf16[256,128]{1,0:T(8,128)(2,1)S(1)}, bf16[256,128]{1,0:T(8,128)(2,1)S(1)}, bf16[256,128]{1,0:T(8,128)(2,1)S(1)}) custom-call(bf16[1024,2048]{1,0:T(8,128)(2,1)S(1)} %place_tiles.1.dense_ref, bf16[256,128]{1,0:T(8,128)(2,1)S(1)} %multiply_convert_fusion.2.refs_0_, ...), custom_call_target="tpu_custom_call" | custom-call | flops 536870912 | bytes 4194304 | tf_op jit(solution)/shard_map/dense_products/pallas_call | solution.py:148
  15.2 1.9 %collective-permute-start.7 = (bf16[256,128]{1,0:T(8,128)(2,1)S(1)}, bf16[256,128]{1,0:T(8,128)(2,1)S(1)}, u32[]{:S(2)}, u32[]{:S(2)}) collective-permute-start(bf16[256,128]{1,0:T(8,128)(2,1)S(1)} %get-tuple-element.27), channel_id=1, source_target_pairs={{0,8},{8,0},{16,24},{24,16},{1,9},{9,1},{17,25},{25,17},{2,10},{10... | collective-permute-start | bytes 196616 | tf_op jit(solution)/shard_map/ppermute | solution.py:17
  17.1 1.4 %collective-permute-start.8 = (bf16[256,128]{1,0:T(8,128)(2,1)S(1)}, bf16[256,128]{1,0:T(8,128)(2,1)S(1)}, u32[]{:S(2)}, u32[]{:S(2)}) collective-permute-start(bf16[256,128]{1,0:T(8,128)(2,1)S(1)} %get-tuple-element.28), channel_id=1, source_target_pairs={{0,16},{8,24},{16,0},{24,8},{1,17},{9,25},{17,1},{25,9},{2,18},{10... | collective-permute-start | bytes 196616 | tf_op jit(solution)/shard_map/ppermute | solution.py:17
  19.8 1.7 %collective-permute-done.8 = bf16[256,128]{1,0:T(8,128)(2,1)S(1)} collective-permute-done((bf16[256,128]{1,0:T(8,128)(2,1)S(1)}, bf16[256,128]{1,0:T(8,128)(2,1)S(1)}, u32[]{:S(2)}, u32[]{:S(2)}) %collective-permute-start.8) | collective-permute-done | bytes 65568 | tf_op jit(solution)/shard_map/ppermute | solution.py:17
  21.4 2.3 %collective-permute-done.9 = bf16[256,128]{1,0:T(8,128)(2,1)S(1)} collective-permute-done((bf16[256,128]{1,0:T(8,128)(2,1)S(1)}, bf16[256,128]{1,0:T(8,128)(2,1)S(1)}, u32[]{:S(2)}, u32[]{:S(2)}) %collective-permute-start.9) | collective-permute-done | bytes 65568 | tf_op jit(solution)/shard_map/ppermute | solution.py:17
  23.8 3.4 %collective-permute-start.15 = (bf16[256,128]{1,0:T(8,128)(2,1)S(1)}, bf16[256,128]{1,0:T(8,128)(2,1)S(1)}, u32[]{:S(2)}, u32[]{:S(2)}) collective-permute-start(bf16[256,128]{1,0:T(8,128)(2,1)S(1)} %get-tuple-element.44.refs_0_), channel_id=1, source_target_pairs={{0,6},{1,7},{2,4},{3,5},{4,2},{5,3},{6,0},{7,1},{8,14},{9,15},{10,... | collective-permute-start | bytes 196616 | tf_op jit(solution)/shard_map/ppermute | solution.py:17
  27.2 1.1 %collective-permute-start.11 = (bf16[256,128]{1,0:T(8,128)(2,1)S(1)}, bf16[256,128]{1,0:T(8,128)(2,1)S(1)}, u32[]{:S(2)}, u32[]{:S(2)}) collective-permute-start(bf16[256,128]{1,0:T(8,128)(2,1)S(1)} %get-tuple-element.44.refs_0_), channel_id=1, source_target_pairs={{0,2},{1,3},{2,0},{3,1},{4,6},{5,7},{6,4},{7,5},{8,10},{9,11},{10,... | collective-permute-start | bytes 196616 | tf_op jit(solution)/shard_map/ppermute | solution.py:17
  28.3 1.7 %collective-permute-done.15.refs_6_ = bf16[256,128]{1,0:T(8,128)(2,1)S(1)} collective-permute-done((bf16[256,128]{1,0:T(8,128)(2,1)S(1)}, bf16[256,128]{1,0:T(8,128)(2,1)S(1)}, u32[]{:S(2)}, u32[]{:S(2)}) %collective-permute-start.15) | collective-permute-done | bytes 65568 | tf_op jit(solution)/shard_map/ppermute | solution.py:17
  29.9 2.4 %collective-permute-done.13.refs_4_ = bf16[256,128]{1,0:T(8,128)(2,1)S(1)} collective-permute-done((bf16[256,128]{1,0:T(8,128)(2,1)S(1)}, bf16[256,128]{1,0:T(8,128)(2,1)S(1)}, u32[]{:S(2)}, u32[]{:S(2)}) %collective-permute-start.13) | collective-permute-done | bytes 65568 | tf_op jit(solution)/shard_map/ppermute | solution.py:17
  33.8 1.3 %dense_products.4 = (f32[256,128]{1,0:T(8,128)S(1)}, bf16[256,128]{1,0:T(8,128)(2,1)S(1)}, bf16[256,128]{1,0:T(8,128)(2,1)S(1)}, bf16[256,128]{1,0:T(8,128)(2,1)S(1)}) custom-call(bf16[1024,2048]{1,0:T(8,128)(2,1)S(1)} %place_tiles.1.dense_ref, bf16[256,128]{1,0:T(8,128)(2,1)S(1)} %get-tuple-element.44.refs_0_, ...), custom_call_target="tpu_custom_call" | custom-call | flops 536870912 | bytes 4194304 | tf_op jit(solution)/shard_map/dense_products/pallas_call | solution.py:148
  35.7 1.1 %collective-permute-start.18 = (bf16[256,128]{1,0:T(8,128)(2,1)S(1)}, bf16[256,128]{1,0:T(8,128)(2,1)S(1)}, u32[]{:S(2)}, u32[]{:S(2)}) collective-permute-start(bf16[256,128]{1,0:T(8,128)(2,1)S(1)} %get-tuple-element.32), channel_id=1, source_target_pairs={{0,16},{8,24},{16,0},{24,8},{1,17},{9,25},{17,1},{25,9},{2,18},{10... | collective-permute-start | bytes 196616 | tf_op jit(solution)/shard_map/ppermute | solution.py:17
  36.8 1.8 %collective-permute-start.19 = (bf16[256,128]{1,0:T(8,128)(2,1)S(1)}, bf16[256,128]{1,0:T(8,128)(2,1)S(1)}, u32[]{:S(2)}, u32[]{:S(2)}) collective-permute-start(bf16[256,128]{1,0:T(8,128)(2,1)S(1)} %get-tuple-element.33), channel_id=1, source_target_pairs={{0,24},{8,16},{16,8},{24,0},{1,25},{9,17},{17,9},{25,1},{2,26},{10... | collective-permute-start | bytes 196616 | tf_op jit(solution)/shard_map/ppermute | solution.py:17
  39.9 2.0 %collective-permute-done.19 = bf16[256,128]{1,0:T(8,128)(2,1)S(1)} collective-permute-done((bf16[256,128]{1,0:T(8,128)(2,1)S(1)}, bf16[256,128]{1,0:T(8,128)(2,1)S(1)}, u32[]{:S(2)}, u32[]{:S(2)}) %collective-permute-start.19) | collective-permute-done | bytes 65568 | tf_op jit(solution)/shard_map/ppermute | solution.py:17
  43.0 2.0 %collective-permute-start.25 = (bf16[256,128]{1,0:T(8,128)(2,1)S(1)}, bf16[256,128]{1,0:T(8,128)(2,1)S(1)}, u32[]{:S(2)}, u32[]{:S(2)}) collective-permute-start(bf16[256,128]{1,0:T(8,128)(2,1)S(1)} %get-tuple-element.42.refs_0_), channel_id=1, source_target_pairs={{0,6},{1,7},{2,4},{3,5},{4,2},{5,3},{6,0},{7,1},{8,14},{9,15},{10,... | collective-permute-start | bytes 196616 | tf_op jit(solution)/shard_map/ppermute | solution.py:17
  45.1 2.4 %collective-permute-start.21 = (bf16[256,128]{1,0:T(8,128)(2,1)S(1)}, bf16[256,128]{1,0:T(8,128)(2,1)S(1)}, u32[]{:S(2)}, u32[]{:S(2)}) collective-permute-start(bf16[256,128]{1,0:T(8,128)(2,1)S(1)} %get-tuple-element.42.refs_0_), channel_id=1, source_target_pairs={{0,2},{1,3},{2,0},{3,1},{4,6},{5,7},{6,4},{7,5},{8,10},{9,11},{10,... | collective-permute-start | bytes 196616 | tf_op jit(solution)/shard_map/ppermute | solution.py:17
  48.5 1.5 %collective-permute-start.30 = (f32[80,128]{1,0:T(8,128)S(1)}, f32[80,128]{1,0:T(8,128)S(1)}, u32[]{:S(2)}, u32[]{:S(2)}) collective-permute-start(f32[80,128]{1,0:T(8,128)S(1)} %get-tuple-element.47), channel_id=1, source_target_pairs={{0,24},{8,16},{16,8},{24,0},{1,25},{9,17},{17,9},{25,1},{2,26},{10... | collective-permute-start | bytes 122888 | tf_op jit(solution)/shard_map/ppermute | solution.py:17
  50.0 1.1 %collective-permute-start.29 = (f32[80,128]{1,0:T(8,128)S(1)}, f32[80,128]{1,0:T(8,128)S(1)}, u32[]{:S(2)}, u32[]{:S(2)}) collective-permute-start(f32[80,128]{1,0:T(8,128)S(1)} %get-tuple-element.48), channel_id=1, source_target_pairs={{0,16},{8,24},{16,0},{24,8},{1,17},{9,25},{17,1},{25,9},{2,18},{10... | collective-permute-start | bytes 122888 | tf_op jit(solution)/shard_map/ppermute | solution.py:17
  51.1 1.1 %collective-permute-done.23.refs_4_ = bf16[256,128]{1,0:T(8,128)(2,1)S(1)} collective-permute-done((bf16[256,128]{1,0:T(8,128)(2,1)S(1)}, bf16[256,128]{1,0:T(8,128)(2,1)S(1)}, u32[]{:S(2)}, u32[]{:S(2)}) %collective-permute-start.23) | collective-permute-done | bytes 65568 | tf_op jit(solution)/shard_map/ppermute | solution.py:17
  54.0 2.3 %collective-permute-start.33 = (f32[80,128]{1,0:T(8,128)S(1)}, f32[80,128]{1,0:T(8,128)S(1)}, u32[]{:S(2)}, u32[]{:S(2)}) collective-permute-start(f32[80,128]{1,0:T(8,128)S(1)} %fusion.6), channel_id=1, source_target_pairs={{0,6},{1,7},{2,4},{3,5},{4,2},{5,3},{6,0},{7,1},{8,14},{9,15},{10,... | collective-permute-start | bytes 122888 | tf_op jit(solution)/shard_map/ppermute | solution.py:17
  56.7 1.8 %collective-permute-start.31 = (f32[80,128]{1,0:T(8,128)S(1)}, f32[80,128]{1,0:T(8,128)S(1)}, u32[]{:S(2)}, u32[]{:S(2)}) collective-permute-start(f32[80,128]{1,0:T(8,128)S(1)} %fusion.6), channel_id=1, source_target_pairs={{0,2},{1,3},{2,0},{3,1},{4,6},{5,7},{6,4},{7,5},{8,10},{9,11},{10,... | collective-permute-start | bytes 122888 | tf_op jit(solution)/shard_map/ppermute | solution.py:17
  58.5 1.3 %dense_products.5 = (f32[256,128]{1,0:T(8,128)S(1)}, bf16[256,128]{1,0:T(8,128)(2,1)S(1)}, bf16[256,128]{1,0:T(8,128)(2,1)S(1)}, bf16[256,128]{1,0:T(8,128)(2,1)S(1)}) custom-call(bf16[1024,2048]{1,0:T(8,128)(2,1)S(1)} %place_tiles.1.dense_ref, bf16[256,128]{1,0:T(8,128)(2,1)S(1)} %get-tuple-element.42.refs_0_, ...), custom_call_target="tpu_custom_call" | custom-call | flops 536870912 | bytes 4194304 | tf_op jit(solution)/shard_map/dense_products/pallas_call | solution.py:148
  59.9 1.4 %collective-permute-done.32 = f32[80,128]{1,0:T(8,128)S(1)} collective-permute-done((f32[80,128]{1,0:T(8,128)S(1)}, f32[80,128]{1,0:T(8,128)S(1)}, u32[]{:S(2)}, u32[]{:S(2)}) %collective-permute-start.32) | collective-permute-done | bytes 40992 | tf_op jit(solution)/shard_map/ppermute | solution.py:17
  61.3 1.4 %collective-permute-start.34 = (bf16[416,128]{1,0:T(8,128)(2,1)S(1)}, bf16[416,128]{1,0:T(8,128)(2,1)S(1)}, u32[]{:S(2)}, u32[]{:S(2)}) collective-permute-start(bf16[416,128]{1,0:T(8,128)(2,1)S(1)} %get-tuple-element.49), channel_id=1, source_target_pairs={{0,8},{8,0},{16,24},{24,16},{1,9},{9,1},{17,25},{25,17},{2,10},{10... | collective-permute-start | bytes 319496 | tf_op jit(solution)/shard_map/ppermute | solution.py:17
  62.7 1.3 %collective-permute-start.35 = (bf16[416,128]{1,0:T(8,128)(2,1)S(1)}, bf16[416,128]{1,0:T(8,128)(2,1)S(1)}, u32[]{:S(2)}, u32[]{:S(2)}) collective-permute-start(bf16[416,128]{1,0:T(8,128)(2,1)S(1)} %get-tuple-element.50), channel_id=1, source_target_pairs={{0,16},{8,24},{16,0},{24,8},{1,17},{9,25},{17,1},{25,9},{2,18},{10... | collective-permute-start | bytes 319496 | tf_op jit(solution)/shard_map/ppermute | solution.py:17
  64.9 2.2 %collective-permute-done.34 = bf16[416,128]{1,0:T(8,128)(2,1)S(1)} collective-permute-done((bf16[416,128]{1,0:T(8,128)(2,1)S(1)}, bf16[416,128]{1,0:T(8,128)(2,1)S(1)}, u32[]{:S(2)}, u32[]{:S(2)}) %collective-permute-start.34) | collective-permute-done | bytes 106528 | tf_op jit(solution)/shard_map/ppermute | solution.py:17
  67.1 1.2 %collective-permute-done.35 = bf16[416,128]{1,0:T(8,128)(2,1)S(1)} collective-permute-done((bf16[416,128]{1,0:T(8,128)(2,1)S(1)}, bf16[416,128]{1,0:T(8,128)(2,1)S(1)}, u32[]{:S(2)}, u32[]{:S(2)}) %collective-permute-start.35) | collective-permute-done | bytes 106528 | tf_op jit(solution)/shard_map/ppermute | solution.py:17
  68.3 1.3 %collective-permute-done.36 = bf16[416,128]{1,0:T(8,128)(2,1)S(1)} collective-permute-done((bf16[416,128]{1,0:T(8,128)(2,1)S(1)}, bf16[416,128]{1,0:T(8,128)(2,1)S(1)}, u32[]{:S(2)}, u32[]{:S(2)}) %collective-permute-start.36) | collective-permute-done | bytes 106528 | tf_op jit(solution)/shard_map/ppermute | solution.py:17
  69.8 1.3 %collective-permute-done.37.far_ref = f32[4,80,128]{2,1,0:T(8,128)S(1)} collective-permute-done((f32[4,80,128]{2,1,0:T(8,128)S(1)}, f32[4,80,128]{2,1,0:T(8,128)S(1)}, u32[]{:S(2)}, u32[]{:S(2)}) %collective-permute-start.37) | collective-permute-done | bytes 163872 | tf_op jit(solution)/shard_map/ppermute | solution.py:17
  71.1 4.2 %finish.1 = (f32[256,128]{1,0:T(8,128)}, f32[256,128]{1,0:T(8,128)}) custom-call(s32[1]{0:T(128)} %bitcast.2.index_ref, f32[256,128]{1,0:T(8,128)S(1)} %copy-done.1, f32[256,128]{1,0:T(8,128)S(1)} %get-tuple-element.45.z1_ref, f32[256,128]{1,0:T(8,128)S(1)} %get-tuple-element.43.z2_ref, f32[256,128]{1,0:T(8,128)S(1)} %add_multiply_fusion.z3_ref, ...), custom_call_target="tpu_custom_call" | custom-call | tf_op jit(solution)/shard_map/finish/pallas_call | solution.py:305
  (78 shorter events, 14.6 us)
Async XLA Ops:
  1.6 10.4 %collective-permute-start.5 = (bf16[256,128]{1,0:T(8,128)(2,1)S(1)}, bf16[256,128]{1,0:T(8,128)(2,1)S(1)}, u32[]{:S(2)}, u32[]{:S(2)}) collective-permute-start(bf16[256,128]{1,0:T(8,128)(2,1)S(1)} %multiply_convert_fusion.2.refs_0_), channel_id=1, source_target_pairs={{0,6},{1,7},{2,4},{3,5},{4,2},{5,3},{6,0},{7,1},{8,14},{9,15},{10,... | collective-permute-start | bytes 196616 | tf_op jit(solution)/shard_map/ppermute | solution.py:17
  6.8 5.8 %collective-permute-start.3 = (bf16[256,128]{1,0:T(8,128)(2,1)S(1)}, bf16[256,128]{1,0:T(8,128)(2,1)S(1)}, u32[]{:S(2)}, u32[]{:S(2)}) collective-permute-start(bf16[256,128]{1,0:T(8,128)(2,1)S(1)} %multiply_convert_fusion.2.refs_0_), channel_id=1, source_target_pairs={{0,4},{1,5},{2,6},{3,7},{4,0},{5,1},{6,2},{7,3},{8,12},{9,13},{10,... | collective-permute-start | bytes 196616 | tf_op jit(solution)/shard_map/ppermute | solution.py:17
  6.8 5.9 %collective-permute-start.1 = (bf16[256,128]{1,0:T(8,128)(2,1)S(1)}, bf16[256,128]{1,0:T(8,128)(2,1)S(1)}, u32[]{:S(2)}, u32[]{:S(2)}) collective-permute-start(bf16[256,128]{1,0:T(8,128)(2,1)S(1)} %multiply_convert_fusion.2.refs_0_), channel_id=1, source_target_pairs={{0,2},{1,3},{2,0},{3,1},{4,6},{5,7},{6,4},{7,5},{8,10},{9,11},{10,... | collective-permute-start | bytes 196616 | tf_op jit(solution)/shard_map/ppermute | solution.py:17
  15.2 4.5 %collective-permute-start.7 = (bf16[256,128]{1,0:T(8,128)(2,1)S(1)}, bf16[256,128]{1,0:T(8,128)(2,1)S(1)}, u32[]{:S(2)}, u32[]{:S(2)}) collective-permute-start(bf16[256,128]{1,0:T(8,128)(2,1)S(1)} %get-tuple-element.27), channel_id=1, source_target_pairs={{0,8},{8,0},{16,24},{24,16},{1,9},{9,1},{17,25},{25,17},{2,10},{10... | collective-permute-start | bytes 196616 | tf_op jit(solution)/shard_map/ppermute | solution.py:17
  17.1 4.3 %collective-permute-start.8 = (bf16[256,128]{1,0:T(8,128)(2,1)S(1)}, bf16[256,128]{1,0:T(8,128)(2,1)S(1)}, u32[]{:S(2)}, u32[]{:S(2)}) collective-permute-start(bf16[256,128]{1,0:T(8,128)(2,1)S(1)} %get-tuple-element.28), channel_id=1, source_target_pairs={{0,16},{8,24},{16,0},{24,8},{1,17},{9,25},{17,1},{25,9},{2,18},{10... | collective-permute-start | bytes 196616 | tf_op jit(solution)/shard_map/ppermute | solution.py:17
  18.5 5.2 %collective-permute-start.9 = (bf16[256,128]{1,0:T(8,128)(2,1)S(1)}, bf16[256,128]{1,0:T(8,128)(2,1)S(1)}, u32[]{:S(2)}, u32[]{:S(2)}) collective-permute-start(bf16[256,128]{1,0:T(8,128)(2,1)S(1)} %get-tuple-element.29), channel_id=1, source_target_pairs={{0,24},{8,16},{16,8},{24,0},{1,25},{9,17},{17,9},{25,1},{2,26},{10... | collective-permute-start | bytes 196616 | tf_op jit(solution)/shard_map/ppermute | solution.py:17
  23.8 6.1 %collective-permute-start.15 = (bf16[256,128]{1,0:T(8,128)(2,1)S(1)}, bf16[256,128]{1,0:T(8,128)(2,1)S(1)}, u32[]{:S(2)}, u32[]{:S(2)}) collective-permute-start(bf16[256,128]{1,0:T(8,128)(2,1)S(1)} %get-tuple-element.44.refs_0_), channel_id=1, source_target_pairs={{0,6},{1,7},{2,4},{3,5},{4,2},{5,3},{6,0},{7,1},{8,14},{9,15},{10,... | collective-permute-start | bytes 196616 | tf_op jit(solution)/shard_map/ppermute | solution.py:17
  27.2 5.2 %collective-permute-start.13 = (bf16[256,128]{1,0:T(8,128)(2,1)S(1)}, bf16[256,128]{1,0:T(8,128)(2,1)S(1)}, u32[]{:S(2)}, u32[]{:S(2)}) collective-permute-start(bf16[256,128]{1,0:T(8,128)(2,1)S(1)} %get-tuple-element.44.refs_0_), channel_id=1, source_target_pairs={{0,4},{1,5},{2,6},{3,7},{4,0},{5,1},{6,2},{7,3},{8,12},{9,13},{10,... | collective-permute-start | bytes 196616 | tf_op jit(solution)/shard_map/ppermute | solution.py:17
  27.2 5.2 %collective-permute-start.11 = (bf16[256,128]{1,0:T(8,128)(2,1)S(1)}, bf16[256,128]{1,0:T(8,128)(2,1)S(1)}, u32[]{:S(2)}, u32[]{:S(2)}) collective-permute-start(bf16[256,128]{1,0:T(8,128)(2,1)S(1)} %get-tuple-element.44.refs_0_), channel_id=1, source_target_pairs={{0,2},{1,3},{2,0},{3,1},{4,6},{5,7},{6,4},{7,5},{8,10},{9,11},{10,... | collective-permute-start | bytes 196616 | tf_op jit(solution)/shard_map/ppermute | solution.py:17
  28.3 4.6 %collective-permute-start.10 = (bf16[256,128]{1,0:T(8,128)(2,1)S(1)}, bf16[256,128]{1,0:T(8,128)(2,1)S(1)}, u32[]{:S(2)}, u32[]{:S(2)}) collective-permute-start(bf16[256,128]{1,0:T(8,128)(2,1)S(1)} %get-tuple-element.44.refs_0_), channel_id=1, source_target_pairs={{0,1},{1,0},{2,3},{3,2},{4,5},{5,4},{6,7},{7,6},{8,9},{9,8},{10,11... | collective-permute-start | bytes 196616 | tf_op jit(solution)/shard_map/ppermute | solution.py:17
  29.9 2.9 %collective-permute-start.16 = (bf16[256,128]{1,0:T(8,128)(2,1)S(1)}, bf16[256,128]{1,0:T(8,128)(2,1)S(1)}, u32[]{:S(2)}, u32[]{:S(2)}) collective-permute-start(bf16[256,128]{1,0:T(8,128)(2,1)S(1)} %collective-permute-done.15.refs_6_), channel_id=1, source_target_pairs={{0,1},{1,0},{2,3},{3,2},{4,5},{5,4},{6,7},{7,6},{8,9},{9,8},{10,11... | collective-permute-start | bytes 196616 | tf_op jit(solution)/shard_map/ppermute | solution.py:17
  35.0 4.4 %collective-permute-start.17 = (bf16[256,128]{1,0:T(8,128)(2,1)S(1)}, bf16[256,128]{1,0:T(8,128)(2,1)S(1)}, u32[]{:S(2)}, u32[]{:S(2)}) collective-permute-start(bf16[256,128]{1,0:T(8,128)(2,1)S(1)} %get-tuple-element.31), channel_id=1, source_target_pairs={{0,8},{8,0},{16,24},{24,16},{1,9},{9,1},{17,25},{25,17},{2,10},{10... | collective-permute-start | bytes 196616 | tf_op jit(solution)/shard_map/ppermute | solution.py:17
  35.7 4.3 %collective-permute-start.18 = (bf16[256,128]{1,0:T(8,128)(2,1)S(1)}, bf16[256,128]{1,0:T(8,128)(2,1)S(1)}, u32[]{:S(2)}, u32[]{:S(2)}) collective-permute-start(bf16[256,128]{1,0:T(8,128)(2,1)S(1)} %get-tuple-element.32), channel_id=1, source_target_pairs={{0,16},{8,24},{16,0},{24,8},{1,17},{9,25},{17,1},{25,9},{2,18},{10... | collective-permute-start | bytes 196616 | tf_op jit(solution)/shard_map/ppermute | solution.py:17
  36.8 5.2 %collective-permute-start.19 = (bf16[256,128]{1,0:T(8,128)(2,1)S(1)}, bf16[256,128]{1,0:T(8,128)(2,1)S(1)}, u32[]{:S(2)}, u32[]{:S(2)}) collective-permute-start(bf16[256,128]{1,0:T(8,128)(2,1)S(1)} %get-tuple-element.33), channel_id=1, source_target_pairs={{0,24},{8,16},{16,8},{24,0},{1,25},{9,17},{17,9},{25,1},{2,26},{10... | collective-permute-start | bytes 196616 | tf_op jit(solution)/shard_map/ppermute | solution.py:17
  43.0 4.5 %collective-permute-start.27 = (f32[4,80,128]{2,1,0:T(8,128)S(1)}, f32[4,80,128]{2,1,0:T(8,128)S(1)}, u32[]{:S(2)}, u32[]{:S(2)}) collective-permute-start(f32[4,80,128]{2,1,0:T(8,128)S(1)} %get-tuple-element.37), channel_id=1, source_target_pairs={{0,1},{1,0},{2,3},{3,2},{4,5},{5,4},{6,7},{7,6},{8,9},{9,8},{10,11... | collective-permute-start | bytes 491528 | tf_op jit(solution)/shard_map/ppermute | solution.py:17
  43.0 6.9 %collective-permute-start.25 = (bf16[256,128]{1,0:T(8,128)(2,1)S(1)}, bf16[256,128]{1,0:T(8,128)(2,1)S(1)}, u32[]{:S(2)}, u32[]{:S(2)}) collective-permute-start(bf16[256,128]{1,0:T(8,128)(2,1)S(1)} %get-tuple-element.42.refs_0_), channel_id=1, source_target_pairs={{0,6},{1,7},{2,4},{3,5},{4,2},{5,3},{6,0},{7,1},{8,14},{9,15},{10,... | collective-permute-start | bytes 196616 | tf_op jit(solution)/shard_map/ppermute | solution.py:17
  45.1 7.1 %collective-permute-start.23 = (bf16[256,128]{1,0:T(8,128)(2,1)S(1)}, bf16[256,128]{1,0:T(8,128)(2,1)S(1)}, u32[]{:S(2)}, u32[]{:S(2)}) collective-permute-start(bf16[256,128]{1,0:T(8,128)(2,1)S(1)} %get-tuple-element.42.refs_0_), channel_id=1, source_target_pairs={{0,4},{1,5},{2,6},{3,7},{4,0},{5,1},{6,2},{7,3},{8,12},{9,13},{10,... | collective-permute-start | bytes 196616 | tf_op jit(solution)/shard_map/ppermute | solution.py:17
  45.1 7.1 %collective-permute-start.21 = (bf16[256,128]{1,0:T(8,128)(2,1)S(1)}, bf16[256,128]{1,0:T(8,128)(2,1)S(1)}, u32[]{:S(2)}, u32[]{:S(2)}) collective-permute-start(bf16[256,128]{1,0:T(8,128)(2,1)S(1)} %get-tuple-element.42.refs_0_), channel_id=1, source_target_pairs={{0,2},{1,3},{2,0},{3,1},{4,6},{5,7},{6,4},{7,5},{8,10},{9,11},{10,... | collective-permute-start | bytes 196616 | tf_op jit(solution)/shard_map/ppermute | solution.py:17
  47.5 5.1 %collective-permute-start.28 = (f32[80,128]{1,0:T(8,128)S(1)}, f32[80,128]{1,0:T(8,128)S(1)}, u32[]{:S(2)}, u32[]{:S(2)}) collective-permute-start(f32[80,128]{1,0:T(8,128)S(1)} %get-tuple-element.46), channel_id=1, source_target_pairs={{0,8},{8,0},{16,24},{24,16},{1,9},{9,1},{17,25},{25,17},{2,10},{10... | collective-permute-start | bytes 122888 | tf_op jit(solution)/shard_map/ppermute | solution.py:17
  48.5 4.9 %collective-permute-start.30 = (f32[80,128]{1,0:T(8,128)S(1)}, f32[80,128]{1,0:T(8,128)S(1)}, u32[]{:S(2)}, u32[]{:S(2)}) collective-permute-start(f32[80,128]{1,0:T(8,128)S(1)} %get-tuple-element.47), channel_id=1, source_target_pairs={{0,24},{8,16},{16,8},{24,0},{1,25},{9,17},{17,9},{25,1},{2,26},{10... | collective-permute-start | bytes 122888 | tf_op jit(solution)/shard_map/ppermute | solution.py:17
  50.0 4.0 %collective-permute-start.29 = (f32[80,128]{1,0:T(8,128)S(1)}, f32[80,128]{1,0:T(8,128)S(1)}, u32[]{:S(2)}, u32[]{:S(2)}) collective-permute-start(f32[80,128]{1,0:T(8,128)S(1)} %get-tuple-element.48), channel_id=1, source_target_pairs={{0,16},{8,24},{16,0},{24,8},{1,17},{9,25},{17,1},{25,9},{2,18},{10... | collective-permute-start | bytes 122888 | tf_op jit(solution)/shard_map/ppermute | solution.py:17
  52.2 4.1 %collective-permute-start.20 = (bf16[256,128]{1,0:T(8,128)(2,1)S(1)}, bf16[256,128]{1,0:T(8,128)(2,1)S(1)}, u32[]{:S(2)}, u32[]{:S(2)}) collective-permute-start(bf16[256,128]{1,0:T(8,128)(2,1)S(1)} %get-tuple-element.42.refs_0_), channel_id=1, source_target_pairs={{0,1},{1,0},{2,3},{3,2},{4,5},{5,4},{6,7},{7,6},{8,9},{9,8},{10,11... | collective-permute-start | bytes 196616 | tf_op jit(solution)/shard_map/ppermute | solution.py:17
  52.2 4.5 %collective-permute-start.26 = (bf16[256,128]{1,0:T(8,128)(2,1)S(1)}, bf16[256,128]{1,0:T(8,128)(2,1)S(1)}, u32[]{:S(2)}, u32[]{:S(2)}) collective-permute-start(bf16[256,128]{1,0:T(8,128)(2,1)S(1)} %collective-permute-done.25.refs_6_), channel_id=1, source_target_pairs={{0,1},{1,0},{2,3},{3,2},{4,5},{5,4},{6,7},{7,6},{8,9},{9,8},{10,11... | collective-permute-start | bytes 196616 | tf_op jit(solution)/shard_map/ppermute | solution.py:17
  52.7 5.8 %collective-permute-start.24 = (bf16[256,128]{1,0:T(8,128)(2,1)S(1)}, bf16[256,128]{1,0:T(8,128)(2,1)S(1)}, u32[]{:S(2)}, u32[]{:S(2)}) collective-permute-start(bf16[256,128]{1,0:T(8,128)(2,1)S(1)} %collective-permute-done.23.refs_4_), channel_id=1, source_target_pairs={{0,1},{1,0},{2,3},{3,2},{4,5},{5,4},{6,7},{7,6},{8,9},{9,8},{10,11... | collective-permute-start | bytes 196616 | tf_op jit(solution)/shard_map/ppermute | solution.py:17
  53.4 5.1 %collective-permute-start.22 = (bf16[256,128]{1,0:T(8,128)(2,1)S(1)}, bf16[256,128]{1,0:T(8,128)(2,1)S(1)}, u32[]{:S(2)}, u32[]{:S(2)}) collective-permute-start(bf16[256,128]{1,0:T(8,128)(2,1)S(1)} %collective-permute-done.21.refs_2_), channel_id=1, source_target_pairs={{0,1},{1,0},{2,3},{3,2},{4,5},{5,4},{6,7},{7,6},{8,9},{9,8},{10,11... | collective-permute-start | bytes 196616 | tf_op jit(solution)/shard_map/ppermute | solution.py:17
  54.0 5.9 %collective-permute-start.33 = (f32[80,128]{1,0:T(8,128)S(1)}, f32[80,128]{1,0:T(8,128)S(1)}, u32[]{:S(2)}, u32[]{:S(2)}) collective-permute-start(f32[80,128]{1,0:T(8,128)S(1)} %fusion.6), channel_id=1, source_target_pairs={{0,6},{1,7},{2,4},{3,5},{4,2},{5,3},{6,0},{7,1},{8,14},{9,15},{10,... | collective-permute-start | bytes 122888 | tf_op jit(solution)/shard_map/ppermute | solution.py:17
  56.3 5.0 %collective-permute-start.32 = (f32[80,128]{1,0:T(8,128)S(1)}, f32[80,128]{1,0:T(8,128)S(1)}, u32[]{:S(2)}, u32[]{:S(2)}) collective-permute-start(f32[80,128]{1,0:T(8,128)S(1)} %fusion.6), channel_id=1, source_target_pairs={{0,4},{1,5},{2,6},{3,7},{4,0},{5,1},{6,2},{7,3},{8,12},{9,13},{10,... | collective-permute-start | bytes 122888 | tf_op jit(solution)/shard_map/ppermute | solution.py:17
  56.7 4.6 %collective-permute-start.31 = (f32[80,128]{1,0:T(8,128)S(1)}, f32[80,128]{1,0:T(8,128)S(1)}, u32[]{:S(2)}, u32[]{:S(2)}) collective-permute-start(f32[80,128]{1,0:T(8,128)S(1)} %fusion.6), channel_id=1, source_target_pairs={{0,2},{1,3},{2,0},{3,1},{4,6},{5,7},{6,4},{7,5},{8,10},{9,11},{10,... | collective-permute-start | bytes 122888 | tf_op jit(solution)/shard_map/ppermute | solution.py:17
  61.3 5.7 %collective-permute-start.34 = (bf16[416,128]{1,0:T(8,128)(2,1)S(1)}, bf16[416,128]{1,0:T(8,128)(2,1)S(1)}, u32[]{:S(2)}, u32[]{:S(2)}) collective-permute-start(bf16[416,128]{1,0:T(8,128)(2,1)S(1)} %get-tuple-element.49), channel_id=1, source_target_pairs={{0,8},{8,0},{16,24},{24,16},{1,9},{9,1},{17,25},{25,17},{2,10},{10... | collective-permute-start | bytes 319496 | tf_op jit(solution)/shard_map/ppermute | solution.py:17
  62.7 5.6 %collective-permute-start.35 = (bf16[416,128]{1,0:T(8,128)(2,1)S(1)}, bf16[416,128]{1,0:T(8,128)(2,1)S(1)}, u32[]{:S(2)}, u32[]{:S(2)}) collective-permute-start(bf16[416,128]{1,0:T(8,128)(2,1)S(1)} %get-tuple-element.50), channel_id=1, source_target_pairs={{0,16},{8,24},{16,0},{24,8},{1,17},{9,25},{17,1},{25,9},{2,18},{10... | collective-permute-start | bytes 319496 | tf_op jit(solution)/shard_map/ppermute | solution.py:17
  64.0 5.6 %collective-permute-start.36 = (bf16[416,128]{1,0:T(8,128)(2,1)S(1)}, bf16[416,128]{1,0:T(8,128)(2,1)S(1)}, u32[]{:S(2)}, u32[]{:S(2)}) collective-permute-start(bf16[416,128]{1,0:T(8,128)(2,1)S(1)} %get-tuple-element.51), channel_id=1, source_target_pairs={{0,24},{8,16},{16,8},{24,0},{1,25},{9,17},{17,9},{25,1},{2,26},{10... | collective-permute-start | bytes 319496 | tf_op jit(solution)/shard_map/ppermute | solution.py:17
  69.6 1.5 %collective-permute-start.37 = (f32[4,80,128]{2,1,0:T(8,128)S(1)}, f32[4,80,128]{2,1,0:T(8,128)S(1)}, u32[]{:S(2)}, u32[]{:S(2)}) collective-permute-start(f32[4,80,128]{2,1,0:T(8,128)S(1)} %pad_maximum_fusion.6.near_ref), channel_id=1, source_target_pairs={{0,1},{1,0},{2,3},{3,2},{4,5},{5,4},{6,7},{7,6},{8,9},{9,8},{10,11... | collective-permute-start | bytes 491528 | tf_op jit(solution)/shard_map/ppermute | solution.py:17
  (11 other events, 111.1 us)

commit v4 on v3

--- a/solution.py
+++ b/solution.py
@@ -130,36 +130,68 @@
     )(count, cols, rows, tiles)
 
 
-def dense_kernel(n_col, n_row, dense_ref, *refs):
-    pieces, outs, panel = refs[:n_col], refs[n_col : n_col + n_row], refs[-1]
+def near_kernel(dense_ref, *refs):
+    pieces, total_ref, panel = refs[:-2], refs[-2], refs[-1]
     sub = pieces[0].shape[0]
     for m, piece in enumerate(pieces):
         panel[m * sub : (m + 1) * sub] = piece[...]
-    for k in range(n_row):
-        part = jnp.dot(
-            dense_ref[k * sub : (k + 1) * sub], panel[...], preferred_element_type=jnp.float32
+    for at in range(0, total_ref.shape[0], sub):
+        total_ref[at : at + sub] = jnp.dot(
+            dense_ref[at : at + sub, : len(pieces) * sub],
+            panel[...],
+            preferred_element_type=jnp.float32,
         )
-        outs[k][...] = part.astype(outs[k].dtype)
-
-
-def dense_products(dense, pieces, n_row):
-    n_col = len(pieces)
-    sub, width = pieces[0].shape
-    return pl.pallas_call(
-        functools.partial(dense_kernel, n_col, n_row),
+
+
+def far_kernel(dense_ref, total_ref, *refs):
+    count = (len(refs) - 1) - total_ref.shape[0] // refs[0].shape[0]
+    pieces, outs, panel = refs[:count], refs[count:-1], refs[-1]
+    sub = pieces[0].shape[0]
+    for m, piece in enumerate(pieces):
+        panel[m * sub : (m + 1) * sub] = piece[...]
+    for k, out in enumerate(outs):
+        part = total_ref[k * sub : (k + 1) * sub] + jnp.dot(
+            dense_ref[k * sub : (k + 1) * sub, count * sub :],
+            panel[...],
+            preferred_element_type=jnp.float32,
+        )
+        out[...] = part.astype(out.dtype)
+
+
+def near_products(dense, near):
+    sub, width = near[0].shape
+    return pl.pallas_call(
+        near_kernel,
+        out_shape=jax.ShapeDtypeStruct((dense.shape[0], width), jnp.float32),
+        in_specs=vmem(1 + len(near)),
+        out_specs=vmem(1)[0],
+        scratch_shapes=[pltpu.VMEM((len(near) * sub, width), jnp.bfloat16)],
+        compiler_params=pltpu.CompilerParams(vmem_limit_bytes=VMEM_BYTES),
+        cost_estimate=pl.CostEstimate(
+            flops=dense.size * width, bytes_accessed=dense.size, transcendentals=0
+        ),
+        name="near_products",
+    )(dense, *near)
+
+
+def far_products(dense, total, far):
+    sub, width = far[0].shape
+    n_row = dense.shape[0] // sub
+    return pl.pallas_call(
+        far_kernel,
         out_shape=[
             jax.ShapeDtypeStruct((sub, width), jnp.float32 if k == 0 else jnp.bfloat16)
             for k in range(n_row)
         ],
-        in_specs=vmem(1 + n_col),
+        in_specs=vmem(2 + len(far)),
         out_specs=vmem(n_row),
-        scratch_shapes=[pltpu.VMEM((n_col * sub, width), jnp.bfloat16)],
+        scratch_shapes=[pltpu.VMEM((len(far) * sub, width), jnp.bfloat16)],
         compiler_params=pltpu.CompilerParams(vmem_limit_bytes=VMEM_BYTES),
         cost_estimate=pl.CostEstimate(
-            flops=2 * dense.size * width, bytes_accessed=2 * dense.size, transcendentals=0
+            flops=dense.size * width, bytes_accessed=dense.size, transcendentals=0
         ),
-        name="dense_products",
-    )(dense, *pieces)
+        name="far_products",
+    )(dense, total, *far)
 
 
 def indices(width):
@@ -173,22 +205,44 @@
     return jnp.sum(array, axis=0, keepdims=True)
 
 
-def gram_kernel(pieces, index_ref, x_ref, z1_ref, z2_ref, near_ref, far_ref, whole):
-    x, z1, z2 = x_ref[...], z1_ref[...], z2_ref[...]
+def early_kernel(x_ref, z1_ref, out_ref):
+    x, z1 = x_ref[...], z1_ref[...]
+    row, col = indices(x.shape[1])
+    eye = (row == col).astype(jnp.float32)
+    out_ref[0] = dot(x, x, ((0,), (0,))) - x.shape[0] * eye
+    out_ref[1] = dot(x, z1, ((0,), (0,)))
+    out_ref[2] = dot(z1, z1, ((0,), (0,)))
+
+
+def early_grams(x, z1):
     width = x.shape[1]
+    return pl.pallas_call(
+        early_kernel,
+        out_shape=jax.ShapeDtypeStruct((3, width, width), jnp.float32),
+        in_specs=vmem(2),
+        out_specs=vmem(1)[0],
+        compiler_params=pltpu.CompilerParams(vmem_limit_bytes=4 * VMEM_BYTES),
+        name="early_grams",
+    )(x, z1)
+
+
+def gram_kernel(pieces, index_ref, early_ref, x_ref, z1_ref, z2_ref, near_ref, far_ref, whole):
+    z2 = z2_ref[...]
+    width = z2.shape[1]
     row, col = indices(width)
     eye = (row == col).astype(jnp.float32)
-    contract = ((0,), (0,))
-    n00 = dot(x, x, contract) - x.shape[0] * eye
-    n11 = dot(z1, z1, contract)
-    n22 = dot(z2, z2, contract)
+    n00, n11 = early_ref[0], early_ref[2]
+    side = jnp.concatenate([x_ref[...], z1_ref[...], z2], axis=1)
+    late = dot_short(side.T, z2)
     diagonal = column_sum(eye * n11)
     last = jnp.where((row == width - 2) & (col == 0), n11[width - 1 :, width - 1 :], 0.0)
     whole[0] = jnp.where(row <= col, n00, n11)
-    whole[1] = jnp.where(row <= col, n22, jnp.where(row == width - 1, diagonal, last))
-    whole[2] = dot(x, z1, contract)
-    whole[3] = dot(x, z2, contract)
-    whole[4] = dot(z1, z2, contract)
+    whole[1] = jnp.where(
+        row <= col, late[2 * width :], jnp.where(row == width - 1, diagonal, last)
+    )
+    whole[2] = early_ref[1]
+    whole[3] = late[:width]
+    whole[4] = late[width : 2 * width]
     rows = width // pieces
     for m in range(pieces):
         out = far_ref if m % 2 else near_ref
@@ -197,18 +251,18 @@
             out[m // 2, at * rows : (at + 1) * rows] = whole[at, pl.ds(start, rows), :]
 
 
-def grams(index, x, z1, z2, pieces):
+def grams(index, early, x, z1, z2, pieces):
     width = x.shape[1]
     cut = jax.ShapeDtypeStruct((pieces // 2, 5 * (width // pieces), width), jnp.float32)
     return pl.pallas_call(
         functools.partial(gram_kernel, pieces),
         out_shape=[cut, cut],
-        in_specs=smem(1) + vmem(3),
+        in_specs=smem(1) + vmem(4),
         out_specs=vmem(2),
         scratch_shapes=[pltpu.VMEM((5, width, width), jnp.float32)],
         compiler_params=pltpu.CompilerParams(vmem_limit_bytes=4 * VMEM_BYTES),
         name="grams",
-    )(index, x, z1, z2)
+    )(index, early, x, z1, z2)
 
 
 def finish_kernel(
@@ -242,7 +296,6 @@
         col[:1] == width - 1, third[width - 2 : width - 1, :1], third[width - 1 :, :]
     )
     excess = jnp.where(row <= col, first, first_t)
-    n00 = excess + verts_all * eye
     n11 = jnp.where(row > col, first, jnp.where(row < col, first_t, diagonal))
     n22 = jnp.where(row <= col, third, third.T)
     n10, n21 = n01.T, n12.T
@@ -253,13 +306,16 @@
         return jnp.sum(eye * norm, axis=1, keepdims=True)
 
     keep0 = (n01 - excess) * scale
-    colsq0 = column_sum(keep0 * (dot(n00, keep0) - 2.0 * n01) + eye * n11)
+    colsq0 = column_sum(
+        keep0 * (verts_all * keep0 + dot_short(excess, keep0) - 2.0 * n01) + eye * n11
+    )
     q = inverse_norm(colsq0) * first_ref[width:]
-    p = first_ref[:width] + dot(keep0, q)
+    p = first_ref[:width] + dot_short(keep0, q)
+    square = dot(p, p, ((0,), (0,)))
     coeff = jnp.concatenate([p, -q], axis=0)
     blocks = jnp.concatenate(
         [
-            jnp.concatenate([n00, n01], axis=1),
+            jnp.concatenate([excess, n01], axis=1),
             jnp.concatenate([n10, n11], axis=1),
             jnp.concatenate([n01, n02], axis=1),
             jnp.concatenate([n11, n12], axis=1),
@@ -267,17 +323,18 @@
         ],
         axis=0,
     )
-    applied = dot(blocks, coeff)
+    applied = dot_short(blocks, coeff)
     pair = jnp.concatenate(
         [applied[: 2 * width], applied[2 * width : 4 * width]], axis=1
     )
-    both = dot(coeff, pair, ((0,), (0,)))
-    s, t = both[:, :width], both[:, width:]
-    u = column_sum(coeff * applied[3 * width :])
-    keep1 = eye - (s - t) * scale
-    colsq1 = column_sum(keep1 * (dot(s, keep1) - 2.0 * t)) + u
-    v = inverse_norm(colsq1) * second_ref[width : 2 * width]
-    e = second_ref[:width] + dot(keep1, v)
+    both = dot_short(coeff.T, pair)
+    s, t = both[:, :width] * scale, both[:, width:] * scale
+    u = column_sum(coeff * applied[3 * width :]) * scale
+    keep1 = (eye - square) - (s - t)
+    s = s + square
+    colsq1 = column_sum(keep1 * (dot_short(s, keep1) - 2.0 * t)) + u
+    v = inverse_norm(colsq1 * verts_all) * second_ref[width : 2 * width]
+    e = second_ref[:width] + dot_short(keep1, v)
     f = dot_short(q, second_ref[2 * width :])
     mixed = dot_short(jnp.concatenate([p, q], axis=0), jnp.concatenate([e, v], axis=1))
     a0 = mixed[:width, :width] + dot_short(keep0, f)
@@ -340,7 +397,9 @@
     tiles = adj_tiles[0, 0]
     halves = sub // tiles.shape[1]
     slots = jnp.arange(tiles.shape[0], dtype=jnp.int32)
-    cols = ((tile_col[0, 0] // halves) ^ col_at) * halves + tile_col[0, 0] % halves
+    distance = (tile_col[0, 0] // halves) ^ col_at
+    place = (distance % 2 + 1) * (n_col // 2) - 1 - distance // 2
+    cols = place * halves + tile_col[0, 0] % halves
     rows = ((tile_row[0, 0] // halves) ^ row_at) * halves + tile_row[0, 0] % halves
     width = start_block.shape[1]
     inner = [("col", m) for m in range(2, n_col, 2)]
@@ -365,10 +424,9 @@
         return [swap(piece, "col", 1) for piece in near]
 
     def multiply(near, far):
-        pieces = [piece for pair in zip(near, far) for piece in pair]
         if dense is None:
-            return tile_products(cols, rows, tiles, pieces, n_row)
-        return dense_products(dense, pieces, n_row)
+            return tile_products(cols, rows, tiles, near[::-1] + far[::-1], n_row)
+        return far_products(dense, near_products(dense, near[::-1]), far[::-1])
 
     def send(parts, extra=None):
         if extra is None:
@@ -384,8 +442,8 @@
             summed = summed + part.astype(jnp.float32)
         return scale * summed
 
-    def cut_grams(x, z1, z2):
-        near, far = grams(index, x, z1, z2, 2 * (len(outer) + 1))
+    def cut_grams(early, x, z1, z2):
+        near, far = grams(index, early, x, z1, z2, 2 * (len(outer) + 1))
         near = near + swap(far, "col", 1)
         return [near[q] for q in range(len(outer) + 1)]
 
@@ -399,8 +457,9 @@
         near[0], dense = lax.optimization_barrier((near[0], dense))
     z1 = collect(send(multiply(near, twin(near)))[0])
     near = spread(z1)
+    early = early_grams(start_block, z1)
     z2 = collect(send(multiply(near, twin(near)))[0])
-    gram = cut_grams(start_block, z1, z2)
+    gram = cut_grams(early, start_block, z1, z2)
     near = spread(z2)
     gram = add(gram[0], [swap(gram[q + 1], *hop) for q, hop in enumerate(outer)])
     gram = add(gram, [swap(gram, *hop) for hop in inner])

time: 75.4 us -> 71.9 us (0.954)
  waiting for transfers between devices: 23.9 us -> 20.6 us
    ppermute x38, waiting for transfers between devices: 23.9 us -> 20.6 us  [swap(): return lax.ppermute(array, axis, [(k, k ^ mask) for k in range(size)])]
    pallas_call x3 -> x7, Pallas kernels: 3.84 us -> 4.87 us  [the longest x3 2.19 us: far_products(): pl.pallas_call(far_kernel, out_shape=[jax.ShapeDtypeStruct((sub, width),...]
    pallas_call x1, Pallas kernels: 4.25 us -> 3.33 us  [finish(): pl.pallas_call(functools.partial(finish_kernel, pieces, verts_all), out_s...]
  transfers between devices with their start and end apart: 38 -> 38, of which waited for: 23 -> 18; matrix products, arithmetic and copies ran while one was open for 1% -> 1% of each run, Pallas kernels for 4% -> 7%
where the time goes in v4:
time: 71.9 us; the launch traced here: 71.6 us
  starting transfers between devices  35.7 us (50%)
  waiting for transfers between devices  20.6 us (29%)
  Pallas kernels  9.93 us (14%)
  other arithmetic  2.14 us (3%)
  between operations  1.63 us (2%)
  local copies, waits for them, and re-layouts  1.62 us (2%)
    ppermute x38, starting transfers between devices, swap(): return lax.ppermute(array, axis, [(k, k ^ mask) for k in range(size)])  35.7 us
    ppermute x38, waiting for transfers between devices, swap(): return lax.ppermute(array, axis, [(k, k ^ mask) for k in range(size)])  20.6 us
    pallas_call x1, Pallas kernels, finish(): pl.pallas_call(functools.partial(finish_kernel, pieces, verts_all), out_s...  3.33 us
    pallas_call x3, Pallas kernels, far_products(): pl.pallas_call(far_kernel, out_shape=[jax.ShapeDtypeStruct((sub, width),...  2.19 us
    pallas_call x3, Pallas kernels, near_products(): pl.pallas_call(near_kernel, out_shape=jax.ShapeDtypeStruct((dense.shape[0...  2.16 us
    unnamed x10, local copies, waits for them, and re-layouts  1.61 us
  transfers between devices with their start and end apart: 38, of which 18 were waited for; matrix products, arithmetic and copies ran while one was open for 1% of the time, Pallas kernels for 7%

profile of v4, /device:TPU:0, one launch (start us, length us, event | category | flops | bytes accessed | tf_op | source)
XLA Modules:
  0.0 71.6 jit_solution(1714552923506790235)
XLA Ops:
  0.6 1.0 %multiply_convert_fusion.2.refs_3_ = bf16[256,128]{1,0:T(8,128)(2,1)S(1)} fusion(f32[256,128]{1,0:T(8,128)} %x_ref.5, f32[256]{0:T(256)} %param.9), kind=kLoop, calls=%fused_computation.12 | loop fusion | flops 65536 | bytes 197632 | tf_op jit(solution)/shard_map/convert_element_type | solution.py:420
  1.6 5.1 %collective-permute-start = (bf16[256,128]{1,0:T(8,128)(2,1)S(1)}, bf16[256,128]{1,0:T(8,128)(2,1)S(1)}, u32[]{:S(2)}, u32[]{:S(2)}) collective-permute-start(bf16[256,128]{1,0:T(8,128)(2,1)S(1)} %multiply_convert_fusion.2.refs_3_), channel_id=1, source_target_pairs={{0,6},{1,7},{2,4},{3,5},{4,2},{5,3},{6,0},{7,1},{8,14},{9,15},{10,... | collective-permute-start | bytes 196616 | tf_op jit(solution)/shard_map/ppermute | solution.py:17
  8.8 1.6 %copy-done.1 = bf16[1,1,64,128,128]{4,3,2,1,0:T(8,128)(2,1)S(1)} copy-done((bf16[1,1,64,128,128]{4,3,2,1,0:T(8,128)(2,1)S(1)}, bf16[1,1,64,128,128]{4,3,2,1,0:T(8,128)(2,1)}, u32[]{:S(2)}) %copy-start.1) | copy-done | bytes 2097176
  10.3 1.3 %place_tiles.1.dense_ref = bf16[1024,2048]{1,0:T(8,128)(2,1)S(1)} custom-call(s32[1]{0:T(128)} %bitcast.50.count_ref, s32[64]{0:T(128)S(1)} %get-tuple-element.22.cols_ref, s32[64]{0:T(128)S(1)} %get-tuple-element.23.rows_ref, bf16[64,128,128]{2,1,0:T(8,128)(2,1)S(1)} %bitcast.51), custom_call_target="tpu_custom_call" | custom-call | bytes 8388608 | tf_op jit(solution)/shard_map/place_tiles/pallas_call | solution.py:120
  13.8 0.7 %far_products.3 = (f32[256,128]{1,0:T(8,128)S(1)}, bf16[256,128]{1,0:T(8,128)(2,1)S(1)}, bf16[256,128]{1,0:T(8,128)(2,1)S(1)}, bf16[256,128]{1,0:T(8,128)(2,1)S(1)}) custom-call(bf16[1024,2048]{1,0:T(8,128)(2,1)S(1)} %place_tiles.1.dense_ref, f32[1024,128]{1,0:T(8,128)S(1)} %near_products.3.total_ref, bf16[256,128]{1,0:T(8,128)(2,1)S(1)} %collective-permute-done.3.refs_0_, ...), custom_call_target="tpu_custom_call" | custom-call | flops 268435456 | bytes 2097152 | tf_op jit(solution)/shard_map/far_products/pallas_call | solution.py:180
  14.5 2.5 %collective-permute-start.9 = (bf16[256,128]{1,0:T(8,128)(2,1)S(1)}, bf16[256,128]{1,0:T(8,128)(2,1)S(1)}, u32[]{:S(2)}, u32[]{:S(2)}) collective-permute-start(bf16[256,128]{1,0:T(8,128)(2,1)S(1)} %get-tuple-element.29), channel_id=1, source_target_pairs={{0,24},{8,16},{16,8},{24,0},{1,25},{9,17},{17,9},{25,1},{2,26},{10... | collective-permute-start | bytes 196616 | tf_op jit(solution)/shard_map/ppermute | solution.py:17
  18.1 1.8 %collective-permute-done.9 = bf16[256,128]{1,0:T(8,128)(2,1)S(1)} collective-permute-done((bf16[256,128]{1,0:T(8,128)(2,1)S(1)}, bf16[256,128]{1,0:T(8,128)(2,1)S(1)}, u32[]{:S(2)}, u32[]{:S(2)}) %collective-permute-start.9) | collective-permute-done | bytes 65568 | tf_op jit(solution)/shard_map/ppermute | solution.py:17
  19.8 1.5 %collective-permute-done.8 = bf16[256,128]{1,0:T(8,128)(2,1)S(1)} collective-permute-done((bf16[256,128]{1,0:T(8,128)(2,1)S(1)}, bf16[256,128]{1,0:T(8,128)(2,1)S(1)}, u32[]{:S(2)}, u32[]{:S(2)}) %collective-permute-start.8) | collective-permute-done | bytes 65568 | tf_op jit(solution)/shard_map/ppermute | solution.py:17
  22.1 3.6 %collective-permute-start.10 = (bf16[256,128]{1,0:T(8,128)(2,1)S(1)}, bf16[256,128]{1,0:T(8,128)(2,1)S(1)}, u32[]{:S(2)}, u32[]{:S(2)}) collective-permute-start(bf16[256,128]{1,0:T(8,128)(2,1)S(1)} %get-tuple-element.44.refs_3_), channel_id=1, source_target_pairs={{0,6},{1,7},{2,4},{3,5},{4,2},{5,3},{6,0},{7,1},{8,14},{9,15},{10,... | collective-permute-start | bytes 196616 | tf_op jit(solution)/shard_map/ppermute | solution.py:17
  25.7 0.9 %collective-permute-start.12 = (bf16[256,128]{1,0:T(8,128)(2,1)S(1)}, bf16[256,128]{1,0:T(8,128)(2,1)S(1)}, u32[]{:S(2)}, u32[]{:S(2)}) collective-permute-start(bf16[256,128]{1,0:T(8,128)(2,1)S(1)} %get-tuple-element.44.refs_3_), channel_id=1, source_target_pairs={{0,2},{1,3},{2,0},{3,1},{4,6},{5,7},{6,4},{7,5},{8,10},{9,11},{10,... | collective-permute-start | bytes 196616 | tf_op jit(solution)/shard_map/ppermute | solution.py:17
  26.6 1.9 %collective-permute-done.10.refs_0_ = bf16[256,128]{1,0:T(8,128)(2,1)S(1)} collective-permute-done((bf16[256,128]{1,0:T(8,128)(2,1)S(1)}, bf16[256,128]{1,0:T(8,128)(2,1)S(1)}, u32[]{:S(2)}, u32[]{:S(2)}) %collective-permute-start.10) | collective-permute-done | bytes 65568 | tf_op jit(solution)/shard_map/ppermute | solution.py:17
  28.4 2.7 %collective-permute-done.11.refs_1_ = bf16[256,128]{1,0:T(8,128)(2,1)S(1)} collective-permute-done((bf16[256,128]{1,0:T(8,128)(2,1)S(1)}, bf16[256,128]{1,0:T(8,128)(2,1)S(1)}, u32[]{:S(2)}, u32[]{:S(2)}) %collective-permute-start.11) | collective-permute-done | bytes 65568 | tf_op jit(solution)/shard_map/ppermute | solution.py:17
  32.5 0.7 %far_products.4 = (f32[256,128]{1,0:T(8,128)S(1)}, bf16[256,128]{1,0:T(8,128)(2,1)S(1)}, bf16[256,128]{1,0:T(8,128)(2,1)S(1)}, bf16[256,128]{1,0:T(8,128)(2,1)S(1)}) custom-call(bf16[1024,2048]{1,0:T(8,128)(2,1)S(1)} %place_tiles.1.dense_ref, f32[1024,128]{1,0:T(8,128)S(1)} %near_products.4.total_ref, bf16[256,128]{1,0:T(8,128)(2,1)S(1)} %collective-permute-done.13.refs_0_, ...), custom_call_target="tpu_custom_call" | custom-call | flops 268435456 | bytes 2097152 | tf_op jit(solution)/shard_map/far_products/pallas_call | solution.py:180
  33.3 1.8 %collective-permute-start.19 = (bf16[256,128]{1,0:T(8,128)(2,1)S(1)}, bf16[256,128]{1,0:T(8,128)(2,1)S(1)}, u32[]{:S(2)}, u32[]{:S(2)}) collective-permute-start(bf16[256,128]{1,0:T(8,128)(2,1)S(1)} %get-tuple-element.33), channel_id=1, source_target_pairs={{0,24},{8,16},{16,8},{24,0},{1,25},{9,17},{17,9},{25,1},{2,26},{10... | collective-permute-start | bytes 196616 | tf_op jit(solution)/shard_map/ppermute | solution.py:17
  35.1 1.3 %collective-permute-start.18 = (bf16[256,128]{1,0:T(8,128)(2,1)S(1)}, bf16[256,128]{1,0:T(8,128)(2,1)S(1)}, u32[]{:S(2)}, u32[]{:S(2)}) collective-permute-start(bf16[256,128]{1,0:T(8,128)(2,1)S(1)} %get-tuple-element.32), channel_id=1, source_target_pairs={{0,16},{8,24},{16,0},{24,8},{1,17},{9,25},{17,1},{25,9},{2,18},{10... | collective-permute-start | bytes 196616 | tf_op jit(solution)/shard_map/ppermute | solution.py:17
  37.4 1.3 %collective-permute-done.19 = bf16[256,128]{1,0:T(8,128)(2,1)S(1)} collective-permute-done((bf16[256,128]{1,0:T(8,128)(2,1)S(1)}, bf16[256,128]{1,0:T(8,128)(2,1)S(1)}, u32[]{:S(2)}, u32[]{:S(2)}) %collective-permute-start.19) | collective-permute-done | bytes 65568 | tf_op jit(solution)/shard_map/ppermute | solution.py:17
  38.7 1.3 %collective-permute-done.18 = bf16[256,128]{1,0:T(8,128)(2,1)S(1)} collective-permute-done((bf16[256,128]{1,0:T(8,128)(2,1)S(1)}, bf16[256,128]{1,0:T(8,128)(2,1)S(1)}, u32[]{:S(2)}, u32[]{:S(2)}) %collective-permute-start.18) | collective-permute-done | bytes 65568 | tf_op jit(solution)/shard_map/ppermute | solution.py:17
  41.2 2.2 %collective-permute-start.20 = (bf16[256,128]{1,0:T(8,128)(2,1)S(1)}, bf16[256,128]{1,0:T(8,128)(2,1)S(1)}, u32[]{:S(2)}, u32[]{:S(2)}) collective-permute-start(bf16[256,128]{1,0:T(8,128)(2,1)S(1)} %get-tuple-element.42.refs_3_), channel_id=1, source_target_pairs={{0,6},{1,7},{2,4},{3,5},{4,2},{5,3},{6,0},{7,1},{8,14},{9,15},{10,... | collective-permute-start | bytes 196616 | tf_op jit(solution)/shard_map/ppermute | solution.py:17
  43.4 2.2 %collective-permute-start.22 = (bf16[256,128]{1,0:T(8,128)(2,1)S(1)}, bf16[256,128]{1,0:T(8,128)(2,1)S(1)}, u32[]{:S(2)}, u32[]{:S(2)}) collective-permute-start(bf16[256,128]{1,0:T(8,128)(2,1)S(1)} %get-tuple-element.42.refs_3_), channel_id=1, source_target_pairs={{0,2},{1,3},{2,0},{3,1},{4,6},{5,7},{6,4},{7,5},{8,10},{9,11},{10,... | collective-permute-start | bytes 196616 | tf_op jit(solution)/shard_map/ppermute | solution.py:17
  45.7 1.9 %collective-permute-start.30 = (f32[80,128]{1,0:T(8,128)S(1)}, f32[80,128]{1,0:T(8,128)S(1)}, u32[]{:S(2)}, u32[]{:S(2)}) collective-permute-start(f32[80,128]{1,0:T(8,128)S(1)} %get-tuple-element.47), channel_id=1, source_target_pairs={{0,24},{8,16},{16,8},{24,0},{1,25},{9,17},{17,9},{25,1},{2,26},{10... | collective-permute-start | bytes 122888 | tf_op jit(solution)/shard_map/ppermute | solution.py:17
  48.1 1.1 %collective-permute-start.28 = (f32[80,128]{1,0:T(8,128)S(1)}, f32[80,128]{1,0:T(8,128)S(1)}, u32[]{:S(2)}, u32[]{:S(2)}) collective-permute-start(f32[80,128]{1,0:T(8,128)S(1)} %get-tuple-element.46), channel_id=1, source_target_pairs={{0,8},{8,0},{16,24},{24,16},{1,9},{9,1},{17,25},{25,17},{2,10},{10... | collective-permute-start | bytes 122888 | tf_op jit(solution)/shard_map/ppermute | solution.py:17
  49.2 1.1 %collective-permute-done.21.refs_1_ = bf16[256,128]{1,0:T(8,128)(2,1)S(1)} collective-permute-done((bf16[256,128]{1,0:T(8,128)(2,1)S(1)}, bf16[256,128]{1,0:T(8,128)(2,1)S(1)}, u32[]{:S(2)}, u32[]{:S(2)}) %collective-permute-start.21) | collective-permute-done | bytes 65568 | tf_op jit(solution)/shard_map/ppermute | solution.py:17
  50.9 0.7 %collective-permute-done.29 = f32[80,128]{1,0:T(8,128)S(1)} collective-permute-done((f32[80,128]{1,0:T(8,128)S(1)}, f32[80,128]{1,0:T(8,128)S(1)}, u32[]{:S(2)}, u32[]{:S(2)}) %collective-permute-start.29) | collective-permute-done | bytes 40992 | tf_op jit(solution)/shard_map/ppermute | solution.py:17
  52.2 2.2 %collective-permute-start.33 = (f32[80,128]{1,0:T(8,128)S(1)}, f32[80,128]{1,0:T(8,128)S(1)}, u32[]{:S(2)}, u32[]{:S(2)}) collective-permute-start(f32[80,128]{1,0:T(8,128)S(1)} %fusion.6), channel_id=1, source_target_pairs={{0,6},{1,7},{2,4},{3,5},{4,2},{5,3},{6,0},{7,1},{8,14},{9,15},{10,... | collective-permute-start | bytes 122888 | tf_op jit(solution)/shard_map/ppermute | solution.py:17
  54.3 2.3 %collective-permute-start.31 = (f32[80,128]{1,0:T(8,128)S(1)}, f32[80,128]{1,0:T(8,128)S(1)}, u32[]{:S(2)}, u32[]{:S(2)}) collective-permute-start(f32[80,128]{1,0:T(8,128)S(1)} %fusion.6), channel_id=1, source_target_pairs={{0,2},{1,3},{2,0},{3,1},{4,6},{5,7},{6,4},{7,5},{8,10},{9,11},{10,... | collective-permute-start | bytes 122888 | tf_op jit(solution)/shard_map/ppermute | solution.py:17
  57.4 0.7 %far_products.5 = (f32[256,128]{1,0:T(8,128)S(1)}, bf16[256,128]{1,0:T(8,128)(2,1)S(1)}, bf16[256,128]{1,0:T(8,128)(2,1)S(1)}, bf16[256,128]{1,0:T(8,128)(2,1)S(1)}) custom-call(bf16[1024,2048]{1,0:T(8,128)(2,1)S(1)} %place_tiles.1.dense_ref, f32[1024,128]{1,0:T(8,128)S(1)} %near_products.5.total_ref, bf16[256,128]{1,0:T(8,128)(2,1)S(1)} %collective-permute-done.23.refs_0_, ...), custom_call_target="tpu_custom_call" | custom-call | flops 268435456 | bytes 2097152 | tf_op jit(solution)/shard_map/far_products/pallas_call | solution.py:180
  58.1 1.3 %collective-permute-done.32 = f32[80,128]{1,0:T(8,128)S(1)} collective-permute-done((f32[80,128]{1,0:T(8,128)S(1)}, f32[80,128]{1,0:T(8,128)S(1)}, u32[]{:S(2)}, u32[]{:S(2)}) %collective-permute-start.32) | collective-permute-done | bytes 40992 | tf_op jit(solution)/shard_map/ppermute | solution.py:17
  59.5 1.8 %collective-permute-start.36 = (bf16[416,128]{1,0:T(8,128)(2,1)S(1)}, bf16[416,128]{1,0:T(8,128)(2,1)S(1)}, u32[]{:S(2)}, u32[]{:S(2)}) collective-permute-start(bf16[416,128]{1,0:T(8,128)(2,1)S(1)} %get-tuple-element.51), channel_id=1, source_target_pairs={{0,24},{8,16},{16,8},{24,0},{1,25},{9,17},{17,9},{25,1},{2,26},{10... | collective-permute-start | bytes 319496 | tf_op jit(solution)/shard_map/ppermute | solution.py:17
  61.9 1.1 %collective-permute-start.34 = (bf16[416,128]{1,0:T(8,128)(2,1)S(1)}, bf16[416,128]{1,0:T(8,128)(2,1)S(1)}, u32[]{:S(2)}, u32[]{:S(2)}) collective-permute-start(bf16[416,128]{1,0:T(8,128)(2,1)S(1)} %get-tuple-element.49), channel_id=1, source_target_pairs={{0,8},{8,0},{16,24},{24,16},{1,9},{9,1},{17,25},{25,17},{2,10},{10... | collective-permute-start | bytes 319496 | tf_op jit(solution)/shard_map/ppermute | solution.py:17
  63.1 3.2 %collective-permute-done.36 = bf16[416,128]{1,0:T(8,128)(2,1)S(1)} collective-permute-done((bf16[416,128]{1,0:T(8,128)(2,1)S(1)}, bf16[416,128]{1,0:T(8,128)(2,1)S(1)}, u32[]{:S(2)}, u32[]{:S(2)}) %collective-permute-start.36) | collective-permute-done | bytes 106528 | tf_op jit(solution)/shard_map/ppermute | solution.py:17
  67.0 1.3 %collective-permute-done.37.far_ref = f32[4,80,128]{2,1,0:T(8,128)S(1)} collective-permute-done((f32[4,80,128]{2,1,0:T(8,128)S(1)}, f32[4,80,128]{2,1,0:T(8,128)S(1)}, u32[]{:S(2)}, u32[]{:S(2)}) %collective-permute-start.37) | collective-permute-done | bytes 163872 | tf_op jit(solution)/shard_map/ppermute | solution.py:17
  68.3 3.3 %finish.1 = (f32[256,128]{1,0:T(8,128)}, f32[256,128]{1,0:T(8,128)}) custom-call(s32[1]{0:T(128)} %bitcast.2.index_ref, f32[256,128]{1,0:T(8,128)S(1)} %copy-done, f32[256,128]{1,0:T(8,128)S(1)} %get-tuple-element.45.z1_ref, f32[256,128]{1,0:T(8,128)S(1)} %get-tuple-element.43.z2_ref, f32[256,128]{1,0:T(8,128)S(1)} %add_multiply_fusion.z3_ref, ...), custom_call_target="tpu_custom_call" | custom-call | tf_op jit(solution)/shard_map/finish/pallas_call | solution.py:362
  (82 shorter events, 12.7 us)
Async XLA Ops:
  1.6 10.2 %collective-permute-start = (bf16[256,128]{1,0:T(8,128)(2,1)S(1)}, bf16[256,128]{1,0:T(8,128)(2,1)S(1)}, u32[]{:S(2)}, u32[]{:S(2)}) collective-permute-start(bf16[256,128]{1,0:T(8,128)(2,1)S(1)} %multiply_convert_fusion.2.refs_3_), channel_id=1, source_target_pairs={{0,6},{1,7},{2,4},{3,5},{4,2},{5,3},{6,0},{7,1},{8,14},{9,15},{10,... | collective-permute-start | bytes 196616 | tf_op jit(solution)/shard_map/ppermute | solution.py:17
  6.8 5.6 %collective-permute-start.1 = (bf16[256,128]{1,0:T(8,128)(2,1)S(1)}, bf16[256,128]{1,0:T(8,128)(2,1)S(1)}, u32[]{:S(2)}, u32[]{:S(2)}) collective-permute-start(bf16[256,128]{1,0:T(8,128)(2,1)S(1)} %multiply_convert_fusion.2.refs_3_), channel_id=1, source_target_pairs={{0,4},{1,5},{2,6},{3,7},{4,0},{5,1},{6,2},{7,3},{8,12},{9,13},{10,... | collective-permute-start | bytes 196616 | tf_op jit(solution)/shard_map/ppermute | solution.py:17
  6.8 5.6 %collective-permute-start.2 = (bf16[256,128]{1,0:T(8,128)(2,1)S(1)}, bf16[256,128]{1,0:T(8,128)(2,1)S(1)}, u32[]{:S(2)}, u32[]{:S(2)}) collective-permute-start(bf16[256,128]{1,0:T(8,128)(2,1)S(1)} %multiply_convert_fusion.2.refs_3_), channel_id=1, source_target_pairs={{0,2},{1,3},{2,0},{3,1},{4,6},{5,7},{6,4},{7,5},{8,10},{9,11},{10,... | collective-permute-start | bytes 196616 | tf_op jit(solution)/shard_map/ppermute | solution.py:17
  11.7 1.9 %collective-permute-start.6 = (bf16[256,128]{1,0:T(8,128)(2,1)S(1)}, bf16[256,128]{1,0:T(8,128)(2,1)S(1)}, u32[]{:S(2)}, u32[]{:S(2)}) collective-permute-start(bf16[256,128]{1,0:T(8,128)(2,1)S(1)} %multiply_convert_fusion.2.refs_3_), channel_id=1, source_target_pairs={{0,1},{1,0},{2,3},{3,2},{4,5},{5,4},{6,7},{7,6},{8,9},{9,8},{10,11... | collective-permute-start | bytes 196616 | tf_op jit(solution)/shard_map/ppermute | solution.py:17
  14.5 5.3 %collective-permute-start.9 = (bf16[256,128]{1,0:T(8,128)(2,1)S(1)}, bf16[256,128]{1,0:T(8,128)(2,1)S(1)}, u32[]{:S(2)}, u32[]{:S(2)}) collective-permute-start(bf16[256,128]{1,0:T(8,128)(2,1)S(1)} %get-tuple-element.29), channel_id=1, source_target_pairs={{0,24},{8,16},{16,8},{24,0},{1,25},{9,17},{17,9},{25,1},{2,26},{10... | collective-permute-start | bytes 196616 | tf_op jit(solution)/shard_map/ppermute | solution.py:17
  17.0 4.3 %collective-permute-start.8 = (bf16[256,128]{1,0:T(8,128)(2,1)S(1)}, bf16[256,128]{1,0:T(8,128)(2,1)S(1)}, u32[]{:S(2)}, u32[]{:S(2)}) collective-permute-start(bf16[256,128]{1,0:T(8,128)(2,1)S(1)} %get-tuple-element.28), channel_id=1, source_target_pairs={{0,16},{8,24},{16,0},{24,8},{1,17},{9,25},{17,1},{25,9},{2,18},{10... | collective-permute-start | bytes 196616 | tf_op jit(solution)/shard_map/ppermute | solution.py:17
  17.7 4.3 %collective-permute-start.7 = (bf16[256,128]{1,0:T(8,128)(2,1)S(1)}, bf16[256,128]{1,0:T(8,128)(2,1)S(1)}, u32[]{:S(2)}, u32[]{:S(2)}) collective-permute-start(bf16[256,128]{1,0:T(8,128)(2,1)S(1)} %get-tuple-element.27), channel_id=1, source_target_pairs={{0,8},{8,0},{16,24},{24,16},{1,9},{9,1},{17,25},{25,17},{2,10},{10... | collective-permute-start | bytes 196616 | tf_op jit(solution)/shard_map/ppermute | solution.py:17
  22.1 6.3 %collective-permute-start.10 = (bf16[256,128]{1,0:T(8,128)(2,1)S(1)}, bf16[256,128]{1,0:T(8,128)(2,1)S(1)}, u32[]{:S(2)}, u32[]{:S(2)}) collective-permute-start(bf16[256,128]{1,0:T(8,128)(2,1)S(1)} %get-tuple-element.44.refs_3_), channel_id=1, source_target_pairs={{0,6},{1,7},{2,4},{3,5},{4,2},{5,3},{6,0},{7,1},{8,14},{9,15},{10,... | collective-permute-start | bytes 196616 | tf_op jit(solution)/shard_map/ppermute | solution.py:17
  25.7 5.5 %collective-permute-start.11 = (bf16[256,128]{1,0:T(8,128)(2,1)S(1)}, bf16[256,128]{1,0:T(8,128)(2,1)S(1)}, u32[]{:S(2)}, u32[]{:S(2)}) collective-permute-start(bf16[256,128]{1,0:T(8,128)(2,1)S(1)} %get-tuple-element.44.refs_3_), channel_id=1, source_target_pairs={{0,4},{1,5},{2,6},{3,7},{4,0},{5,1},{6,2},{7,3},{8,12},{9,13},{10,... | collective-permute-start | bytes 196616 | tf_op jit(solution)/shard_map/ppermute | solution.py:17
  25.7 5.5 %collective-permute-start.12 = (bf16[256,128]{1,0:T(8,128)(2,1)S(1)}, bf16[256,128]{1,0:T(8,128)(2,1)S(1)}, u32[]{:S(2)}, u32[]{:S(2)}) collective-permute-start(bf16[256,128]{1,0:T(8,128)(2,1)S(1)} %get-tuple-element.44.refs_3_), channel_id=1, source_target_pairs={{0,2},{1,3},{2,0},{3,1},{4,6},{5,7},{6,4},{7,5},{8,10},{9,11},{10,... | collective-permute-start | bytes 196616 | tf_op jit(solution)/shard_map/ppermute | solution.py:17
  26.6 5.8 %collective-permute-start.16 = (bf16[256,128]{1,0:T(8,128)(2,1)S(1)}, bf16[256,128]{1,0:T(8,128)(2,1)S(1)}, u32[]{:S(2)}, u32[]{:S(2)}) collective-permute-start(bf16[256,128]{1,0:T(8,128)(2,1)S(1)} %get-tuple-element.44.refs_3_), channel_id=1, source_target_pairs={{0,1},{1,0},{2,3},{3,2},{4,5},{5,4},{6,7},{7,6},{8,9},{9,8},{10,11... | collective-permute-start | bytes 196616 | tf_op jit(solution)/shard_map/ppermute | solution.py:17
  28.4 4.0 %collective-permute-start.13 = (bf16[256,128]{1,0:T(8,128)(2,1)S(1)}, bf16[256,128]{1,0:T(8,128)(2,1)S(1)}, u32[]{:S(2)}, u32[]{:S(2)}) collective-permute-start(bf16[256,128]{1,0:T(8,128)(2,1)S(1)} %collective-permute-done.10.refs_0_), channel_id=1, source_target_pairs={{0,1},{1,0},{2,3},{3,2},{4,5},{5,4},{6,7},{7,6},{8,9},{9,8},{10,11... | collective-permute-start | bytes 196616 | tf_op jit(solution)/shard_map/ppermute | solution.py:17
  33.3 5.4 %collective-permute-start.19 = (bf16[256,128]{1,0:T(8,128)(2,1)S(1)}, bf16[256,128]{1,0:T(8,128)(2,1)S(1)}, u32[]{:S(2)}, u32[]{:S(2)}) collective-permute-start(bf16[256,128]{1,0:T(8,128)(2,1)S(1)} %get-tuple-element.33), channel_id=1, source_target_pairs={{0,24},{8,16},{16,8},{24,0},{1,25},{9,17},{17,9},{25,1},{2,26},{10... | collective-permute-start | bytes 196616 | tf_op jit(solution)/shard_map/ppermute | solution.py:17
  35.1 4.9 %collective-permute-start.18 = (bf16[256,128]{1,0:T(8,128)(2,1)S(1)}, bf16[256,128]{1,0:T(8,128)(2,1)S(1)}, u32[]{:S(2)}, u32[]{:S(2)}) collective-permute-start(bf16[256,128]{1,0:T(8,128)(2,1)S(1)} %get-tuple-element.32), channel_id=1, source_target_pairs={{0,16},{8,24},{16,0},{24,8},{1,17},{9,25},{17,1},{25,9},{2,18},{10... | collective-permute-start | bytes 196616 | tf_op jit(solution)/shard_map/ppermute | solution.py:17
  36.3 4.3 %collective-permute-start.17 = (bf16[256,128]{1,0:T(8,128)(2,1)S(1)}, bf16[256,128]{1,0:T(8,128)(2,1)S(1)}, u32[]{:S(2)}, u32[]{:S(2)}) collective-permute-start(bf16[256,128]{1,0:T(8,128)(2,1)S(1)} %get-tuple-element.31), channel_id=1, source_target_pairs={{0,8},{8,0},{16,24},{24,16},{1,9},{9,1},{17,25},{25,17},{2,10},{10... | collective-permute-start | bytes 196616 | tf_op jit(solution)/shard_map/ppermute | solution.py:17
  41.1 4.5 %collective-permute-start.27 = (f32[4,80,128]{2,1,0:T(8,128)S(1)}, f32[4,80,128]{2,1,0:T(8,128)S(1)}, u32[]{:S(2)}, u32[]{:S(2)}) collective-permute-start(f32[4,80,128]{2,1,0:T(8,128)S(1)} %get-tuple-element.37), channel_id=1, source_target_pairs={{0,1},{1,0},{2,3},{3,2},{4,5},{5,4},{6,7},{7,6},{8,9},{9,8},{10,11... | collective-permute-start | bytes 491528 | tf_op jit(solution)/shard_map/ppermute | solution.py:17
  41.2 7.0 %collective-permute-start.20 = (bf16[256,128]{1,0:T(8,128)(2,1)S(1)}, bf16[256,128]{1,0:T(8,128)(2,1)S(1)}, u32[]{:S(2)}, u32[]{:S(2)}) collective-permute-start(bf16[256,128]{1,0:T(8,128)(2,1)S(1)} %get-tuple-element.42.refs_3_), channel_id=1, source_target_pairs={{0,6},{1,7},{2,4},{3,5},{4,2},{5,3},{6,0},{7,1},{8,14},{9,15},{10,... | collective-permute-start | bytes 196616 | tf_op jit(solution)/shard_map/ppermute | solution.py:17
  43.4 7.0 %collective-permute-start.21 = (bf16[256,128]{1,0:T(8,128)(2,1)S(1)}, bf16[256,128]{1,0:T(8,128)(2,1)S(1)}, u32[]{:S(2)}, u32[]{:S(2)}) collective-permute-start(bf16[256,128]{1,0:T(8,128)(2,1)S(1)} %get-tuple-element.42.refs_3_), channel_id=1, source_target_pairs={{0,4},{1,5},{2,6},{3,7},{4,0},{5,1},{6,2},{7,3},{8,12},{9,13},{10,... | collective-permute-start | bytes 196616 | tf_op jit(solution)/shard_map/ppermute | solution.py:17
  43.4 6.9 %collective-permute-start.22 = (bf16[256,128]{1,0:T(8,128)(2,1)S(1)}, bf16[256,128]{1,0:T(8,128)(2,1)S(1)}, u32[]{:S(2)}, u32[]{:S(2)}) collective-permute-start(bf16[256,128]{1,0:T(8,128)(2,1)S(1)} %get-tuple-element.42.refs_3_), channel_id=1, source_target_pairs={{0,2},{1,3},{2,0},{3,1},{4,6},{5,7},{6,4},{7,5},{8,10},{9,11},{10,... | collective-permute-start | bytes 196616 | tf_op jit(solution)/shard_map/ppermute | solution.py:17
  45.7 5.1 %collective-permute-start.30 = (f32[80,128]{1,0:T(8,128)S(1)}, f32[80,128]{1,0:T(8,128)S(1)}, u32[]{:S(2)}, u32[]{:S(2)}) collective-permute-start(f32[80,128]{1,0:T(8,128)S(1)} %get-tuple-element.47), channel_id=1, source_target_pairs={{0,24},{8,16},{16,8},{24,0},{1,25},{9,17},{17,9},{25,1},{2,26},{10... | collective-permute-start | bytes 122888 | tf_op jit(solution)/shard_map/ppermute | solution.py:17
  47.6 4.0 %collective-permute-start.29 = (f32[80,128]{1,0:T(8,128)S(1)}, f32[80,128]{1,0:T(8,128)S(1)}, u32[]{:S(2)}, u32[]{:S(2)}) collective-permute-start(f32[80,128]{1,0:T(8,128)S(1)} %get-tuple-element.48), channel_id=1, source_target_pairs={{0,16},{8,24},{16,0},{24,8},{1,17},{9,25},{17,1},{25,9},{2,18},{10... | collective-permute-start | bytes 122888 | tf_op jit(solution)/shard_map/ppermute | solution.py:17
  48.1 4.0 %collective-permute-start.28 = (f32[80,128]{1,0:T(8,128)S(1)}, f32[80,128]{1,0:T(8,128)S(1)}, u32[]{:S(2)}, u32[]{:S(2)}) collective-permute-start(f32[80,128]{1,0:T(8,128)S(1)} %get-tuple-element.46), channel_id=1, source_target_pairs={{0,8},{8,0},{16,24},{24,16},{1,9},{9,1},{17,25},{25,17},{2,10},{10... | collective-permute-start | bytes 122888 | tf_op jit(solution)/shard_map/ppermute | solution.py:17
  50.3 4.0 %collective-permute-start.26 = (bf16[256,128]{1,0:T(8,128)(2,1)S(1)}, bf16[256,128]{1,0:T(8,128)(2,1)S(1)}, u32[]{:S(2)}, u32[]{:S(2)}) collective-permute-start(bf16[256,128]{1,0:T(8,128)(2,1)S(1)} %get-tuple-element.42.refs_3_), channel_id=1, source_target_pairs={{0,1},{1,0},{2,3},{3,2},{4,5},{5,4},{6,7},{7,6},{8,9},{9,8},{10,11... | collective-permute-start | bytes 196616 | tf_op jit(solution)/shard_map/ppermute | solution.py:17
  50.3 4.0 %collective-permute-start.23 = (bf16[256,128]{1,0:T(8,128)(2,1)S(1)}, bf16[256,128]{1,0:T(8,128)(2,1)S(1)}, u32[]{:S(2)}, u32[]{:S(2)}) collective-permute-start(bf16[256,128]{1,0:T(8,128)(2,1)S(1)} %collective-permute-done.20.refs_0_), channel_id=1, source_target_pairs={{0,1},{1,0},{2,3},{3,2},{4,5},{5,4},{6,7},{7,6},{8,9},{9,8},{10,11... | collective-permute-start | bytes 196616 | tf_op jit(solution)/shard_map/ppermute | solution.py:17
  50.8 6.6 %collective-permute-start.24 = (bf16[256,128]{1,0:T(8,128)(2,1)S(1)}, bf16[256,128]{1,0:T(8,128)(2,1)S(1)}, u32[]{:S(2)}, u32[]{:S(2)}) collective-permute-start(bf16[256,128]{1,0:T(8,128)(2,1)S(1)} %collective-permute-done.21.refs_1_), channel_id=1, source_target_pairs={{0,1},{1,0},{2,3},{3,2},{4,5},{5,4},{6,7},{7,6},{8,9},{9,8},{10,11... | collective-permute-start | bytes 196616 | tf_op jit(solution)/shard_map/ppermute | solution.py:17
  51.6 5.8 %collective-permute-start.25 = (bf16[256,128]{1,0:T(8,128)(2,1)S(1)}, bf16[256,128]{1,0:T(8,128)(2,1)S(1)}, u32[]{:S(2)}, u32[]{:S(2)}) collective-permute-start(bf16[256,128]{1,0:T(8,128)(2,1)S(1)} %collective-permute-done.22.refs_2_), channel_id=1, source_target_pairs={{0,1},{1,0},{2,3},{3,2},{4,5},{5,4},{6,7},{7,6},{8,9},{9,8},{10,11... | collective-permute-start | bytes 196616 | tf_op jit(solution)/shard_map/ppermute | solution.py:17
  52.2 6.0 %collective-permute-start.33 = (f32[80,128]{1,0:T(8,128)S(1)}, f32[80,128]{1,0:T(8,128)S(1)}, u32[]{:S(2)}, u32[]{:S(2)}) collective-permute-start(f32[80,128]{1,0:T(8,128)S(1)} %fusion.6), channel_id=1, source_target_pairs={{0,6},{1,7},{2,4},{3,5},{4,2},{5,3},{6,0},{7,1},{8,14},{9,15},{10,... | collective-permute-start | bytes 122888 | tf_op jit(solution)/shard_map/ppermute | solution.py:17
  54.3 5.1 %collective-permute-start.32 = (f32[80,128]{1,0:T(8,128)S(1)}, f32[80,128]{1,0:T(8,128)S(1)}, u32[]{:S(2)}, u32[]{:S(2)}) collective-permute-start(f32[80,128]{1,0:T(8,128)S(1)} %fusion.6), channel_id=1, source_target_pairs={{0,4},{1,5},{2,6},{3,7},{4,0},{5,1},{6,2},{7,3},{8,12},{9,13},{10,... | collective-permute-start | bytes 122888 | tf_op jit(solution)/shard_map/ppermute | solution.py:17
  54.3 5.1 %collective-permute-start.31 = (f32[80,128]{1,0:T(8,128)S(1)}, f32[80,128]{1,0:T(8,128)S(1)}, u32[]{:S(2)}, u32[]{:S(2)}) collective-permute-start(f32[80,128]{1,0:T(8,128)S(1)} %fusion.6), channel_id=1, source_target_pairs={{0,2},{1,3},{2,0},{3,1},{4,6},{5,7},{6,4},{7,5},{8,10},{9,11},{10,... | collective-permute-start | bytes 122888 | tf_op jit(solution)/shard_map/ppermute | solution.py:17
  59.5 6.7 %collective-permute-start.36 = (bf16[416,128]{1,0:T(8,128)(2,1)S(1)}, bf16[416,128]{1,0:T(8,128)(2,1)S(1)}, u32[]{:S(2)}, u32[]{:S(2)}) collective-permute-start(bf16[416,128]{1,0:T(8,128)(2,1)S(1)} %get-tuple-element.51), channel_id=1, source_target_pairs={{0,24},{8,16},{16,8},{24,0},{1,25},{9,17},{17,9},{25,1},{2,26},{10... | collective-permute-start | bytes 319496 | tf_op jit(solution)/shard_map/ppermute | solution.py:17
  61.3 5.5 %collective-permute-start.35 = (bf16[416,128]{1,0:T(8,128)(2,1)S(1)}, bf16[416,128]{1,0:T(8,128)(2,1)S(1)}, u32[]{:S(2)}, u32[]{:S(2)}) collective-permute-start(bf16[416,128]{1,0:T(8,128)(2,1)S(1)} %get-tuple-element.50), channel_id=1, source_target_pairs={{0,16},{8,24},{16,0},{24,8},{1,17},{9,25},{17,1},{25,9},{2,18},{10... | collective-permute-start | bytes 319496 | tf_op jit(solution)/shard_map/ppermute | solution.py:17
  61.9 4.8 %collective-permute-start.34 = (bf16[416,128]{1,0:T(8,128)(2,1)S(1)}, bf16[416,128]{1,0:T(8,128)(2,1)S(1)}, u32[]{:S(2)}, u32[]{:S(2)}) collective-permute-start(bf16[416,128]{1,0:T(8,128)(2,1)S(1)} %get-tuple-element.49), channel_id=1, source_target_pairs={{0,8},{8,0},{16,24},{24,16},{1,9},{9,1},{17,25},{25,17},{2,10},{10... | collective-permute-start | bytes 319496 | tf_op jit(solution)/shard_map/ppermute | solution.py:17
  (11 other events, 57.1 us)

commit v5 on v4

--- a/solution.py
+++ b/solution.py
@@ -306,24 +306,22 @@
         return jnp.sum(eye * norm, axis=1, keepdims=True)
 
     keep0 = (n01 - excess) * scale
+    second_x = second_ref[:width]
+    left = jnp.concatenate([excess, n10, n01, n11, n21], axis=0)
+    right = jnp.concatenate([n01, n11, n02, n12, n22], axis=0)
+    ready = dot_short(left, jnp.concatenate([keep0, first_ref[:width]], axis=1))
     colsq0 = column_sum(
-        keep0 * (verts_all * keep0 + dot_short(excess, keep0) - 2.0 * n01) + eye * n11
+        keep0 * (verts_all * keep0 + ready[:width, :width] - 2.0 * n01) + eye * n11
     )
     q = inverse_norm(colsq0) * first_ref[width:]
+    applied = ready[:, width:] + dot_short(ready[:, :width] - right, q)
     p = first_ref[:width] + dot_short(keep0, q)
     square = dot(p, p, ((0,), (0,)))
     coeff = jnp.concatenate([p, -q], axis=0)
-    blocks = jnp.concatenate(
-        [
-            jnp.concatenate([excess, n01], axis=1),
-            jnp.concatenate([n10, n11], axis=1),
-            jnp.concatenate([n01, n02], axis=1),
-            jnp.concatenate([n11, n12], axis=1),
-            jnp.concatenate([n21, n22], axis=1),
-        ],
-        axis=0,
-    )
-    applied = dot_short(blocks, coeff)
+    f = dot_short(q, second_ref[2 * width :])
+    start = dot_short(jnp.concatenate([p, q], axis=0), second_x)
+    c0 = start[:width] + dot_short(keep0, f)
+    c1 = -(start[width:] + f)
     pair = jnp.concatenate(
         [applied[: 2 * width], applied[2 * width : 4 * width]], axis=1
     )
@@ -332,15 +330,13 @@
     u = column_sum(coeff * applied[3 * width :]) * scale
     keep1 = (eye - square) - (s - t)
     s = s + square
-    colsq1 = column_sum(keep1 * (dot_short(s, keep1) - 2.0 * t)) + u
+    kept = dot_short(jnp.concatenate([s, p, q], axis=0), keep1)
+    colsq1 = column_sum(keep1 * (kept[:width] - 2.0 * t)) + u
     v = inverse_norm(colsq1 * verts_all) * second_ref[width : 2 * width]
-    e = second_ref[:width] + dot_short(keep1, v)
-    f = dot_short(q, second_ref[2 * width :])
-    mixed = dot_short(jnp.concatenate([p, q], axis=0), jnp.concatenate([e, v], axis=1))
-    a0 = mixed[:width, :width] + dot_short(keep0, f)
-    a1 = -(mixed[width:, :width] + mixed[:width, width:] + f)
-    a2 = mixed[width:, width:]
-    none = jnp.zeros_like(a0)
+    w0, w1 = kept[width : 2 * width], -(kept[2 * width :] + p)
+    none = jnp.zeros_like(c0)
+    mixed = dot_short(jnp.concatenate([w0, w1, q], axis=0), v)
+    a0, a1, a2 = c0 + mixed[:width], c1 + mixed[width : 2 * width], mixed[2 * width :]
     spread = jnp.concatenate(
         [
             jnp.concatenate([a0, none], axis=1),

time: 71.9 us -> 71.6 us (level)
  transfers between devices with their start and end apart: 38 -> 38, of which waited for: 18 -> 18; matrix products, arithmetic and copies ran while one was open for 1% -> 1% of each run, Pallas kernels for 7% -> 8%
where the time goes in v5:
time: 71.6 us
  starting transfers between devices  36 us (50%)
  waiting for transfers between devices  20 us (28%)
  Pallas kernels  10.2 us (14%)
  other arithmetic  2.14 us (3%)
  local copies, waits for them, and re-layouts  1.62 us (2%)
  between operations  1.62 us (2%)
    ppermute x38, starting transfers between devices, swap(): return lax.ppermute(array, axis, [(k, k ^ mask) for k in range(size)])  36 us
    ppermute x38, waiting for transfers between devices, swap(): return lax.ppermute(array, axis, [(k, k ^ mask) for k in range(size)])  20 us
    pallas_call x1, Pallas kernels, finish(): pl.pallas_call(functools.partial(finish_kernel, pieces, verts_all), out_s...  2.92 us
    pallas_call x3, Pallas kernels, far_products(): pl.pallas_call(far_kernel, out_shape=[jax.ShapeDtypeStruct((sub, width),...  2.2 us
    pallas_call x3, Pallas kernels, near_products(): pl.pallas_call(near_kernel, out_shape=jax.ShapeDtypeStruct((dense.shape[0...  2.17 us
    pallas_call x1, Pallas kernels, place_tiles(): pl.pallas_call(place_kernel, out_shape=jax.ShapeDtypeStruct((height, widt...  1.99 us
    unnamed x10, local copies, waits for them, and re-layouts  1.61 us
  transfers between devices with their start and end apart: 38, of which 18 were waited for; matrix products, arithmetic and copies ran while one was open for 1% of the time, Pallas kernels for 8%

profile of v5, /device:TPU:0, one launch (start us, length us, event | category | flops | bytes accessed | tf_op | source)
XLA Modules:
  0.0 71.6 jit_solution(10422062719370611411)
XLA Ops:
  0.6 1.0 %multiply_convert_fusion.2.refs_3_ = bf16[256,128]{1,0:T(8,128)(2,1)S(1)} fusion(f32[256,128]{1,0:T(8,128)} %x_ref.5, f32[256]{0:T(256)} %param.9), kind=kLoop, calls=%fused_computation.12 | loop fusion | flops 65536 | bytes 197632 | tf_op jit(solution)/shard_map/convert_element_type | solution.py:416
  1.6 5.1 %collective-permute-start = (bf16[256,128]{1,0:T(8,128)(2,1)S(1)}, bf16[256,128]{1,0:T(8,128)(2,1)S(1)}, u32[]{:S(2)}, u32[]{:S(2)}) collective-permute-start(bf16[256,128]{1,0:T(8,128)(2,1)S(1)} %multiply_convert_fusion.2.refs_3_), channel_id=1, source_target_pairs={{0,6},{1,7},{2,4},{3,5},{4,2},{5,3},{6,0},{7,1},{8,14},{9,15},{10,... | collective-permute-start | bytes 196616 | tf_op jit(solution)/shard_map/ppermute | solution.py:17
  8.8 1.6 %copy-done.1 = bf16[1,1,64,128,128]{4,3,2,1,0:T(8,128)(2,1)S(1)} copy-done((bf16[1,1,64,128,128]{4,3,2,1,0:T(8,128)(2,1)S(1)}, bf16[1,1,64,128,128]{4,3,2,1,0:T(8,128)(2,1)}, u32[]{:S(2)}) %copy-start.1) | copy-done | bytes 2097176
  10.3 2.0 %place_tiles.1.dense_ref = bf16[1024,2048]{1,0:T(8,128)(2,1)S(1)} custom-call(s32[1]{0:T(128)} %bitcast.50.count_ref, s32[64]{0:T(128)S(1)} %get-tuple-element.22.cols_ref, s32[64]{0:T(128)S(1)} %get-tuple-element.23.rows_ref, bf16[64,128,128]{2,1,0:T(8,128)(2,1)S(1)} %bitcast.51), custom_call_target="tpu_custom_call" | custom-call | bytes 8388608 | tf_op jit(solution)/shard_map/place_tiles/pallas_call | solution.py:120
  14.4 0.7 %far_products.3 = (f32[256,128]{1,0:T(8,128)S(1)}, bf16[256,128]{1,0:T(8,128)(2,1)S(1)}, bf16[256,128]{1,0:T(8,128)(2,1)S(1)}, bf16[256,128]{1,0:T(8,128)(2,1)S(1)}) custom-call(bf16[1024,2048]{1,0:T(8,128)(2,1)S(1)} %place_tiles.1.dense_ref, f32[1024,128]{1,0:T(8,128)S(1)} %near_products.3.total_ref, bf16[256,128]{1,0:T(8,128)(2,1)S(1)} %collective-permute-done.3.refs_0_, ...), custom_call_target="tpu_custom_call" | custom-call | flops 268435456 | bytes 2097152 | tf_op jit(solution)/shard_map/far_products/pallas_call | solution.py:180
  15.1 2.1 %collective-permute-start.9 = (bf16[256,128]{1,0:T(8,128)(2,1)S(1)}, bf16[256,128]{1,0:T(8,128)(2,1)S(1)}, u32[]{:S(2)}, u32[]{:S(2)}) collective-permute-start(bf16[256,128]{1,0:T(8,128)(2,1)S(1)} %get-tuple-element.29), channel_id=1, source_target_pairs={{0,24},{8,16},{16,8},{24,0},{1,25},{9,17},{17,9},{25,1},{2,26},{10... | collective-permute-start | bytes 196616 | tf_op jit(solution)/shard_map/ppermute | solution.py:17
  17.6 1.1 %collective-permute-start.7 = (bf16[256,128]{1,0:T(8,128)(2,1)S(1)}, bf16[256,128]{1,0:T(8,128)(2,1)S(1)}, u32[]{:S(2)}, u32[]{:S(2)}) collective-permute-start(bf16[256,128]{1,0:T(8,128)(2,1)S(1)} %get-tuple-element.27), channel_id=1, source_target_pairs={{0,8},{8,0},{16,24},{24,16},{1,9},{9,1},{17,25},{25,17},{2,10},{10... | collective-permute-start | bytes 196616 | tf_op jit(solution)/shard_map/ppermute | solution.py:17
  18.7 1.8 %collective-permute-done.9 = bf16[256,128]{1,0:T(8,128)(2,1)S(1)} collective-permute-done((bf16[256,128]{1,0:T(8,128)(2,1)S(1)}, bf16[256,128]{1,0:T(8,128)(2,1)S(1)}, u32[]{:S(2)}, u32[]{:S(2)}) %collective-permute-start.9) | collective-permute-done | bytes 65568 | tf_op jit(solution)/shard_map/ppermute | solution.py:17
  20.5 1.3 %collective-permute-done.8 = bf16[256,128]{1,0:T(8,128)(2,1)S(1)} collective-permute-done((bf16[256,128]{1,0:T(8,128)(2,1)S(1)}, bf16[256,128]{1,0:T(8,128)(2,1)S(1)}, u32[]{:S(2)}, u32[]{:S(2)}) %collective-permute-start.8) | collective-permute-done | bytes 65568 | tf_op jit(solution)/shard_map/ppermute | solution.py:17
  21.9 4.2 %collective-permute-start.10 = (bf16[256,128]{1,0:T(8,128)(2,1)S(1)}, bf16[256,128]{1,0:T(8,128)(2,1)S(1)}, u32[]{:S(2)}, u32[]{:S(2)}) collective-permute-start(bf16[256,128]{1,0:T(8,128)(2,1)S(1)} %get-tuple-element.44.refs_3_), channel_id=1, source_target_pairs={{0,6},{1,7},{2,4},{3,5},{4,2},{5,3},{6,0},{7,1},{8,14},{9,15},{10,... | collective-permute-start | bytes 196616 | tf_op jit(solution)/shard_map/ppermute | solution.py:17
  26.8 1.7 %collective-permute-done.10.refs_0_ = bf16[256,128]{1,0:T(8,128)(2,1)S(1)} collective-permute-done((bf16[256,128]{1,0:T(8,128)(2,1)S(1)}, bf16[256,128]{1,0:T(8,128)(2,1)S(1)}, u32[]{:S(2)}, u32[]{:S(2)}) %collective-permute-start.10) | collective-permute-done | bytes 65568 | tf_op jit(solution)/shard_map/ppermute | solution.py:17
  28.5 2.9 %collective-permute-done.11.refs_1_ = bf16[256,128]{1,0:T(8,128)(2,1)S(1)} collective-permute-done((bf16[256,128]{1,0:T(8,128)(2,1)S(1)}, bf16[256,128]{1,0:T(8,128)(2,1)S(1)}, u32[]{:S(2)}, u32[]{:S(2)}) %collective-permute-start.11) | collective-permute-done | bytes 65568 | tf_op jit(solution)/shard_map/ppermute | solution.py:17
  33.6 1.5 %collective-permute-start.19 = (bf16[256,128]{1,0:T(8,128)(2,1)S(1)}, bf16[256,128]{1,0:T(8,128)(2,1)S(1)}, u32[]{:S(2)}, u32[]{:S(2)}) collective-permute-start(bf16[256,128]{1,0:T(8,128)(2,1)S(1)} %get-tuple-element.33), channel_id=1, source_target_pairs={{0,24},{8,16},{16,8},{24,0},{1,25},{9,17},{17,9},{25,1},{2,26},{10... | collective-permute-start | bytes 196616 | tf_op jit(solution)/shard_map/ppermute | solution.py:17
  35.1 1.2 %collective-permute-start.18 = (bf16[256,128]{1,0:T(8,128)(2,1)S(1)}, bf16[256,128]{1,0:T(8,128)(2,1)S(1)}, u32[]{:S(2)}, u32[]{:S(2)}) collective-permute-start(bf16[256,128]{1,0:T(8,128)(2,1)S(1)} %get-tuple-element.32), channel_id=1, source_target_pairs={{0,16},{8,24},{16,0},{24,8},{1,17},{9,25},{17,1},{25,9},{2,18},{10... | collective-permute-start | bytes 196616 | tf_op jit(solution)/shard_map/ppermute | solution.py:17
  36.3 0.9 %collective-permute-start.17 = (bf16[256,128]{1,0:T(8,128)(2,1)S(1)}, bf16[256,128]{1,0:T(8,128)(2,1)S(1)}, u32[]{:S(2)}, u32[]{:S(2)}) collective-permute-start(bf16[256,128]{1,0:T(8,128)(2,1)S(1)} %get-tuple-element.31), channel_id=1, source_target_pairs={{0,8},{8,0},{16,24},{24,16},{1,9},{9,1},{17,25},{25,17},{2,10},{10... | collective-permute-start | bytes 196616 | tf_op jit(solution)/shard_map/ppermute | solution.py:17
  37.6 1.3 %collective-permute-done.19 = bf16[256,128]{1,0:T(8,128)(2,1)S(1)} collective-permute-done((bf16[256,128]{1,0:T(8,128)(2,1)S(1)}, bf16[256,128]{1,0:T(8,128)(2,1)S(1)}, u32[]{:S(2)}, u32[]{:S(2)}) %collective-permute-start.19) | collective-permute-done | bytes 65568 | tf_op jit(solution)/shard_map/ppermute | solution.py:17
  39.0 1.3 %collective-permute-done.18 = bf16[256,128]{1,0:T(8,128)(2,1)S(1)} collective-permute-done((bf16[256,128]{1,0:T(8,128)(2,1)S(1)}, bf16[256,128]{1,0:T(8,128)(2,1)S(1)}, u32[]{:S(2)}, u32[]{:S(2)}) %collective-permute-start.18) | collective-permute-done | bytes 65568 | tf_op jit(solution)/shard_map/ppermute | solution.py:17
  41.1 2.3 %collective-permute-start.20 = (bf16[256,128]{1,0:T(8,128)(2,1)S(1)}, bf16[256,128]{1,0:T(8,128)(2,1)S(1)}, u32[]{:S(2)}, u32[]{:S(2)}) collective-permute-start(bf16[256,128]{1,0:T(8,128)(2,1)S(1)} %get-tuple-element.42.refs_3_), channel_id=1, source_target_pairs={{0,6},{1,7},{2,4},{3,5},{4,2},{5,3},{6,0},{7,1},{8,14},{9,15},{10,... | collective-permute-start | bytes 196616 | tf_op jit(solution)/shard_map/ppermute | solution.py:17
  43.9 1.7 %collective-permute-start.22 = (bf16[256,128]{1,0:T(8,128)(2,1)S(1)}, bf16[256,128]{1,0:T(8,128)(2,1)S(1)}, u32[]{:S(2)}, u32[]{:S(2)}) collective-permute-start(bf16[256,128]{1,0:T(8,128)(2,1)S(1)} %get-tuple-element.42.refs_3_), channel_id=1, source_target_pairs={{0,2},{1,3},{2,0},{3,1},{4,6},{5,7},{6,4},{7,5},{8,10},{9,11},{10,... | collective-permute-start | bytes 196616 | tf_op jit(solution)/shard_map/ppermute | solution.py:17
  45.6 1.8 %collective-permute-start.30 = (f32[80,128]{1,0:T(8,128)S(1)}, f32[80,128]{1,0:T(8,128)S(1)}, u32[]{:S(2)}, u32[]{:S(2)}) collective-permute-start(f32[80,128]{1,0:T(8,128)S(1)} %get-tuple-element.47), channel_id=1, source_target_pairs={{0,24},{8,16},{16,8},{24,0},{1,25},{9,17},{17,9},{25,1},{2,26},{10... | collective-permute-start | bytes 122888 | tf_op jit(solution)/shard_map/ppermute | solution.py:17
  48.0 1.2 %collective-permute-start.28 = (f32[80,128]{1,0:T(8,128)S(1)}, f32[80,128]{1,0:T(8,128)S(1)}, u32[]{:S(2)}, u32[]{:S(2)}) collective-permute-start(f32[80,128]{1,0:T(8,128)S(1)} %get-tuple-element.46), channel_id=1, source_target_pairs={{0,8},{8,0},{16,24},{24,16},{1,9},{9,1},{17,25},{25,17},{2,10},{10... | collective-permute-start | bytes 122888 | tf_op jit(solution)/shard_map/ppermute | solution.py:17
  49.2 1.3 %collective-permute-done.21.refs_1_ = bf16[256,128]{1,0:T(8,128)(2,1)S(1)} collective-permute-done((bf16[256,128]{1,0:T(8,128)(2,1)S(1)}, bf16[256,128]{1,0:T(8,128)(2,1)S(1)}, u32[]{:S(2)}, u32[]{:S(2)}) %collective-permute-start.21) | collective-permute-done | bytes 65568 | tf_op jit(solution)/shard_map/ppermute | solution.py:17
  52.0 2.3 %collective-permute-start.33 = (f32[80,128]{1,0:T(8,128)S(1)}, f32[80,128]{1,0:T(8,128)S(1)}, u32[]{:S(2)}, u32[]{:S(2)}) collective-permute-start(f32[80,128]{1,0:T(8,128)S(1)} %fusion.6), channel_id=1, source_target_pairs={{0,6},{1,7},{2,4},{3,5},{4,2},{5,3},{6,0},{7,1},{8,14},{9,15},{10,... | collective-permute-start | bytes 122888 | tf_op jit(solution)/shard_map/ppermute | solution.py:17
  54.3 0.8 %collective-permute-start.32 = (f32[80,128]{1,0:T(8,128)S(1)}, f32[80,128]{1,0:T(8,128)S(1)}, u32[]{:S(2)}, u32[]{:S(2)}) collective-permute-start(f32[80,128]{1,0:T(8,128)S(1)} %fusion.6), channel_id=1, source_target_pairs={{0,4},{1,5},{2,6},{3,7},{4,0},{5,1},{6,2},{7,3},{8,12},{9,13},{10,... | collective-permute-start | bytes 122888 | tf_op jit(solution)/shard_map/ppermute | solution.py:17
  55.1 1.4 %collective-permute-start.31 = (f32[80,128]{1,0:T(8,128)S(1)}, f32[80,128]{1,0:T(8,128)S(1)}, u32[]{:S(2)}, u32[]{:S(2)}) collective-permute-start(f32[80,128]{1,0:T(8,128)S(1)} %fusion.6), channel_id=1, source_target_pairs={{0,2},{1,3},{2,0},{3,1},{4,6},{5,7},{6,4},{7,5},{8,10},{9,11},{10,... | collective-permute-start | bytes 122888 | tf_op jit(solution)/shard_map/ppermute | solution.py:17
  58.0 1.5 %collective-permute-done.32 = f32[80,128]{1,0:T(8,128)S(1)} collective-permute-done((f32[80,128]{1,0:T(8,128)S(1)}, f32[80,128]{1,0:T(8,128)S(1)}, u32[]{:S(2)}, u32[]{:S(2)}) %collective-permute-start.32) | collective-permute-done | bytes 40992 | tf_op jit(solution)/shard_map/ppermute | solution.py:17
  59.8 1.2 %collective-permute-start.36 = (bf16[416,128]{1,0:T(8,128)(2,1)S(1)}, bf16[416,128]{1,0:T(8,128)(2,1)S(1)}, u32[]{:S(2)}, u32[]{:S(2)}) collective-permute-start(bf16[416,128]{1,0:T(8,128)(2,1)S(1)} %get-tuple-element.51), channel_id=1, source_target_pairs={{0,24},{8,16},{16,8},{24,0},{1,25},{9,17},{17,9},{25,1},{2,26},{10... | collective-permute-start | bytes 319496 | tf_op jit(solution)/shard_map/ppermute | solution.py:17
  61.0 1.0 %collective-permute-start.35 = (bf16[416,128]{1,0:T(8,128)(2,1)S(1)}, bf16[416,128]{1,0:T(8,128)(2,1)S(1)}, u32[]{:S(2)}, u32[]{:S(2)}) collective-permute-start(bf16[416,128]{1,0:T(8,128)(2,1)S(1)} %get-tuple-element.50), channel_id=1, source_target_pairs={{0,16},{8,24},{16,0},{24,8},{1,17},{9,25},{17,1},{25,9},{2,18},{10... | collective-permute-start | bytes 319496 | tf_op jit(solution)/shard_map/ppermute | solution.py:17
  62.0 1.4 %collective-permute-start.34 = (bf16[416,128]{1,0:T(8,128)(2,1)S(1)}, bf16[416,128]{1,0:T(8,128)(2,1)S(1)}, u32[]{:S(2)}, u32[]{:S(2)}) collective-permute-start(bf16[416,128]{1,0:T(8,128)(2,1)S(1)} %get-tuple-element.49), channel_id=1, source_target_pairs={{0,8},{8,0},{16,24},{24,16},{1,9},{9,1},{17,25},{25,17},{2,10},{10... | collective-permute-start | bytes 319496 | tf_op jit(solution)/shard_map/ppermute | solution.py:17
  63.4 3.0 %collective-permute-done.36 = bf16[416,128]{1,0:T(8,128)(2,1)S(1)} collective-permute-done((bf16[416,128]{1,0:T(8,128)(2,1)S(1)}, bf16[416,128]{1,0:T(8,128)(2,1)S(1)}, u32[]{:S(2)}, u32[]{:S(2)}) %collective-permute-start.36) | collective-permute-done | bytes 106528 | tf_op jit(solution)/shard_map/ppermute | solution.py:17
  67.4 1.3 %collective-permute-done.37.far_ref = f32[4,80,128]{2,1,0:T(8,128)S(1)} collective-permute-done((f32[4,80,128]{2,1,0:T(8,128)S(1)}, f32[4,80,128]{2,1,0:T(8,128)S(1)}, u32[]{:S(2)}, u32[]{:S(2)}) %collective-permute-start.37) | collective-permute-done | bytes 163872 | tf_op jit(solution)/shard_map/ppermute | solution.py:17
  68.6 2.9 %finish.1 = (f32[256,128]{1,0:T(8,128)}, f32[256,128]{1,0:T(8,128)}) custom-call(s32[1]{0:T(128)} %bitcast.2.index_ref, f32[256,128]{1,0:T(8,128)S(1)} %copy-done, f32[256,128]{1,0:T(8,128)S(1)} %get-tuple-element.45.z1_ref, f32[256,128]{1,0:T(8,128)S(1)} %get-tuple-element.43.z2_ref, f32[256,128]{1,0:T(8,128)S(1)} %add_multiply_fusion.z3_ref, ...), custom_call_target="tpu_custom_call" | custom-call | tf_op jit(solution)/shard_map/finish/pallas_call | solution.py:358
  (82 shorter events, 13.2 us)
Async XLA Ops:
  1.6 10.8 %collective-permute-start = (bf16[256,128]{1,0:T(8,128)(2,1)S(1)}, bf16[256,128]{1,0:T(8,128)(2,1)S(1)}, u32[]{:S(2)}, u32[]{:S(2)}) collective-permute-start(bf16[256,128]{1,0:T(8,128)(2,1)S(1)} %multiply_convert_fusion.2.refs_3_), channel_id=1, source_target_pairs={{0,6},{1,7},{2,4},{3,5},{4,2},{5,3},{6,0},{7,1},{8,14},{9,15},{10,... | collective-permute-start | bytes 196616 | tf_op jit(solution)/shard_map/ppermute | solution.py:17
  6.8 6.2 %collective-permute-start.1 = (bf16[256,128]{1,0:T(8,128)(2,1)S(1)}, bf16[256,128]{1,0:T(8,128)(2,1)S(1)}, u32[]{:S(2)}, u32[]{:S(2)}) collective-permute-start(bf16[256,128]{1,0:T(8,128)(2,1)S(1)} %multiply_convert_fusion.2.refs_3_), channel_id=1, source_target_pairs={{0,4},{1,5},{2,6},{3,7},{4,0},{5,1},{6,2},{7,3},{8,12},{9,13},{10,... | collective-permute-start | bytes 196616 | tf_op jit(solution)/shard_map/ppermute | solution.py:17
  6.8 6.3 %collective-permute-start.2 = (bf16[256,128]{1,0:T(8,128)(2,1)S(1)}, bf16[256,128]{1,0:T(8,128)(2,1)S(1)}, u32[]{:S(2)}, u32[]{:S(2)}) collective-permute-start(bf16[256,128]{1,0:T(8,128)(2,1)S(1)} %multiply_convert_fusion.2.refs_3_), channel_id=1, source_target_pairs={{0,2},{1,3},{2,0},{3,1},{4,6},{5,7},{6,4},{7,5},{8,10},{9,11},{10,... | collective-permute-start | bytes 196616 | tf_op jit(solution)/shard_map/ppermute | solution.py:17
  12.4 1.8 %collective-permute-start.6 = (bf16[256,128]{1,0:T(8,128)(2,1)S(1)}, bf16[256,128]{1,0:T(8,128)(2,1)S(1)}, u32[]{:S(2)}, u32[]{:S(2)}) collective-permute-start(bf16[256,128]{1,0:T(8,128)(2,1)S(1)} %multiply_convert_fusion.2.refs_3_), channel_id=1, source_target_pairs={{0,1},{1,0},{2,3},{3,2},{4,5},{5,4},{6,7},{7,6},{8,9},{9,8},{10,11... | collective-permute-start | bytes 196616 | tf_op jit(solution)/shard_map/ppermute | solution.py:17
  15.1 5.4 %collective-permute-start.9 = (bf16[256,128]{1,0:T(8,128)(2,1)S(1)}, bf16[256,128]{1,0:T(8,128)(2,1)S(1)}, u32[]{:S(2)}, u32[]{:S(2)}) collective-permute-start(bf16[256,128]{1,0:T(8,128)(2,1)S(1)} %get-tuple-element.29), channel_id=1, source_target_pairs={{0,24},{8,16},{16,8},{24,0},{1,25},{9,17},{17,9},{25,1},{2,26},{10... | collective-permute-start | bytes 196616 | tf_op jit(solution)/shard_map/ppermute | solution.py:17
  17.2 4.6 %collective-permute-start.8 = (bf16[256,128]{1,0:T(8,128)(2,1)S(1)}, bf16[256,128]{1,0:T(8,128)(2,1)S(1)}, u32[]{:S(2)}, u32[]{:S(2)}) collective-permute-start(bf16[256,128]{1,0:T(8,128)(2,1)S(1)} %get-tuple-element.28), channel_id=1, source_target_pairs={{0,16},{8,24},{16,0},{24,8},{1,17},{9,25},{17,1},{25,9},{2,18},{10... | collective-permute-start | bytes 196616 | tf_op jit(solution)/shard_map/ppermute | solution.py:17
  17.6 4.3 %collective-permute-start.7 = (bf16[256,128]{1,0:T(8,128)(2,1)S(1)}, bf16[256,128]{1,0:T(8,128)(2,1)S(1)}, u32[]{:S(2)}, u32[]{:S(2)}) collective-permute-start(bf16[256,128]{1,0:T(8,128)(2,1)S(1)} %get-tuple-element.27), channel_id=1, source_target_pairs={{0,8},{8,0},{16,24},{24,16},{1,9},{9,1},{17,25},{25,17},{2,10},{10... | collective-permute-start | bytes 196616 | tf_op jit(solution)/shard_map/ppermute | solution.py:17
  21.9 6.6 %collective-permute-start.10 = (bf16[256,128]{1,0:T(8,128)(2,1)S(1)}, bf16[256,128]{1,0:T(8,128)(2,1)S(1)}, u32[]{:S(2)}, u32[]{:S(2)}) collective-permute-start(bf16[256,128]{1,0:T(8,128)(2,1)S(1)} %get-tuple-element.44.refs_3_), channel_id=1, source_target_pairs={{0,6},{1,7},{2,4},{3,5},{4,2},{5,3},{6,0},{7,1},{8,14},{9,15},{10,... | collective-permute-start | bytes 196616 | tf_op jit(solution)/shard_map/ppermute | solution.py:17
  26.2 5.2 %collective-permute-start.11 = (bf16[256,128]{1,0:T(8,128)(2,1)S(1)}, bf16[256,128]{1,0:T(8,128)(2,1)S(1)}, u32[]{:S(2)}, u32[]{:S(2)}) collective-permute-start(bf16[256,128]{1,0:T(8,128)(2,1)S(1)} %get-tuple-element.44.refs_3_), channel_id=1, source_target_pairs={{0,4},{1,5},{2,6},{3,7},{4,0},{5,1},{6,2},{7,3},{8,12},{9,13},{10,... | collective-permute-start | bytes 196616 | tf_op jit(solution)/shard_map/ppermute | solution.py:17
  26.2 5.4 %collective-permute-start.12 = (bf16[256,128]{1,0:T(8,128)(2,1)S(1)}, bf16[256,128]{1,0:T(8,128)(2,1)S(1)}, u32[]{:S(2)}, u32[]{:S(2)}) collective-permute-start(bf16[256,128]{1,0:T(8,128)(2,1)S(1)} %get-tuple-element.44.refs_3_), channel_id=1, source_target_pairs={{0,2},{1,3},{2,0},{3,1},{4,6},{5,7},{6,4},{7,5},{8,10},{9,11},{10,... | collective-permute-start | bytes 196616 | tf_op jit(solution)/shard_map/ppermute | solution.py:17
  26.8 5.8 %collective-permute-start.16 = (bf16[256,128]{1,0:T(8,128)(2,1)S(1)}, bf16[256,128]{1,0:T(8,128)(2,1)S(1)}, u32[]{:S(2)}, u32[]{:S(2)}) collective-permute-start(bf16[256,128]{1,0:T(8,128)(2,1)S(1)} %get-tuple-element.44.refs_3_), channel_id=1, source_target_pairs={{0,1},{1,0},{2,3},{3,2},{4,5},{5,4},{6,7},{7,6},{8,9},{9,8},{10,11... | collective-permute-start | bytes 196616 | tf_op jit(solution)/shard_map/ppermute | solution.py:17
  28.5 4.1 %collective-permute-start.13 = (bf16[256,128]{1,0:T(8,128)(2,1)S(1)}, bf16[256,128]{1,0:T(8,128)(2,1)S(1)}, u32[]{:S(2)}, u32[]{:S(2)}) collective-permute-start(bf16[256,128]{1,0:T(8,128)(2,1)S(1)} %collective-permute-done.10.refs_0_), channel_id=1, source_target_pairs={{0,1},{1,0},{2,3},{3,2},{4,5},{5,4},{6,7},{7,6},{8,9},{9,8},{10,11... | collective-permute-start | bytes 196616 | tf_op jit(solution)/shard_map/ppermute | solution.py:17
  33.6 5.4 %collective-permute-start.19 = (bf16[256,128]{1,0:T(8,128)(2,1)S(1)}, bf16[256,128]{1,0:T(8,128)(2,1)S(1)}, u32[]{:S(2)}, u32[]{:S(2)}) collective-permute-start(bf16[256,128]{1,0:T(8,128)(2,1)S(1)} %get-tuple-element.33), channel_id=1, source_target_pairs={{0,24},{8,16},{16,8},{24,0},{1,25},{9,17},{17,9},{25,1},{2,26},{10... | collective-permute-start | bytes 196616 | tf_op jit(solution)/shard_map/ppermute | solution.py:17
  35.1 5.2 %collective-permute-start.18 = (bf16[256,128]{1,0:T(8,128)(2,1)S(1)}, bf16[256,128]{1,0:T(8,128)(2,1)S(1)}, u32[]{:S(2)}, u32[]{:S(2)}) collective-permute-start(bf16[256,128]{1,0:T(8,128)(2,1)S(1)} %get-tuple-element.32), channel_id=1, source_target_pairs={{0,16},{8,24},{16,0},{24,8},{1,17},{9,25},{17,1},{25,9},{2,18},{10... | collective-permute-start | bytes 196616 | tf_op jit(solution)/shard_map/ppermute | solution.py:17
  36.3 4.3 %collective-permute-start.17 = (bf16[256,128]{1,0:T(8,128)(2,1)S(1)}, bf16[256,128]{1,0:T(8,128)(2,1)S(1)}, u32[]{:S(2)}, u32[]{:S(2)}) collective-permute-start(bf16[256,128]{1,0:T(8,128)(2,1)S(1)} %get-tuple-element.31), channel_id=1, source_target_pairs={{0,8},{8,0},{16,24},{24,16},{1,9},{9,1},{17,25},{25,17},{2,10},{10... | collective-permute-start | bytes 196616 | tf_op jit(solution)/shard_map/ppermute | solution.py:17
  41.0 4.5 %collective-permute-start.27 = (f32[4,80,128]{2,1,0:T(8,128)S(1)}, f32[4,80,128]{2,1,0:T(8,128)S(1)}, u32[]{:S(2)}, u32[]{:S(2)}) collective-permute-start(f32[4,80,128]{2,1,0:T(8,128)S(1)} %get-tuple-element.37), channel_id=1, source_target_pairs={{0,1},{1,0},{2,3},{3,2},{4,5},{5,4},{6,7},{7,6},{8,9},{9,8},{10,11... | collective-permute-start | bytes 491528 | tf_op jit(solution)/shard_map/ppermute | solution.py:17
  41.1 6.9 %collective-permute-start.20 = (bf16[256,128]{1,0:T(8,128)(2,1)S(1)}, bf16[256,128]{1,0:T(8,128)(2,1)S(1)}, u32[]{:S(2)}, u32[]{:S(2)}) collective-permute-start(bf16[256,128]{1,0:T(8,128)(2,1)S(1)} %get-tuple-element.42.refs_3_), channel_id=1, source_target_pairs={{0,6},{1,7},{2,4},{3,5},{4,2},{5,3},{6,0},{7,1},{8,14},{9,15},{10,... | collective-permute-start | bytes 196616 | tf_op jit(solution)/shard_map/ppermute | solution.py:17
  43.5 7.0 %collective-permute-start.21 = (bf16[256,128]{1,0:T(8,128)(2,1)S(1)}, bf16[256,128]{1,0:T(8,128)(2,1)S(1)}, u32[]{:S(2)}, u32[]{:S(2)}) collective-permute-start(bf16[256,128]{1,0:T(8,128)(2,1)S(1)} %get-tuple-element.42.refs_3_), channel_id=1, source_target_pairs={{0,4},{1,5},{2,6},{3,7},{4,0},{5,1},{6,2},{7,3},{8,12},{9,13},{10,... | collective-permute-start | bytes 196616 | tf_op jit(solution)/shard_map/ppermute | solution.py:17
  43.9 6.7 %collective-permute-start.22 = (bf16[256,128]{1,0:T(8,128)(2,1)S(1)}, bf16[256,128]{1,0:T(8,128)(2,1)S(1)}, u32[]{:S(2)}, u32[]{:S(2)}) collective-permute-start(bf16[256,128]{1,0:T(8,128)(2,1)S(1)} %get-tuple-element.42.refs_3_), channel_id=1, source_target_pairs={{0,2},{1,3},{2,0},{3,1},{4,6},{5,7},{6,4},{7,5},{8,10},{9,11},{10,... | collective-permute-start | bytes 196616 | tf_op jit(solution)/shard_map/ppermute | solution.py:17
  45.6 5.4 %collective-permute-start.30 = (f32[80,128]{1,0:T(8,128)S(1)}, f32[80,128]{1,0:T(8,128)S(1)}, u32[]{:S(2)}, u32[]{:S(2)}) collective-permute-start(f32[80,128]{1,0:T(8,128)S(1)} %get-tuple-element.47), channel_id=1, source_target_pairs={{0,24},{8,16},{16,8},{24,0},{1,25},{9,17},{17,9},{25,1},{2,26},{10... | collective-permute-start | bytes 122888 | tf_op jit(solution)/shard_map/ppermute | solution.py:17
  47.4 4.0 %collective-permute-start.29 = (f32[80,128]{1,0:T(8,128)S(1)}, f32[80,128]{1,0:T(8,128)S(1)}, u32[]{:S(2)}, u32[]{:S(2)}) collective-permute-start(f32[80,128]{1,0:T(8,128)S(1)} %get-tuple-element.48), channel_id=1, source_target_pairs={{0,16},{8,24},{16,0},{24,8},{1,17},{9,25},{17,1},{25,9},{2,18},{10... | collective-permute-start | bytes 122888 | tf_op jit(solution)/shard_map/ppermute | solution.py:17
  48.0 4.0 %collective-permute-start.28 = (f32[80,128]{1,0:T(8,128)S(1)}, f32[80,128]{1,0:T(8,128)S(1)}, u32[]{:S(2)}, u32[]{:S(2)}) collective-permute-start(f32[80,128]{1,0:T(8,128)S(1)} %get-tuple-element.46), channel_id=1, source_target_pairs={{0,8},{8,0},{16,24},{24,16},{1,9},{9,1},{17,25},{25,17},{2,10},{10... | collective-permute-start | bytes 122888 | tf_op jit(solution)/shard_map/ppermute | solution.py:17
  50.5 3.8 %collective-permute-start.26 = (bf16[256,128]{1,0:T(8,128)(2,1)S(1)}, bf16[256,128]{1,0:T(8,128)(2,1)S(1)}, u32[]{:S(2)}, u32[]{:S(2)}) collective-permute-start(bf16[256,128]{1,0:T(8,128)(2,1)S(1)} %get-tuple-element.42.refs_3_), channel_id=1, source_target_pairs={{0,1},{1,0},{2,3},{3,2},{4,5},{5,4},{6,7},{7,6},{8,9},{9,8},{10,11... | collective-permute-start | bytes 196616 | tf_op jit(solution)/shard_map/ppermute | solution.py:17
  50.5 4.6 %collective-permute-start.23 = (bf16[256,128]{1,0:T(8,128)(2,1)S(1)}, bf16[256,128]{1,0:T(8,128)(2,1)S(1)}, u32[]{:S(2)}, u32[]{:S(2)}) collective-permute-start(bf16[256,128]{1,0:T(8,128)(2,1)S(1)} %collective-permute-done.20.refs_0_), channel_id=1, source_target_pairs={{0,1},{1,0},{2,3},{3,2},{4,5},{5,4},{6,7},{7,6},{8,9},{9,8},{10,11... | collective-permute-start | bytes 196616 | tf_op jit(solution)/shard_map/ppermute | solution.py:17
  51.0 6.2 %collective-permute-start.24 = (bf16[256,128]{1,0:T(8,128)(2,1)S(1)}, bf16[256,128]{1,0:T(8,128)(2,1)S(1)}, u32[]{:S(2)}, u32[]{:S(2)}) collective-permute-start(bf16[256,128]{1,0:T(8,128)(2,1)S(1)} %collective-permute-done.21.refs_1_), channel_id=1, source_target_pairs={{0,1},{1,0},{2,3},{3,2},{4,5},{5,4},{6,7},{7,6},{8,9},{9,8},{10,11... | collective-permute-start | bytes 196616 | tf_op jit(solution)/shard_map/ppermute | solution.py:17
  51.4 5.9 %collective-permute-start.25 = (bf16[256,128]{1,0:T(8,128)(2,1)S(1)}, bf16[256,128]{1,0:T(8,128)(2,1)S(1)}, u32[]{:S(2)}, u32[]{:S(2)}) collective-permute-start(bf16[256,128]{1,0:T(8,128)(2,1)S(1)} %collective-permute-done.22.refs_2_), channel_id=1, source_target_pairs={{0,1},{1,0},{2,3},{3,2},{4,5},{5,4},{6,7},{7,6},{8,9},{9,8},{10,11... | collective-permute-start | bytes 196616 | tf_op jit(solution)/shard_map/ppermute | solution.py:17
  52.0 6.0 %collective-permute-start.33 = (f32[80,128]{1,0:T(8,128)S(1)}, f32[80,128]{1,0:T(8,128)S(1)}, u32[]{:S(2)}, u32[]{:S(2)}) collective-permute-start(f32[80,128]{1,0:T(8,128)S(1)} %fusion.6), channel_id=1, source_target_pairs={{0,6},{1,7},{2,4},{3,5},{4,2},{5,3},{6,0},{7,1},{8,14},{9,15},{10,... | collective-permute-start | bytes 122888 | tf_op jit(solution)/shard_map/ppermute | solution.py:17
  54.3 5.2 %collective-permute-start.32 = (f32[80,128]{1,0:T(8,128)S(1)}, f32[80,128]{1,0:T(8,128)S(1)}, u32[]{:S(2)}, u32[]{:S(2)}) collective-permute-start(f32[80,128]{1,0:T(8,128)S(1)} %fusion.6), channel_id=1, source_target_pairs={{0,4},{1,5},{2,6},{3,7},{4,0},{5,1},{6,2},{7,3},{8,12},{9,13},{10,... | collective-permute-start | bytes 122888 | tf_op jit(solution)/shard_map/ppermute | solution.py:17
  55.1 4.6 %collective-permute-start.31 = (f32[80,128]{1,0:T(8,128)S(1)}, f32[80,128]{1,0:T(8,128)S(1)}, u32[]{:S(2)}, u32[]{:S(2)}) collective-permute-start(f32[80,128]{1,0:T(8,128)S(1)} %fusion.6), channel_id=1, source_target_pairs={{0,2},{1,3},{2,0},{3,1},{4,6},{5,7},{6,4},{7,5},{8,10},{9,11},{10,... | collective-permute-start | bytes 122888 | tf_op jit(solution)/shard_map/ppermute | solution.py:17
  59.8 6.5 %collective-permute-start.36 = (bf16[416,128]{1,0:T(8,128)(2,1)S(1)}, bf16[416,128]{1,0:T(8,128)(2,1)S(1)}, u32[]{:S(2)}, u32[]{:S(2)}) collective-permute-start(bf16[416,128]{1,0:T(8,128)(2,1)S(1)} %get-tuple-element.51), channel_id=1, source_target_pairs={{0,24},{8,16},{16,8},{24,0},{1,25},{9,17},{17,9},{25,1},{2,26},{10... | collective-permute-start | bytes 319496 | tf_op jit(solution)/shard_map/ppermute | solution.py:17
  61.0 6.0 %collective-permute-start.35 = (bf16[416,128]{1,0:T(8,128)(2,1)S(1)}, bf16[416,128]{1,0:T(8,128)(2,1)S(1)}, u32[]{:S(2)}, u32[]{:S(2)}) collective-permute-start(bf16[416,128]{1,0:T(8,128)(2,1)S(1)} %get-tuple-element.50), channel_id=1, source_target_pairs={{0,16},{8,24},{16,0},{24,8},{1,17},{9,25},{17,1},{25,9},{2,18},{10... | collective-permute-start | bytes 319496 | tf_op jit(solution)/shard_map/ppermute | solution.py:17
  62.0 5.1 %collective-permute-start.34 = (bf16[416,128]{1,0:T(8,128)(2,1)S(1)}, bf16[416,128]{1,0:T(8,128)(2,1)S(1)}, u32[]{:S(2)}, u32[]{:S(2)}) collective-permute-start(bf16[416,128]{1,0:T(8,128)(2,1)S(1)} %get-tuple-element.49), channel_id=1, source_target_pairs={{0,8},{8,0},{16,24},{24,16},{1,9},{9,1},{17,25},{25,17},{2,10},{10... | collective-permute-start | bytes 319496 | tf_op jit(solution)/shard_map/ppermute | solution.py:17
  (11 other events, 57.5 us)

commit v6 on v5

--- a/solution.py
+++ b/solution.py
@@ -275,19 +275,17 @@
     z3_ref,
     first_ref,
     second_ref,
-    near_ref,
-    far_ref,
-    block_ref,
-    image_ref,
-    whole,
+    *refs,
 ):
+    near, far = refs[: pieces // 2], refs[pieces // 2 : pieces]
+    block_ref, image_ref, whole = refs[pieces:]
     width = x_ref.shape[1]
     rows = width // pieces
     for m in range(pieces):
-        piece = far_ref if m % 2 else near_ref
+        piece = (far if m % 2 else near)[m // 2]
         start = pl.multiple_of((index_ref[0] ^ m) * rows, rows)
         for at in range(whole.shape[0]):
-            whole[at, pl.ds(start, rows), :] = piece[m // 2, at * rows : (at + 1) * rows]
+            whole[at, pl.ds(start, rows), :] = piece[at * rows : (at + 1) * rows]
     row, col = indices(width)
     eye = (row == col).astype(jnp.float32)
     first, third, n01, n02, n12 = (whole[at] for at in range(5))
@@ -358,12 +356,12 @@
     return pl.pallas_call(
         functools.partial(finish_kernel, pieces, verts_all),
         out_shape=[out, out],
-        in_specs=smem(1) + vmem(8),
+        in_specs=smem(1) + vmem(6 + pieces),
         out_specs=vmem(2),
         scratch_shapes=[pltpu.VMEM((5, width, width), jnp.float32)],
         compiler_params=pltpu.CompilerParams(vmem_limit_bytes=4 * VMEM_BYTES),
         name="finish",
-    )(index, x, z1, z2, z3, first, second, near, far)
+    )(index, x, z1, z2, z3, first, second, *near, *far)
 
 
 def split(array):
@@ -467,8 +465,9 @@
         parts, _ = send(parts)
         arrived = [swap(gram, *hop) for hop in outer]
     z3 = collect(parts)
-    gram_near = jnp.stack([gram] + arrived)
-    gram_far = swap(gram_near, "col", 1)
+    gram_near = [gram] + arrived
+    rest = swap(jnp.stack(arrived[::-1]), "col", 1)
+    gram_far = twin([gram]) + [rest[k] for k in range(len(arrived))][::-1]
     return tuple(
         finish(
             index,
@@ -480,7 +479,7 @@
             rotation_second,
             gram_near,
             gram_far,
-            2 * gram_near.shape[0],
+            2 * len(gram_near),
             verts_all,
         )
     )

time: 71.6 us -> 74.1 us (1.035)
  waiting for transfers between devices: 20 us -> 23.2 us
    ppermute x38 -> x39, waiting for transfers between devices: 20 us -> 23.2 us  [swap(): return lax.ppermute(array, axis, [(k, k ^ mask) for k in range(size)])]
    ppermute x38 -> x39, starting transfers between devices: 36 us -> 35.6 us  [swap(): return lax.ppermute(array, axis, [(k, k ^ mask) for k in range(size)])]
  transfers between devices with their start and end apart: 38 -> 39, of which waited for: 18 -> 17; matrix products, arithmetic and copies ran while one was open for 1% -> 1% of each run, Pallas kernels for 8% -> 7%
where the time goes in v6:
time: 74.1 us; the launch traced here: 74 us
  starting transfers between devices  35.6 us (48%)
  waiting for transfers between devices  23.2 us (31%)
  Pallas kernels  9.75 us (13%)
  other arithmetic  2.16 us (3%)
  between operations  1.68 us (2%)
  local copies, waits for them, and re-layouts  1.63 us (2%)
    ppermute x39, starting transfers between devices, swap(): return lax.ppermute(array, axis, [(k, k ^ mask) for k in range(size)])  35.6 us
    ppermute x39, waiting for transfers between devices, swap(): return lax.ppermute(array, axis, [(k, k ^ mask) for k in range(size)])  23.2 us
    pallas_call x1, Pallas kernels, finish(): pl.pallas_call(functools.partial(finish_kernel, pieces, verts_all), out_s...  2.93 us
    pallas_call x3, Pallas kernels, far_products(): pl.pallas_call(far_kernel, out_shape=[jax.ShapeDtypeStruct((sub, width),...  2.19 us
    pallas_call x3, Pallas kernels, near_products(): pl.pallas_call(near_kernel, out_shape=jax.ShapeDtypeStruct((dense.shape[0...  2.16 us
    unnamed x10, local copies, waits for them, and re-layouts  1.61 us
    pallas_call x1, Pallas kernels, place_tiles(): pl.pallas_call(place_kernel, out_shape=jax.ShapeDtypeStruct((height, widt...  1.57 us
  transfers between devices with their start and end apart: 39, of which 17 were waited for; matrix products, arithmetic and copies ran while one was open for 1% of the time, Pallas kernels for 7%

profile of v6, /device:TPU:0, one launch (start us, length us, event | category | flops | bytes accessed | tf_op | source)
XLA Modules:
  0.0 74.0 jit_solution(13488933818264819111)
XLA Ops:
  0.6 1.0 %multiply_convert_fusion.2.refs_3_ = bf16[256,128]{1,0:T(8,128)(2,1)S(1)} fusion(f32[256,128]{1,0:T(8,128)} %x_ref.5, f32[256]{0:T(256)} %param.9), kind=kLoop, calls=%fused_computation.11 | loop fusion | flops 65536 | bytes 197632 | tf_op jit(solution)/shard_map/convert_element_type | solution.py:414
  1.6 5.1 %collective-permute-start = (bf16[256,128]{1,0:T(8,128)(2,1)S(1)}, bf16[256,128]{1,0:T(8,128)(2,1)S(1)}, u32[]{:S(2)}, u32[]{:S(2)}) collective-permute-start(bf16[256,128]{1,0:T(8,128)(2,1)S(1)} %multiply_convert_fusion.2.refs_3_), channel_id=1, source_target_pairs={{0,6},{1,7},{2,4},{3,5},{4,2},{5,3},{6,0},{7,1},{8,14},{9,15},{10,... | collective-permute-start | bytes 196616 | tf_op jit(solution)/shard_map/ppermute | solution.py:17
  8.8 1.6 %copy-done.1 = bf16[1,1,64,128,128]{4,3,2,1,0:T(8,128)(2,1)S(1)} copy-done((bf16[1,1,64,128,128]{4,3,2,1,0:T(8,128)(2,1)S(1)}, bf16[1,1,64,128,128]{4,3,2,1,0:T(8,128)(2,1)}, u32[]{:S(2)}) %copy-start.1) | copy-done | bytes 2097176
  10.3 1.6 %place_tiles.1.dense_ref = bf16[1024,2048]{1,0:T(8,128)(2,1)S(1)} custom-call(s32[1]{0:T(128)} %bitcast.55.count_ref, s32[64]{0:T(128)S(1)} %get-tuple-element.22.cols_ref, s32[64]{0:T(128)S(1)} %get-tuple-element.23.rows_ref, bf16[64,128,128]{2,1,0:T(8,128)(2,1)S(1)} %bitcast.56), custom_call_target="tpu_custom_call" | custom-call | bytes 8388608 | tf_op jit(solution)/shard_map/place_tiles/pallas_call | solution.py:120
  14.7 2.3 %collective-permute-start.9 = (bf16[256,128]{1,0:T(8,128)(2,1)S(1)}, bf16[256,128]{1,0:T(8,128)(2,1)S(1)}, u32[]{:S(2)}, u32[]{:S(2)}) collective-permute-start(bf16[256,128]{1,0:T(8,128)(2,1)S(1)} %get-tuple-element.29), channel_id=1, source_target_pairs={{0,24},{8,16},{16,8},{24,0},{1,25},{9,17},{17,9},{25,1},{2,26},{10... | collective-permute-start | bytes 196616 | tf_op jit(solution)/shard_map/ppermute | solution.py:17
  17.0 1.1 %collective-permute-start.8 = (bf16[256,128]{1,0:T(8,128)(2,1)S(1)}, bf16[256,128]{1,0:T(8,128)(2,1)S(1)}, u32[]{:S(2)}, u32[]{:S(2)}) collective-permute-start(bf16[256,128]{1,0:T(8,128)(2,1)S(1)} %get-tuple-element.28), channel_id=1, source_target_pairs={{0,16},{8,24},{16,0},{24,8},{1,17},{9,25},{17,1},{25,9},{2,18},{10... | collective-permute-start | bytes 196616 | tf_op jit(solution)/shard_map/ppermute | solution.py:17
  18.2 1.8 %collective-permute-done.9 = bf16[256,128]{1,0:T(8,128)(2,1)S(1)} collective-permute-done((bf16[256,128]{1,0:T(8,128)(2,1)S(1)}, bf16[256,128]{1,0:T(8,128)(2,1)S(1)}, u32[]{:S(2)}, u32[]{:S(2)}) %collective-permute-start.9) | collective-permute-done | bytes 65568 | tf_op jit(solution)/shard_map/ppermute | solution.py:17
  20.0 1.4 %collective-permute-done.8 = bf16[256,128]{1,0:T(8,128)(2,1)S(1)} collective-permute-done((bf16[256,128]{1,0:T(8,128)(2,1)S(1)}, bf16[256,128]{1,0:T(8,128)(2,1)S(1)}, u32[]{:S(2)}, u32[]{:S(2)}) %collective-permute-start.8) | collective-permute-done | bytes 65568 | tf_op jit(solution)/shard_map/ppermute | solution.py:17
  21.4 1.0 %collective-permute-done.7 = bf16[256,128]{1,0:T(8,128)(2,1)S(1)} collective-permute-done((bf16[256,128]{1,0:T(8,128)(2,1)S(1)}, bf16[256,128]{1,0:T(8,128)(2,1)S(1)}, u32[]{:S(2)}, u32[]{:S(2)}) %collective-permute-start.7) | collective-permute-done | bytes 65568 | tf_op jit(solution)/shard_map/ppermute | solution.py:17
  22.6 3.7 %collective-permute-start.10 = (bf16[256,128]{1,0:T(8,128)(2,1)S(1)}, bf16[256,128]{1,0:T(8,128)(2,1)S(1)}, u32[]{:S(2)}, u32[]{:S(2)}) collective-permute-start(bf16[256,128]{1,0:T(8,128)(2,1)S(1)} %get-tuple-element.44.refs_3_), channel_id=1, source_target_pairs={{0,6},{1,7},{2,4},{3,5},{4,2},{5,3},{6,0},{7,1},{8,14},{9,15},{10,... | collective-permute-start | bytes 196616 | tf_op jit(solution)/shard_map/ppermute | solution.py:17
  26.3 0.7 %collective-permute-start.12 = (bf16[256,128]{1,0:T(8,128)(2,1)S(1)}, bf16[256,128]{1,0:T(8,128)(2,1)S(1)}, u32[]{:S(2)}, u32[]{:S(2)}) collective-permute-start(bf16[256,128]{1,0:T(8,128)(2,1)S(1)} %get-tuple-element.44.refs_3_), channel_id=1, source_target_pairs={{0,2},{1,3},{2,0},{3,1},{4,6},{5,7},{6,4},{7,5},{8,10},{9,11},{10,... | collective-permute-start | bytes 196616 | tf_op jit(solution)/shard_map/ppermute | solution.py:17
  27.0 1.8 %collective-permute-done.10.refs_0_ = bf16[256,128]{1,0:T(8,128)(2,1)S(1)} collective-permute-done((bf16[256,128]{1,0:T(8,128)(2,1)S(1)}, bf16[256,128]{1,0:T(8,128)(2,1)S(1)}, u32[]{:S(2)}, u32[]{:S(2)}) %collective-permute-start.10) | collective-permute-done | bytes 65568 | tf_op jit(solution)/shard_map/ppermute | solution.py:17
  28.8 2.7 %collective-permute-done.11.refs_1_ = bf16[256,128]{1,0:T(8,128)(2,1)S(1)} collective-permute-done((bf16[256,128]{1,0:T(8,128)(2,1)S(1)}, bf16[256,128]{1,0:T(8,128)(2,1)S(1)}, u32[]{:S(2)}, u32[]{:S(2)}) %collective-permute-start.11) | collective-permute-done | bytes 65568 | tf_op jit(solution)/shard_map/ppermute | solution.py:17
  33.6 1.3 %collective-permute-start.19 = (bf16[256,128]{1,0:T(8,128)(2,1)S(1)}, bf16[256,128]{1,0:T(8,128)(2,1)S(1)}, u32[]{:S(2)}, u32[]{:S(2)}) collective-permute-start(bf16[256,128]{1,0:T(8,128)(2,1)S(1)} %get-tuple-element.33), channel_id=1, source_target_pairs={{0,24},{8,16},{16,8},{24,0},{1,25},{9,17},{17,9},{25,1},{2,26},{10... | collective-permute-start | bytes 196616 | tf_op jit(solution)/shard_map/ppermute | solution.py:17
  34.9 1.2 %collective-permute-start.18 = (bf16[256,128]{1,0:T(8,128)(2,1)S(1)}, bf16[256,128]{1,0:T(8,128)(2,1)S(1)}, u32[]{:S(2)}, u32[]{:S(2)}) collective-permute-start(bf16[256,128]{1,0:T(8,128)(2,1)S(1)} %get-tuple-element.32), channel_id=1, source_target_pairs={{0,16},{8,24},{16,0},{24,8},{1,17},{9,25},{17,1},{25,9},{2,18},{10... | collective-permute-start | bytes 196616 | tf_op jit(solution)/shard_map/ppermute | solution.py:17
  36.1 1.1 %collective-permute-start.17 = (bf16[256,128]{1,0:T(8,128)(2,1)S(1)}, bf16[256,128]{1,0:T(8,128)(2,1)S(1)}, u32[]{:S(2)}, u32[]{:S(2)}) collective-permute-start(bf16[256,128]{1,0:T(8,128)(2,1)S(1)} %get-tuple-element.31), channel_id=1, source_target_pairs={{0,8},{8,0},{16,24},{24,16},{1,9},{9,1},{17,25},{25,17},{2,10},{10... | collective-permute-start | bytes 196616 | tf_op jit(solution)/shard_map/ppermute | solution.py:17
  37.7 1.5 %collective-permute-done.19 = bf16[256,128]{1,0:T(8,128)(2,1)S(1)} collective-permute-done((bf16[256,128]{1,0:T(8,128)(2,1)S(1)}, bf16[256,128]{1,0:T(8,128)(2,1)S(1)}, u32[]{:S(2)}, u32[]{:S(2)}) %collective-permute-start.19) | collective-permute-done | bytes 65568 | tf_op jit(solution)/shard_map/ppermute | solution.py:17
  39.2 1.2 %collective-permute-done.18 = bf16[256,128]{1,0:T(8,128)(2,1)S(1)} collective-permute-done((bf16[256,128]{1,0:T(8,128)(2,1)S(1)}, bf16[256,128]{1,0:T(8,128)(2,1)S(1)}, u32[]{:S(2)}, u32[]{:S(2)}) %collective-permute-start.18) | collective-permute-done | bytes 65568 | tf_op jit(solution)/shard_map/ppermute | solution.py:17
  41.0 2.6 %collective-permute-start.20 = (bf16[256,128]{1,0:T(8,128)(2,1)S(1)}, bf16[256,128]{1,0:T(8,128)(2,1)S(1)}, u32[]{:S(2)}, u32[]{:S(2)}) collective-permute-start(bf16[256,128]{1,0:T(8,128)(2,1)S(1)} %get-tuple-element.42.refs_3_), channel_id=1, source_target_pairs={{0,6},{1,7},{2,4},{3,5},{4,2},{5,3},{6,0},{7,1},{8,14},{9,15},{10,... | collective-permute-start | bytes 196616 | tf_op jit(solution)/shard_map/ppermute | solution.py:17
  43.5 1.9 %collective-permute-start.22 = (bf16[256,128]{1,0:T(8,128)(2,1)S(1)}, bf16[256,128]{1,0:T(8,128)(2,1)S(1)}, u32[]{:S(2)}, u32[]{:S(2)}) collective-permute-start(bf16[256,128]{1,0:T(8,128)(2,1)S(1)} %get-tuple-element.42.refs_3_), channel_id=1, source_target_pairs={{0,2},{1,3},{2,0},{3,1},{4,6},{5,7},{6,4},{7,5},{8,10},{9,11},{10,... | collective-permute-start | bytes 196616 | tf_op jit(solution)/shard_map/ppermute | solution.py:17
  45.5 1.9 %collective-permute-start.30 = (f32[80,128]{1,0:T(8,128)S(1)}, f32[80,128]{1,0:T(8,128)S(1)}, u32[]{:S(2)}, u32[]{:S(2)}) collective-permute-start(f32[80,128]{1,0:T(8,128)S(1)} %get-tuple-element.47), channel_id=1, source_target_pairs={{0,24},{8,16},{16,8},{24,0},{1,25},{9,17},{17,9},{25,1},{2,26},{10... | collective-permute-start | bytes 122888 | tf_op jit(solution)/shard_map/ppermute | solution.py:17
  48.1 1.0 %collective-permute-start.28 = (f32[80,128]{1,0:T(8,128)S(1)}, f32[80,128]{1,0:T(8,128)S(1)}, u32[]{:S(2)}, u32[]{:S(2)}) collective-permute-start(f32[80,128]{1,0:T(8,128)S(1)} %get-tuple-element.46), channel_id=1, source_target_pairs={{0,8},{8,0},{16,24},{24,16},{1,9},{9,1},{17,25},{25,17},{2,10},{10... | collective-permute-start | bytes 122888 | tf_op jit(solution)/shard_map/ppermute | solution.py:17
  49.0 1.1 %collective-permute-done.21.refs_1_ = bf16[256,128]{1,0:T(8,128)(2,1)S(1)} collective-permute-done((bf16[256,128]{1,0:T(8,128)(2,1)S(1)}, bf16[256,128]{1,0:T(8,128)(2,1)S(1)}, u32[]{:S(2)}, u32[]{:S(2)}) %collective-permute-start.21) | collective-permute-done | bytes 65568 | tf_op jit(solution)/shard_map/ppermute | solution.py:17
  52.1 2.4 %collective-permute-start.33 = (f32[80,128]{1,0:T(8,128)S(1)}, f32[80,128]{1,0:T(8,128)S(1)}, u32[]{:S(2)}, u32[]{:S(2)}) collective-permute-start(f32[80,128]{1,0:T(8,128)S(1)} %fusion.3), channel_id=1, source_target_pairs={{0,6},{1,7},{2,4},{3,5},{4,2},{5,3},{6,0},{7,1},{8,14},{9,15},{10,... | collective-permute-start | bytes 122888 | tf_op jit(solution)/shard_map/ppermute | solution.py:17
  54.5 2.0 %collective-permute-start.31 = (f32[80,128]{1,0:T(8,128)S(1)}, f32[80,128]{1,0:T(8,128)S(1)}, u32[]{:S(2)}, u32[]{:S(2)}) collective-permute-start(f32[80,128]{1,0:T(8,128)S(1)} %fusion.3), channel_id=1, source_target_pairs={{0,2},{1,3},{2,0},{3,1},{4,6},{5,7},{6,4},{7,5},{8,10},{9,11},{10,... | collective-permute-start | bytes 122888 | tf_op jit(solution)/shard_map/ppermute | solution.py:17
  58.1 1.4 %collective-permute-done.32 = f32[80,128]{1,0:T(8,128)S(1)} collective-permute-done((f32[80,128]{1,0:T(8,128)S(1)}, f32[80,128]{1,0:T(8,128)S(1)}, u32[]{:S(2)}, u32[]{:S(2)}) %collective-permute-start.32) | collective-permute-done | bytes 40992 | tf_op jit(solution)/shard_map/ppermute | solution.py:17
  59.5 1.2 %collective-permute-start.34 = (bf16[416,128]{1,0:T(8,128)(2,1)S(1)}, bf16[416,128]{1,0:T(8,128)(2,1)S(1)}, u32[]{:S(2)}, u32[]{:S(2)}) collective-permute-start(bf16[416,128]{1,0:T(8,128)(2,1)S(1)} %get-tuple-element.52), channel_id=1, source_target_pairs={{0,8},{8,0},{16,24},{24,16},{1,9},{9,1},{17,25},{25,17},{2,10},{10... | collective-permute-start | bytes 319496 | tf_op jit(solution)/shard_map/ppermute | solution.py:17
  60.6 1.9 %collective-permute-start.36 = (bf16[416,128]{1,0:T(8,128)(2,1)S(1)}, bf16[416,128]{1,0:T(8,128)(2,1)S(1)}, u32[]{:S(2)}, u32[]{:S(2)}) collective-permute-start(bf16[416,128]{1,0:T(8,128)(2,1)S(1)} %get-tuple-element.54), channel_id=1, source_target_pairs={{0,24},{8,16},{16,8},{24,0},{1,25},{9,17},{17,9},{25,1},{2,26},{10... | collective-permute-start | bytes 319496 | tf_op jit(solution)/shard_map/ppermute | solution.py:17
  63.0 1.2 %collective-permute-done.34 = bf16[416,128]{1,0:T(8,128)(2,1)S(1)} collective-permute-done((bf16[416,128]{1,0:T(8,128)(2,1)S(1)}, bf16[416,128]{1,0:T(8,128)(2,1)S(1)}, u32[]{:S(2)}, u32[]{:S(2)}) %collective-permute-start.34) | collective-permute-done | bytes 106528 | tf_op jit(solution)/shard_map/ppermute | solution.py:17
  64.3 5.2 %collective-permute-done.35 = bf16[416,128]{1,0:T(8,128)(2,1)S(1)} collective-permute-done((bf16[416,128]{1,0:T(8,128)(2,1)S(1)}, bf16[416,128]{1,0:T(8,128)(2,1)S(1)}, u32[]{:S(2)}, u32[]{:S(2)}) %collective-permute-start.35) | collective-permute-done | bytes 106528 | tf_op jit(solution)/shard_map/ppermute | solution.py:17
  69.8 1.2 %collective-permute-done.38 = f32[3,80,128]{2,1,0:T(8,128)S(1)} collective-permute-done((f32[3,80,128]{2,1,0:T(8,128)S(1)}, f32[3,80,128]{2,1,0:T(8,128)S(1)}, u32[]{:S(2)}, u32[]{:S(2)}) %collective-permute-start.38) | collective-permute-done | bytes 122912 | tf_op jit(solution)/shard_map/ppermute | solution.py:17
  71.1 2.9 %finish.1 = (f32[256,128]{1,0:T(8,128)}, f32[256,128]{1,0:T(8,128)}) custom-call(s32[1]{0:T(128)} %bitcast.2.index_ref, f32[256,128]{1,0:T(8,128)S(1)} %copy-done, f32[256,128]{1,0:T(8,128)S(1)} %get-tuple-element.45.z1_ref, f32[256,128]{1,0:T(8,128)S(1)} %get-tuple-element.43.z2_ref, f32[256,128]{1,0:T(8,128)S(1)} %add_multiply_fusion.z3_ref, ...), custom_call_target="tpu_custom_call" | custom-call | tf_op jit(solution)/shard_map/finish/pallas_call | solution.py:356
  (88 shorter events, 12.5 us)
Async XLA Ops:
  1.6 10.4 %collective-permute-start = (bf16[256,128]{1,0:T(8,128)(2,1)S(1)}, bf16[256,128]{1,0:T(8,128)(2,1)S(1)}, u32[]{:S(2)}, u32[]{:S(2)}) collective-permute-start(bf16[256,128]{1,0:T(8,128)(2,1)S(1)} %multiply_convert_fusion.2.refs_3_), channel_id=1, source_target_pairs={{0,6},{1,7},{2,4},{3,5},{4,2},{5,3},{6,0},{7,1},{8,14},{9,15},{10,... | collective-permute-start | bytes 196616 | tf_op jit(solution)/shard_map/ppermute | solution.py:17
  6.8 5.8 %collective-permute-start.1 = (bf16[256,128]{1,0:T(8,128)(2,1)S(1)}, bf16[256,128]{1,0:T(8,128)(2,1)S(1)}, u32[]{:S(2)}, u32[]{:S(2)}) collective-permute-start(bf16[256,128]{1,0:T(8,128)(2,1)S(1)} %multiply_convert_fusion.2.refs_3_), channel_id=1, source_target_pairs={{0,4},{1,5},{2,6},{3,7},{4,0},{5,1},{6,2},{7,3},{8,12},{9,13},{10,... | collective-permute-start | bytes 196616 | tf_op jit(solution)/shard_map/ppermute | solution.py:17
  6.8 5.9 %collective-permute-start.2 = (bf16[256,128]{1,0:T(8,128)(2,1)S(1)}, bf16[256,128]{1,0:T(8,128)(2,1)S(1)}, u32[]{:S(2)}, u32[]{:S(2)}) collective-permute-start(bf16[256,128]{1,0:T(8,128)(2,1)S(1)} %multiply_convert_fusion.2.refs_3_), channel_id=1, source_target_pairs={{0,2},{1,3},{2,0},{3,1},{4,6},{5,7},{6,4},{7,5},{8,10},{9,11},{10,... | collective-permute-start | bytes 196616 | tf_op jit(solution)/shard_map/ppermute | solution.py:17
  14.7 5.4 %collective-permute-start.9 = (bf16[256,128]{1,0:T(8,128)(2,1)S(1)}, bf16[256,128]{1,0:T(8,128)(2,1)S(1)}, u32[]{:S(2)}, u32[]{:S(2)}) collective-permute-start(bf16[256,128]{1,0:T(8,128)(2,1)S(1)} %get-tuple-element.29), channel_id=1, source_target_pairs={{0,24},{8,16},{16,8},{24,0},{1,25},{9,17},{17,9},{25,1},{2,26},{10... | collective-permute-start | bytes 196616 | tf_op jit(solution)/shard_map/ppermute | solution.py:17
  17.0 4.4 %collective-permute-start.8 = (bf16[256,128]{1,0:T(8,128)(2,1)S(1)}, bf16[256,128]{1,0:T(8,128)(2,1)S(1)}, u32[]{:S(2)}, u32[]{:S(2)}) collective-permute-start(bf16[256,128]{1,0:T(8,128)(2,1)S(1)} %get-tuple-element.28), channel_id=1, source_target_pairs={{0,16},{8,24},{16,0},{24,8},{1,17},{9,25},{17,1},{25,9},{2,18},{10... | collective-permute-start | bytes 196616 | tf_op jit(solution)/shard_map/ppermute | solution.py:17
  18.2 4.3 %collective-permute-start.7 = (bf16[256,128]{1,0:T(8,128)(2,1)S(1)}, bf16[256,128]{1,0:T(8,128)(2,1)S(1)}, u32[]{:S(2)}, u32[]{:S(2)}) collective-permute-start(bf16[256,128]{1,0:T(8,128)(2,1)S(1)} %get-tuple-element.27), channel_id=1, source_target_pairs={{0,8},{8,0},{16,24},{24,16},{1,9},{9,1},{17,25},{25,17},{2,10},{10... | collective-permute-start | bytes 196616 | tf_op jit(solution)/shard_map/ppermute | solution.py:17
  22.6 6.2 %collective-permute-start.10 = (bf16[256,128]{1,0:T(8,128)(2,1)S(1)}, bf16[256,128]{1,0:T(8,128)(2,1)S(1)}, u32[]{:S(2)}, u32[]{:S(2)}) collective-permute-start(bf16[256,128]{1,0:T(8,128)(2,1)S(1)} %get-tuple-element.44.refs_3_), channel_id=1, source_target_pairs={{0,6},{1,7},{2,4},{3,5},{4,2},{5,3},{6,0},{7,1},{8,14},{9,15},{10,... | collective-permute-start | bytes 196616 | tf_op jit(solution)/shard_map/ppermute | solution.py:17
  26.3 5.2 %collective-permute-start.11 = (bf16[256,128]{1,0:T(8,128)(2,1)S(1)}, bf16[256,128]{1,0:T(8,128)(2,1)S(1)}, u32[]{:S(2)}, u32[]{:S(2)}) collective-permute-start(bf16[256,128]{1,0:T(8,128)(2,1)S(1)} %get-tuple-element.44.refs_3_), channel_id=1, source_target_pairs={{0,4},{1,5},{2,6},{3,7},{4,0},{5,1},{6,2},{7,3},{8,12},{9,13},{10,... | collective-permute-start | bytes 196616 | tf_op jit(solution)/shard_map/ppermute | solution.py:17
  26.3 5.3 %collective-permute-start.12 = (bf16[256,128]{1,0:T(8,128)(2,1)S(1)}, bf16[256,128]{1,0:T(8,128)(2,1)S(1)}, u32[]{:S(2)}, u32[]{:S(2)}) collective-permute-start(bf16[256,128]{1,0:T(8,128)(2,1)S(1)} %get-tuple-element.44.refs_3_), channel_id=1, source_target_pairs={{0,2},{1,3},{2,0},{3,1},{4,6},{5,7},{6,4},{7,5},{8,10},{9,11},{10,... | collective-permute-start | bytes 196616 | tf_op jit(solution)/shard_map/ppermute | solution.py:17
  27.0 5.7 %collective-permute-start.16 = (bf16[256,128]{1,0:T(8,128)(2,1)S(1)}, bf16[256,128]{1,0:T(8,128)(2,1)S(1)}, u32[]{:S(2)}, u32[]{:S(2)}) collective-permute-start(bf16[256,128]{1,0:T(8,128)(2,1)S(1)} %get-tuple-element.44.refs_3_), channel_id=1, source_target_pairs={{0,1},{1,0},{2,3},{3,2},{4,5},{5,4},{6,7},{7,6},{8,9},{9,8},{10,11... | collective-permute-start | bytes 196616 | tf_op jit(solution)/shard_map/ppermute | solution.py:17
  28.8 3.9 %collective-permute-start.13 = (bf16[256,128]{1,0:T(8,128)(2,1)S(1)}, bf16[256,128]{1,0:T(8,128)(2,1)S(1)}, u32[]{:S(2)}, u32[]{:S(2)}) collective-permute-start(bf16[256,128]{1,0:T(8,128)(2,1)S(1)} %collective-permute-done.10.refs_0_), channel_id=1, source_target_pairs={{0,1},{1,0},{2,3},{3,2},{4,5},{5,4},{6,7},{7,6},{8,9},{9,8},{10,11... | collective-permute-start | bytes 196616 | tf_op jit(solution)/shard_map/ppermute | solution.py:17
  33.6 5.5 %collective-permute-start.19 = (bf16[256,128]{1,0:T(8,128)(2,1)S(1)}, bf16[256,128]{1,0:T(8,128)(2,1)S(1)}, u32[]{:S(2)}, u32[]{:S(2)}) collective-permute-start(bf16[256,128]{1,0:T(8,128)(2,1)S(1)} %get-tuple-element.33), channel_id=1, source_target_pairs={{0,24},{8,16},{16,8},{24,0},{1,25},{9,17},{17,9},{25,1},{2,26},{10... | collective-permute-start | bytes 196616 | tf_op jit(solution)/shard_map/ppermute | solution.py:17
  34.9 5.4 %collective-permute-start.18 = (bf16[256,128]{1,0:T(8,128)(2,1)S(1)}, bf16[256,128]{1,0:T(8,128)(2,1)S(1)}, u32[]{:S(2)}, u32[]{:S(2)}) collective-permute-start(bf16[256,128]{1,0:T(8,128)(2,1)S(1)} %get-tuple-element.32), channel_id=1, source_target_pairs={{0,16},{8,24},{16,0},{24,8},{1,17},{9,25},{17,1},{25,9},{2,18},{10... | collective-permute-start | bytes 196616 | tf_op jit(solution)/shard_map/ppermute | solution.py:17
  36.1 4.3 %collective-permute-start.17 = (bf16[256,128]{1,0:T(8,128)(2,1)S(1)}, bf16[256,128]{1,0:T(8,128)(2,1)S(1)}, u32[]{:S(2)}, u32[]{:S(2)}) collective-permute-start(bf16[256,128]{1,0:T(8,128)(2,1)S(1)} %get-tuple-element.31), channel_id=1, source_target_pairs={{0,8},{8,0},{16,24},{24,16},{1,9},{9,1},{17,25},{25,17},{2,10},{10... | collective-permute-start | bytes 196616 | tf_op jit(solution)/shard_map/ppermute | solution.py:17
  40.9 4.5 %collective-permute-start.27 = (f32[4,80,128]{2,1,0:T(8,128)S(1)}, f32[4,80,128]{2,1,0:T(8,128)S(1)}, u32[]{:S(2)}, u32[]{:S(2)}) collective-permute-start(f32[4,80,128]{2,1,0:T(8,128)S(1)} %get-tuple-element.37), channel_id=1, source_target_pairs={{0,1},{1,0},{2,3},{3,2},{4,5},{5,4},{6,7},{7,6},{8,9},{9,8},{10,11... | collective-permute-start | bytes 491528 | tf_op jit(solution)/shard_map/ppermute | solution.py:17
  41.0 7.1 %collective-permute-start.20 = (bf16[256,128]{1,0:T(8,128)(2,1)S(1)}, bf16[256,128]{1,0:T(8,128)(2,1)S(1)}, u32[]{:S(2)}, u32[]{:S(2)}) collective-permute-start(bf16[256,128]{1,0:T(8,128)(2,1)S(1)} %get-tuple-element.42.refs_3_), channel_id=1, source_target_pairs={{0,6},{1,7},{2,4},{3,5},{4,2},{5,3},{6,0},{7,1},{8,14},{9,15},{10,... | collective-permute-start | bytes 196616 | tf_op jit(solution)/shard_map/ppermute | solution.py:17
  43.5 6.6 %collective-permute-start.21 = (bf16[256,128]{1,0:T(8,128)(2,1)S(1)}, bf16[256,128]{1,0:T(8,128)(2,1)S(1)}, u32[]{:S(2)}, u32[]{:S(2)}) collective-permute-start(bf16[256,128]{1,0:T(8,128)(2,1)S(1)} %get-tuple-element.42.refs_3_), channel_id=1, source_target_pairs={{0,4},{1,5},{2,6},{3,7},{4,0},{5,1},{6,2},{7,3},{8,12},{9,13},{10,... | collective-permute-start | bytes 196616 | tf_op jit(solution)/shard_map/ppermute | solution.py:17
  43.5 6.6 %collective-permute-start.22 = (bf16[256,128]{1,0:T(8,128)(2,1)S(1)}, bf16[256,128]{1,0:T(8,128)(2,1)S(1)}, u32[]{:S(2)}, u32[]{:S(2)}) collective-permute-start(bf16[256,128]{1,0:T(8,128)(2,1)S(1)} %get-tuple-element.42.refs_3_), channel_id=1, source_target_pairs={{0,2},{1,3},{2,0},{3,1},{4,6},{5,7},{6,4},{7,5},{8,10},{9,11},{10,... | collective-permute-start | bytes 196616 | tf_op jit(solution)/shard_map/ppermute | solution.py:17
  45.5 5.1 %collective-permute-start.30 = (f32[80,128]{1,0:T(8,128)S(1)}, f32[80,128]{1,0:T(8,128)S(1)}, u32[]{:S(2)}, u32[]{:S(2)}) collective-permute-start(f32[80,128]{1,0:T(8,128)S(1)} %get-tuple-element.47), channel_id=1, source_target_pairs={{0,24},{8,16},{16,8},{24,0},{1,25},{9,17},{17,9},{25,1},{2,26},{10... | collective-permute-start | bytes 122888 | tf_op jit(solution)/shard_map/ppermute | solution.py:17
  47.4 4.0 %collective-permute-start.29 = (f32[80,128]{1,0:T(8,128)S(1)}, f32[80,128]{1,0:T(8,128)S(1)}, u32[]{:S(2)}, u32[]{:S(2)}) collective-permute-start(f32[80,128]{1,0:T(8,128)S(1)} %get-tuple-element.48), channel_id=1, source_target_pairs={{0,16},{8,24},{16,0},{24,8},{1,17},{9,25},{17,1},{25,9},{2,18},{10... | collective-permute-start | bytes 122888 | tf_op jit(solution)/shard_map/ppermute | solution.py:17
  48.1 4.0 %collective-permute-start.28 = (f32[80,128]{1,0:T(8,128)S(1)}, f32[80,128]{1,0:T(8,128)S(1)}, u32[]{:S(2)}, u32[]{:S(2)}) collective-permute-start(f32[80,128]{1,0:T(8,128)S(1)} %get-tuple-element.46), channel_id=1, source_target_pairs={{0,8},{8,0},{16,24},{24,16},{1,9},{9,1},{17,25},{25,17},{2,10},{10... | collective-permute-start | bytes 122888 | tf_op jit(solution)/shard_map/ppermute | solution.py:17
  50.1 4.4 %collective-permute-start.26 = (bf16[256,128]{1,0:T(8,128)(2,1)S(1)}, bf16[256,128]{1,0:T(8,128)(2,1)S(1)}, u32[]{:S(2)}, u32[]{:S(2)}) collective-permute-start(bf16[256,128]{1,0:T(8,128)(2,1)S(1)} %get-tuple-element.42.refs_3_), channel_id=1, source_target_pairs={{0,1},{1,0},{2,3},{3,2},{4,5},{5,4},{6,7},{7,6},{8,9},{9,8},{10,11... | collective-permute-start | bytes 196616 | tf_op jit(solution)/shard_map/ppermute | solution.py:17
  50.1 4.4 %collective-permute-start.23 = (bf16[256,128]{1,0:T(8,128)(2,1)S(1)}, bf16[256,128]{1,0:T(8,128)(2,1)S(1)}, u32[]{:S(2)}, u32[]{:S(2)}) collective-permute-start(bf16[256,128]{1,0:T(8,128)(2,1)S(1)} %collective-permute-done.20.refs_0_), channel_id=1, source_target_pairs={{0,1},{1,0},{2,3},{3,2},{4,5},{5,4},{6,7},{7,6},{8,9},{9,8},{10,11... | collective-permute-start | bytes 196616 | tf_op jit(solution)/shard_map/ppermute | solution.py:17
  50.6 6.7 %collective-permute-start.24 = (bf16[256,128]{1,0:T(8,128)(2,1)S(1)}, bf16[256,128]{1,0:T(8,128)(2,1)S(1)}, u32[]{:S(2)}, u32[]{:S(2)}) collective-permute-start(bf16[256,128]{1,0:T(8,128)(2,1)S(1)} %collective-permute-done.21.refs_1_), channel_id=1, source_target_pairs={{0,1},{1,0},{2,3},{3,2},{4,5},{5,4},{6,7},{7,6},{8,9},{9,8},{10,11... | collective-permute-start | bytes 196616 | tf_op jit(solution)/shard_map/ppermute | solution.py:17
  51.4 5.9 %collective-permute-start.25 = (bf16[256,128]{1,0:T(8,128)(2,1)S(1)}, bf16[256,128]{1,0:T(8,128)(2,1)S(1)}, u32[]{:S(2)}, u32[]{:S(2)}) collective-permute-start(bf16[256,128]{1,0:T(8,128)(2,1)S(1)} %collective-permute-done.22.refs_2_), channel_id=1, source_target_pairs={{0,1},{1,0},{2,3},{3,2},{4,5},{5,4},{6,7},{7,6},{8,9},{9,8},{10,11... | collective-permute-start | bytes 196616 | tf_op jit(solution)/shard_map/ppermute | solution.py:17
  52.1 6.0 %collective-permute-start.33 = (f32[80,128]{1,0:T(8,128)S(1)}, f32[80,128]{1,0:T(8,128)S(1)}, u32[]{:S(2)}, u32[]{:S(2)}) collective-permute-start(f32[80,128]{1,0:T(8,128)S(1)} %fusion.3), channel_id=1, source_target_pairs={{0,6},{1,7},{2,4},{3,5},{4,2},{5,3},{6,0},{7,1},{8,14},{9,15},{10,... | collective-permute-start | bytes 122888 | tf_op jit(solution)/shard_map/ppermute | solution.py:17
  54.5 4.9 %collective-permute-start.32 = (f32[80,128]{1,0:T(8,128)S(1)}, f32[80,128]{1,0:T(8,128)S(1)}, u32[]{:S(2)}, u32[]{:S(2)}) collective-permute-start(f32[80,128]{1,0:T(8,128)S(1)} %fusion.3), channel_id=1, source_target_pairs={{0,4},{1,5},{2,6},{3,7},{4,0},{5,1},{6,2},{7,3},{8,12},{9,13},{10,... | collective-permute-start | bytes 122888 | tf_op jit(solution)/shard_map/ppermute | solution.py:17
  54.5 4.9 %collective-permute-start.31 = (f32[80,128]{1,0:T(8,128)S(1)}, f32[80,128]{1,0:T(8,128)S(1)}, u32[]{:S(2)}, u32[]{:S(2)}) collective-permute-start(f32[80,128]{1,0:T(8,128)S(1)} %fusion.3), channel_id=1, source_target_pairs={{0,2},{1,3},{2,0},{3,1},{4,6},{5,7},{6,4},{7,5},{8,10},{9,11},{10,... | collective-permute-start | bytes 122888 | tf_op jit(solution)/shard_map/ppermute | solution.py:17
  59.5 4.8 %collective-permute-start.34 = (bf16[416,128]{1,0:T(8,128)(2,1)S(1)}, bf16[416,128]{1,0:T(8,128)(2,1)S(1)}, u32[]{:S(2)}, u32[]{:S(2)}) collective-permute-start(bf16[416,128]{1,0:T(8,128)(2,1)S(1)} %get-tuple-element.52), channel_id=1, source_target_pairs={{0,8},{8,0},{16,24},{24,16},{1,9},{9,1},{17,25},{25,17},{2,10},{10... | collective-permute-start | bytes 319496 | tf_op jit(solution)/shard_map/ppermute | solution.py:17
  60.6 10.4 %collective-permute-start.37 = (f32[80,128]{1,0:T(8,128)S(1)}, f32[80,128]{1,0:T(8,128)S(1)}, u32[]{:S(2)}, u32[]{:S(2)}) collective-permute-start(f32[80,128]{1,0:T(8,128)S(1)} %get-tuple-element.41.refs_0_), channel_id=1, source_target_pairs={{0,1},{1,0},{2,3},{3,2},{4,5},{5,4},{6,7},{7,6},{8,9},{9,8},{10,11... | collective-permute-start | bytes 122888 | tf_op jit(solution)/shard_map/ppermute | solution.py:17
  60.6 8.9 %collective-permute-start.36 = (bf16[416,128]{1,0:T(8,128)(2,1)S(1)}, bf16[416,128]{1,0:T(8,128)(2,1)S(1)}, u32[]{:S(2)}, u32[]{:S(2)}) collective-permute-start(bf16[416,128]{1,0:T(8,128)(2,1)S(1)} %get-tuple-element.54), channel_id=1, source_target_pairs={{0,24},{8,16},{16,8},{24,0},{1,25},{9,17},{17,9},{25,1},{2,26},{10... | collective-permute-start | bytes 319496 | tf_op jit(solution)/shard_map/ppermute | solution.py:17
  62.5 7.0 %collective-permute-start.35 = (bf16[416,128]{1,0:T(8,128)(2,1)S(1)}, bf16[416,128]{1,0:T(8,128)(2,1)S(1)}, u32[]{:S(2)}, u32[]{:S(2)}) collective-permute-start(bf16[416,128]{1,0:T(8,128)(2,1)S(1)} %get-tuple-element.53), channel_id=1, source_target_pairs={{0,16},{8,24},{16,0},{24,8},{1,17},{9,25},{17,1},{25,9},{2,18},{10... | collective-permute-start | bytes 319496 | tf_op jit(solution)/shard_map/ppermute | solution.py:17
  (12 other events, 64.5 us)
